TPU v7x, 32 devices: a whole 2x2x4 slice. The times are simulated.
32 devices in a mesh: dp: 8 (over z, y), seq: 4 (over x, core).
Axes of the slice: x: 2, y: 2, z: 4, core: 2. Of those that a mesh axis runs over, the one named last changes fastest.
Arguments:
- block_input: bfloat16 [16, 2048, 768], P('dp', 'seq'), may hold values from -6 to 6
- slot_spans: int32 [16, 2], P('dp'), may hold values from 0 to 2048, as said below
- output_adjoint: bfloat16 [16, 2048, 768], P('dp', 'seq'), may hold values from -6 to 6
- opening_scale_factor: bfloat16 [768], P(('dp', 'seq')), may hold values from 0.5 to 1.5
- opening_offset_vector: bfloat16 [768], P(('dp', 'seq')), may hold values from -1.796875 to 1.796875
- intake_coefficients: bfloat16 [768, 2304], P(None, ('dp', 'seq')), may hold values from -0.21875 to 0.21875
- intake_offset: bfloat16 [2304], P(('dp', 'seq')), may hold values from -1.796875 to 1.796875
- brief_filter_coefficients: bfloat16 [3, 2304], P(None, ('dp', 'seq')), may hold values from -3.5 to 3.5
- brief_filter_offset: bfloat16 [2304], P(('dp', 'seq')), may hold values from -1.796875 to 1.796875
- direct_path_factor: bfloat16 [768], P(('dp', 'seq')), may hold values from -4 to 4
- filter_final_coefficients: bfloat16 [64, 768], P(None, ('dp', 'seq')), may hold values from -0.0625 to 0.0625
- mixer_output_coefficients: bfloat16 [768, 768], P(None, ('dp', 'seq')), may hold values from -0.21875 to 0.21875
- mixer_output_offset: bfloat16 [768], P(('dp', 'seq')), may hold values from -1.796875 to 1.796875
- closing_scale_factor: bfloat16 [768], P(('dp', 'seq')), may hold values from 0.5 to 1.5
- closing_offset_vector: bfloat16 [768], P(('dp', 'seq')), may hold values from -1.796875 to 1.796875
- expand_coefficients: bfloat16 [768, 3072], P(None, ('dp', 'seq')), may hold values from -0.21875 to 0.21875
- expand_offset: bfloat16 [3072], P(('dp', 'seq')), may hold values from -1.796875 to 1.796875
- contract_coefficients: bfloat16 [3072, 768], P(None, ('dp', 'seq')), may hold values from -0.109375 to 0.109375
- contract_offset: bfloat16 [768], P(('dp', 'seq')), may hold values from -1.796875 to 1.796875
- filter_entry_coefficients: float32 [33, 64], replicated, may hold values from -1 to 1
- filter_entry_offset: float32 [64], replicated, may hold values from -1 to 1
- filter_second_coefficients: float32 [64, 64], replicated, may hold values from -0.75 to 0.75
- filter_second_offset: float32 [64], replicated, may hold values from -1 to 1
- filter_third_coefficients: float32 [64, 64], replicated, may hold values from -0.75 to 0.75
- filter_third_offset: float32 [64], replicated, may hold values from -1 to 1
- periodic_frequency: float32 [64], replicated, may hold values from 0.1 to 1.9
Outputs:
- output: bfloat16 [16, 2048, 768], P('dp', 'seq')
- tokens_grad: bfloat16 [16, 2048, 768], P('dp', 'seq')
- pregain_grad: float32 [768], P(('dp', 'seq'))
- preshift_grad: float32 [768], P(('dp', 'seq'))
- projection_grad: float32 [768, 2304], P(None, ('dp', 'seq'))
- projbias_grad: float32 [2304], P(('dp', 'seq'))
- shortconv_grad: float32 [3, 2304], P(None, ('dp', 'seq'))
- shortbias_grad: float32 [2304], P(('dp', 'seq'))
- skipgain_grad: float32 [768], P(('dp', 'seq'))
- filterout_grad: float32 [64, 768], P(None, ('dp', 'seq'))
- mixweight_grad: float32 [768, 768], P(None, ('dp', 'seq'))
- mixbias_grad: float32 [768], P(('dp', 'seq'))
- postgain_grad: float32 [768], P(('dp', 'seq'))
- postshift_grad: float32 [768], P(('dp', 'seq'))
- upweight_grad: float32 [768, 3072], P(None, ('dp', 'seq'))
- upbias_grad: float32 [3072], P(('dp', 'seq'))
- downweight_grad: float32 [3072, 768], P(None, ('dp', 'seq'))
- downbias_grad: float32 [768], P(('dp', 'seq'))
- featmap_grad: float32 [33, 64], replicated
- featbias_grad: float32 [64], replicated
- midmap_grad: float32 [64, 64], replicated
- midbias_grad: float32 [64], replicated
- topmap_grad: float32 [64, 64], replicated
- topbias_grad: float32 [64], replicated
- sinescale_grad: float32 [64], replicated
Inputs may be any that keep to these rules, and one draw needn't show every extreme that they name: `slot_spans`: column 1 of a row is the slot's count of valid positions, from 512 to 2048, and slot 0 has all 2048; column 0 is its first valid position, and the two add up to at most 2048.
All inputs are finite; a program needn't handle non-finite values.
Results may differ from a plain program's by a relative error of at most 0.013.
Values may be sent and summed in bfloat16 or wider, within the bound.
No kernel may reach another device: no remote copies, remote signals or barrier semaphores. Data moves between devices by JAX's collectives and lax.ppermute only.
A program may use at most 256 MiB of HBM per device.

v0:
```python
import math

import jax
import jax.numpy as jnp
from jax import lax
from jax.sharding import PartitionSpec as P


def from_behind(value, axis, by):
    peers = lax.axis_size(axis)
    pairs = [(i, i + by) for i in range(peers) if 0 <= i + by < peers]
    return lax.ppermute(value, axis, pairs)


def product(left, right):
    return jnp.dot(left, right, precision=lax.Precision.HIGHEST, preferred_element_type=jnp.float32)


def standardize_features(values, norm_gain, norm_shift):
    centre = values - jnp.mean(values, axis=-1, keepdims=True)
    spread = jnp.mean(centre * centre, axis=-1, keepdims=True)
    return centre * lax.rsqrt(spread + 1e-05) * norm_gain + norm_shift


def norm_back(values, norm_gain, norm_shift, incoming):
    result, pullback = jax.vjp(standardize_features, values, norm_gain, norm_shift)
    return pullback(incoming)


def gelu_tanh(values):
    return jax.nn.gelu(values, approximate=True)


def position_features(length, emb_width):
    band_count = (emb_width - 1) // 2
    places = jnp.arange(length).astype(jnp.float32)
    standardized_values = places / (length - 1)
    angles = 2.0 * math.pi * places / length
    band_rates = 0.0001 + (band_count - 1 - 0.0001) * jnp.arange(band_count).astype(jnp.float32) / (
        band_count - 1
    )
    phases = angles[:, None] * band_rates[None, :]
    return jnp.concatenate(
        [standardized_values[:, None], jnp.cos(phases), -jnp.sin(phases)], axis=1
    )


def filter_hidden(
    features,
    filter_entry_coefficients,
    filter_entry_offset,
    filter_second_coefficients,
    filter_second_offset,
    filter_third_coefficients,
    filter_third_offset,
    periodic_frequency,
):
    first = jnp.sin(
        periodic_frequency * (product(features, filter_entry_coefficients) + filter_entry_offset)
    )
    middle = jnp.sin(
        periodic_frequency * (product(first, filter_second_coefficients) + filter_second_offset)
    )
    return jnp.sin(
        periodic_frequency * (product(middle, filter_third_coefficients) + filter_third_offset)
    )


def modulation(length, model_width, offset, channels):
    standardized_values = jnp.arange(length).astype(jnp.float32) / (length - 1)
    slowest = math.log(0.01) / 1.5
    fastest = math.log(0.01) / 0.3
    columns = (offset + jnp.arange(channels)).astype(jnp.float32)
    decays = slowest + (fastest - slowest) * columns / (model_width - 1)
    return jnp.exp(-standardized_values[:, None] * jnp.abs(decays)[None, :]) + 0.05


def dft_tables(length):
    padded_len = 2 * length
    lane_count = 128
    blocks = padded_len // lane_count
    halves = blocks // 2
    block_ids = jnp.arange(blocks, dtype=jnp.int32)
    lane_ids = jnp.arange(lane_count, dtype=jnp.int32)
    half_ids = jnp.arange(halves, dtype=jnp.int32)
    first_angle = (
        2.0
        * math.pi
        / blocks
        * (block_ids[:, None] * half_ids[None, :] % blocks).astype(jnp.float32)
    )
    twist_angle = (
        2.0
        * math.pi
        / padded_len
        * (block_ids[:, None] * lane_ids[None, :] % padded_len).astype(jnp.float32)
    )
    lane_angle = (
        2.0
        * math.pi
        / lane_count
        * (lane_ids[:, None] * lane_ids[None, :] % lane_count).astype(jnp.float32)
    )
    return (
        jnp.cos(first_angle),
        jnp.sin(first_angle),
        jnp.cos(twist_angle),
        jnp.sin(twist_angle),
        jnp.cos(lane_angle),
        jnp.sin(lane_angle),
    )


def lane_mul(values, table):
    return jnp.einsum("ckm,mj->ckj", values, table, precision=lax.Precision.HIGH)


def forward_dft(signal, tables):
    first_cos, first_sin, twist_cos, twist_sin, lane_cos, lane_sin = tables
    part_real = jnp.einsum("kn,cnm->ckm", first_cos, signal, precision=lax.Precision.HIGH)
    part_imaginary = -jnp.einsum("kn,cnm->ckm", first_sin, signal, precision=lax.Precision.HIGH)
    turned_real = part_real * twist_cos + part_imaginary * twist_sin
    turned_imaginary = part_imaginary * twist_cos - part_real * twist_sin
    whole_real = lane_mul(turned_real, lane_cos) + lane_mul(turned_imaginary, lane_sin)
    whole_imaginary = lane_mul(turned_imaginary, lane_cos) - lane_mul(turned_real, lane_sin)
    return (whole_real, whole_imaginary)


def inverse_dft(spec_real, spec_imaginary, tables):
    first_cos, first_sin, twist_cos, twist_sin, lane_cos, lane_sin = tables
    back_real = lane_mul(spec_real, lane_cos) - lane_mul(spec_imaginary, lane_sin)
    back_imaginary = lane_mul(spec_real, lane_sin) + lane_mul(spec_imaginary, lane_cos)
    twisted_real = back_real * twist_cos - back_imaginary * twist_sin
    twisted_imaginary = back_real * twist_sin + back_imaginary * twist_cos
    result = jnp.einsum("kn,ckm->cnm", first_cos, twisted_real, precision=lax.Precision.HIGH)
    result = result - jnp.einsum(
        "kn,ckm->cnm", first_sin, twisted_imaginary, precision=lax.Precision.HIGH
    )
    return result / (first_cos.shape[0] * lane_cos.shape[0])


def multiply(left_real, left_imaginary, right_real, right_imaginary):
    return (
        left_real * right_real - left_imaginary * right_imaginary,
        left_real * right_imaginary + left_imaginary * right_real,
    )


def multiply_conj(left_real, left_imaginary, right_real, right_imaginary):
    return (
        left_real * right_real + left_imaginary * right_imaginary,
        left_imaginary * right_real - left_real * right_imaginary,
    )


def per_device(
    block_input,
    slot_spans,
    output_adjoint,
    opening_scale_factor,
    opening_offset_vector,
    intake_coefficients,
    intake_offset,
    brief_filter_coefficients,
    brief_filter_offset,
    direct_path_factor,
    filter_final_coefficients,
    mixer_output_coefficients,
    mixer_output_offset,
    closing_scale_factor,
    closing_offset_vector,
    expand_coefficients,
    expand_offset,
    contract_coefficients,
    contract_offset,
    filter_entry_coefficients,
    filter_entry_offset,
    filter_second_coefficients,
    filter_second_offset,
    filter_third_coefficients,
    filter_third_offset,
    periodic_frequency,
):
    micro_count = block_input.shape[0]
    local = block_input.shape[1]
    model_width = block_input.shape[2]
    seq_count = lax.axis_size("seq")
    seq_index = lax.axis_index("seq")
    length = local * seq_count
    channels = model_width // seq_count
    chan_start = seq_index * channels
    places = seq_index * local + jnp.arange(local, dtype=jnp.int32)
    tables = dft_tables(length)
    features = position_features(length, filter_entry_coefficients.shape[0])
    hidden = filter_hidden(
        features,
        filter_entry_coefficients,
        filter_entry_offset,
        filter_second_coefficients,
        filter_second_offset,
        filter_third_coefficients,
        filter_third_offset,
        periodic_frequency,
    )
    shaping = modulation(length, model_width, chan_start, channels)
    float_type = jnp.float32
    low_type = jnp.bfloat16
    outputs = []
    input_grads = []
    leading_sums = None
    trailing_sums = None
    cross_real = None
    cross_imaginary = None
    for micro_index in range(micro_count):
        gathered = (
            lax.all_gather(opening_scale_factor, ("dp", "seq"), axis=0, tiled=True),
            lax.all_gather(opening_offset_vector, ("dp", "seq"), axis=0, tiled=True),
            lax.all_gather(intake_coefficients, ("dp", "seq"), axis=1, tiled=True),
            lax.all_gather(intake_offset, ("dp", "seq"), axis=0, tiled=True),
            lax.all_gather(brief_filter_coefficients, ("dp", "seq"), axis=1, tiled=True),
            lax.all_gather(brief_filter_offset, ("dp", "seq"), axis=0, tiled=True),
            lax.all_gather(direct_path_factor, ("dp", "seq"), axis=0, tiled=True),
            lax.all_gather(filter_final_coefficients, ("dp", "seq"), axis=1, tiled=True),
            lax.all_gather(mixer_output_coefficients, ("dp", "seq"), axis=1, tiled=True),
            lax.all_gather(mixer_output_offset, ("dp", "seq"), axis=0, tiled=True),
            lax.all_gather(closing_scale_factor, ("dp", "seq"), axis=0, tiled=True),
            lax.all_gather(closing_offset_vector, ("dp", "seq"), axis=0, tiled=True),
            lax.all_gather(expand_coefficients, ("dp", "seq"), axis=1, tiled=True),
            lax.all_gather(expand_offset, ("dp", "seq"), axis=0, tiled=True),
            lax.all_gather(contract_coefficients, ("dp", "seq"), axis=1, tiled=True),
            lax.all_gather(contract_offset, ("dp", "seq"), axis=0, tiled=True),
        )
        columns = lax.dynamic_slice_in_dim(gathered[7], chan_start, channels, 1).astype(float_type)
        kernel = product(hidden, columns) * shaping
        spec_real, spec_imaginary = forward_dft(
            kernel.T.reshape(channels, length // 128, 128), tables
        )
        columns, spec_real, spec_imaginary = (columns, spec_real, spec_imaginary)
        gain_one = gathered[0].astype(float_type)
        shift_one = gathered[1].astype(float_type)
        project_matrix = gathered[2]
        project_bias = gathered[3].astype(float_type)
        conv_taps = gathered[4].astype(float_type)
        conv_bias = gathered[5].astype(float_type)
        skip_gain = gathered[6].astype(float_type)
        mix_matrix = gathered[8]
        mix_bias = gathered[9].astype(float_type)
        gain_two = gathered[10].astype(float_type)
        shift_two = gathered[11].astype(float_type)
        up_matrix = gathered[12]
        up_bias = gathered[13].astype(float_type)
        down_matrix = gathered[14]
        down_bias = gathered[15].astype(float_type)
        sequence_entries = block_input[micro_index].astype(float_type)
        first_pos = slot_spans[micro_index, 0]
        pos_count = slot_spans[micro_index, 1]
        row_mask = ((places >= first_pos) & (places < first_pos + pos_count)).astype(float_type)[
            :, None
        ]
        standardized_values = standardize_features(sequence_entries, gain_one, shift_one)
        normed_low = standardized_values.astype(low_type)
        projected = row_mask * (
            jnp.dot(normed_low, project_matrix, preferred_element_type=float_type) + project_bias
        )
        before = from_behind(projected[local - 2 :], "seq", 1)
        extended = jnp.concatenate([before, projected], axis=0)
        conv_out = (
            conv_bias
            + conv_taps[0] * extended[:local]
            + conv_taps[1] * extended[1 : local + 1]
            + conv_taps[2] * extended[2:]
        )
        outer_gate = conv_out[:, :model_width]
        inner_gate = conv_out[:, model_width : 2 * model_width]
        values = conv_out[:, 2 * model_width :]
        signal = (row_mask * inner_gate * values).astype(low_type)
        sent = lax.all_to_all(signal.T, "seq", split_axis=0, concat_axis=1, tiled=True)
        sig_real, sig_imaginary = forward_dft(
            sent.astype(float_type).reshape(channels, length // 128, 128), tables
        )
        conv_real, conv_imaginary = multiply(sig_real, sig_imaginary, spec_real, spec_imaginary)
        carried_cols = (
            inverse_dft(conv_real, conv_imaginary, tables)
            .reshape(channels, length)
            .astype(low_type)
        )
        carried = lax.all_to_all(
            carried_cols, "seq", split_axis=1, concat_axis=0, tiled=True
        ).T.astype(float_type)
        signal_wide = signal.astype(float_type)
        joined = carried + skip_gain * signal_wide
        gated_mix = (joined * outer_gate).astype(low_type)
        residual = (
            sequence_entries
            + jnp.dot(gated_mix, mix_matrix, preferred_element_type=float_type)
            + mix_bias
        )
        second_low = standardize_features(residual, gain_two, shift_two).astype(low_type)
        up_proj = jnp.dot(second_low, up_matrix, preferred_element_type=float_type) + up_bias
        active_low = gelu_tanh(up_proj).astype(low_type)
        down_proj = jnp.dot(active_low, down_matrix, preferred_element_type=float_type) + down_bias
        outputs.append((row_mask * (residual + down_proj)).astype(low_type))
        grad_out = row_mask * output_adjoint[micro_index].astype(float_type)
        grad_low = grad_out.astype(low_type)
        down_bias_grad = jnp.sum(grad_out, axis=0)
        down_grad = jnp.einsum("tf,td->fd", active_low, grad_low, preferred_element_type=float_type)
        grad_active = jnp.einsum(
            "td,fd->tf", grad_low, down_matrix, preferred_element_type=float_type
        )
        gelu_value, gelu_pull = jax.vjp(gelu_tanh, up_proj)
        grad_up = gelu_pull(grad_active)[0]
        up_bias_grad = jnp.sum(grad_up, axis=0)
        grad_up_low = grad_up.astype(low_type)
        up_grad = jnp.einsum(
            "td,tf->df", second_low, grad_up_low, preferred_element_type=float_type
        )
        grad_second = jnp.einsum(
            "tf,df->td", grad_up_low, up_matrix, preferred_element_type=float_type
        )
        resid_part, gain_two_grad, shift_two_grad = norm_back(
            residual, gain_two, shift_two, grad_second
        )
        grad_residual = grad_out + resid_part
        mix_bias_grad = jnp.sum(grad_residual, axis=0)
        resid_low = grad_residual.astype(low_type)
        mix_grad = jnp.einsum("td,te->de", gated_mix, resid_low, preferred_element_type=float_type)
        trailing_partials = (
            mix_grad,
            mix_bias_grad,
            gain_two_grad,
            shift_two_grad,
            up_grad,
            up_bias_grad,
            down_grad,
            down_bias_grad,
        )
        if micro_index == 0:
            trailing_sums = trailing_partials
        else:
            trailing_sums = tuple(
                (
                    running_total + partial_term
                    for running_total, partial_term in zip(trailing_sums, trailing_partials)
                )
            )
        grad_gated = jnp.einsum(
            "te,de->td", resid_low, mix_matrix, preferred_element_type=float_type
        )
        grad_outer = grad_gated * joined
        grad_joined = grad_gated * outer_gate
        skip_grad = jnp.sum(grad_joined * signal_wide, axis=0)
        back_sent = lax.all_to_all(
            grad_joined.astype(low_type).T, "seq", split_axis=0, concat_axis=1, tiled=True
        )
        back_real, back_imaginary = forward_dft(
            back_sent.astype(float_type).reshape(channels, length // 128, 128), tables
        )
        input_real, input_imaginary = multiply_conj(
            back_real, back_imaginary, spec_real, spec_imaginary
        )
        pair_real, pair_imaginary = multiply_conj(
            back_real, back_imaginary, sig_real, sig_imaginary
        )
        if micro_index == 0:
            cross_real = pair_real
            cross_imaginary = pair_imaginary
        else:
            cross_real = cross_real + pair_real
            cross_imaginary = cross_imaginary + pair_imaginary
        conv_back_cols = (
            inverse_dft(input_real, input_imaginary, tables)
            .reshape(channels, length)
            .astype(low_type)
        )
        conv_back = lax.all_to_all(
            conv_back_cols, "seq", split_axis=1, concat_axis=0, tiled=True
        ).T.astype(float_type)
        grad_signal = row_mask * (conv_back + skip_gain * grad_joined)
        grad_conv = jnp.concatenate(
            [grad_outer, grad_signal * values, grad_signal * inner_gate], axis=1
        )
        conv_bias_grad = jnp.sum(grad_conv, axis=0)
        taps_grad = jnp.stack(
            [
                jnp.sum(grad_conv * extended[tap_index : tap_index + local], axis=0)
                for tap_index in range(3)
            ]
        )
        after = from_behind(grad_conv[:2], "seq", -1)
        grad_extended = jnp.concatenate([grad_conv, after], axis=0)
        grad_projected = row_mask * (
            conv_taps[2] * grad_extended[:local]
            + conv_taps[1] * grad_extended[1 : local + 1]
            + conv_taps[0] * grad_extended[2 : local + 2]
        )
        project_bias_grad = jnp.sum(grad_projected, axis=0)
        projected_low = grad_projected.astype(low_type)
        project_grad = jnp.einsum(
            "td,te->de", normed_low, projected_low, preferred_element_type=float_type
        )
        grad_normed = jnp.einsum(
            "te,de->td", projected_low, project_matrix, preferred_element_type=float_type
        )
        rows_part, gain_one_grad, shift_one_grad = norm_back(
            sequence_entries, gain_one, shift_one, grad_normed
        )
        input_grads.append((grad_residual + rows_part).astype(low_type))
        leading_partials = (
            gain_one_grad,
            shift_one_grad,
            project_grad,
            project_bias_grad,
            taps_grad,
            conv_bias_grad,
            skip_grad,
        )
        if micro_index == 0:
            leading_sums = leading_partials
        else:
            leading_sums = tuple(
                (
                    running_total + partial_term
                    for running_total, partial_term in zip(leading_sums, leading_partials)
                )
            )
    kernel_grad = (
        inverse_dft(cross_real, cross_imaginary, tables).reshape(channels, length).T * shaping
    )
    column_grad = product(hidden.T, kernel_grad)
    filter_full = lax.dynamic_update_slice_in_dim(
        jnp.zeros((filter_final_coefficients.shape[0], model_width), float_type),
        column_grad,
        chan_start,
        1,
    )
    hidden_grad = product(kernel_grad, columns.T)

    def filter_net(
        filter_entry_coefficients,
        filter_entry_offset,
        filter_second_coefficients,
        filter_second_offset,
        filter_third_coefficients,
        filter_third_offset,
        periodic_frequency,
    ):
        return filter_hidden(
            features,
            filter_entry_coefficients,
            filter_entry_offset,
            filter_second_coefficients,
            filter_second_offset,
            filter_third_coefficients,
            filter_third_offset,
            periodic_frequency,
        )

    filter_value, filter_pull = jax.vjp(
        filter_net,
        filter_entry_coefficients,
        filter_entry_offset,
        filter_second_coefficients,
        filter_second_offset,
        filter_third_coefficients,
        filter_third_offset,
        periodic_frequency,
    )
    net_grads = filter_pull(hidden_grad)
    summed = lax.psum(
        (
            net_grads[0],
            net_grads[1],
            net_grads[2],
            net_grads[3],
            net_grads[4],
            net_grads[5],
            net_grads[6],
        ),
        ("dp", "seq"),
    )
    shards = (
        lax.psum_scatter(leading_sums[0], ("dp", "seq"), scatter_dimension=0, tiled=True),
        lax.psum_scatter(leading_sums[1], ("dp", "seq"), scatter_dimension=0, tiled=True),
        lax.psum_scatter(leading_sums[2], ("dp", "seq"), scatter_dimension=1, tiled=True),
        lax.psum_scatter(leading_sums[3], ("dp", "seq"), scatter_dimension=0, tiled=True),
        lax.psum_scatter(leading_sums[4], ("dp", "seq"), scatter_dimension=1, tiled=True),
        lax.psum_scatter(leading_sums[5], ("dp", "seq"), scatter_dimension=0, tiled=True),
        lax.psum_scatter(leading_sums[6], ("dp", "seq"), scatter_dimension=0, tiled=True),
        lax.psum_scatter(filter_full, ("dp", "seq"), scatter_dimension=1, tiled=True),
        lax.psum_scatter(trailing_sums[0], ("dp", "seq"), scatter_dimension=1, tiled=True),
        lax.psum_scatter(trailing_sums[1], ("dp", "seq"), scatter_dimension=0, tiled=True),
        lax.psum_scatter(trailing_sums[2], ("dp", "seq"), scatter_dimension=0, tiled=True),
        lax.psum_scatter(trailing_sums[3], ("dp", "seq"), scatter_dimension=0, tiled=True),
        lax.psum_scatter(trailing_sums[4], ("dp", "seq"), scatter_dimension=1, tiled=True),
        lax.psum_scatter(trailing_sums[5], ("dp", "seq"), scatter_dimension=0, tiled=True),
        lax.psum_scatter(trailing_sums[6], ("dp", "seq"), scatter_dimension=1, tiled=True),
        lax.psum_scatter(trailing_sums[7], ("dp", "seq"), scatter_dimension=0, tiled=True),
    )
    return (jnp.stack(outputs), jnp.stack(input_grads)) + tuple(shards) + tuple(summed)


def solution(mesh):
    in_specs = (
        P("dp", "seq", None),
        P("dp", None),
        P("dp", "seq", None),
        P(("dp", "seq")),
        P(("dp", "seq")),
        P(None, ("dp", "seq")),
        P(("dp", "seq")),
        P(None, ("dp", "seq")),
        P(("dp", "seq")),
        P(("dp", "seq")),
        P(None, ("dp", "seq")),
        P(None, ("dp", "seq")),
        P(("dp", "seq")),
        P(("dp", "seq")),
        P(("dp", "seq")),
        P(None, ("dp", "seq")),
        P(("dp", "seq")),
        P(None, ("dp", "seq")),
        P(("dp", "seq")),
        P(),
        P(),
        P(),
        P(),
        P(),
        P(),
        P(),
    )
    out_specs = (
        P("dp", "seq", None),
        P("dp", "seq", None),
        P(("dp", "seq")),
        P(("dp", "seq")),
        P(None, ("dp", "seq")),
        P(("dp", "seq")),
        P(None, ("dp", "seq")),
        P(("dp", "seq")),
        P(("dp", "seq")),
        P(None, ("dp", "seq")),
        P(None, ("dp", "seq")),
        P(("dp", "seq")),
        P(("dp", "seq")),
        P(("dp", "seq")),
        P(None, ("dp", "seq")),
        P(("dp", "seq")),
        P(None, ("dp", "seq")),
        P(("dp", "seq")),
        P(),
        P(),
        P(),
        P(),
        P(),
        P(),
        P(),
    )
    return jax.shard_map(
        per_device, mesh=mesh, in_specs=in_specs, out_specs=out_specs, check_vma=False
    )
```

profile of v0, /device:TPU:0, one launch (start us, length us, event | category | flops | bytes accessed | tf_op | source)
XLA Modules:
  0.0 1381.4 jit_solution(3900842694186064144)
XLA Ops:
  10.2 44.2 %all_gather.70 = bf16[64,768]{0,1:T(8,128)(2,1)S(1)} all-gather(bf16[64,24]{0,1:T(8,128)(2,1)} %param.36), channel_id=1, replica_groups=mesh['dp'=8,'seq'=4] {'dp','seq'}, dimensions={1}, use_global_device_ids=true | all-gather | bytes 101376 | tf_op jit(solution)/shard_map/all_gather | solution.py:223
  70.9 3.8 fusion.182
  80.8 38.0 %all-reduce.23 = (bf16[2304]{0:T(1024)(128)(2,1)S(1)}, bf16[768]{0:T(1024)(128)(2,1)S(1)}, bf16[768]{0:T(1024)(128)(2,1)S(1)}, bf16[2304]{0:T(1024)(128)(2,1)S(1...) all-reduce(bf16[2304]{0:T(1024)(128)(2,1)S(1)} %dynamic-update-slic, ...), channel_id=1, replica_groups=mesh['dp'=8,'seq'=4] {'dp','seq'}, use_global_device_ids=true, to_apply=%add.3 | all-reduce | flops 13056 | bytes 52224
  127.0 40.1 %all-gather = bf16[32,72,3]{1,2,0:T(4,128)(2,1)S(1)} all-gather(bf16[1,72,3]{1,2,0:T(4,128)(2,1)S(1)} %bitcast.544), channel_id=1, replica_groups=mesh['dp'=8,'seq'=4] {'dp','seq'}, dimensions={0}, use_global_device_ids=true | all-gather | bytes 14256 | tf_op jit(solution)/shard_map/all_gather | solution.py:220
  167.2 6.3 convolution_subtract_fusion.8
  173.5 4.7 fusion.12
  185.5 4.7 multiply_add_fusion.1
  195.8 4.2 all-to-all-start.2
  200.0 6.3 convolution_add_fusion.16
  212.7 4.4 all-to-all-start
  258.5 10.6 multiply_add_fusion.5
  286.2 4.4 all-to-all-start.3
  309.0 8.6 all-to-all-done.1
  318.3 6.6 multiply_convert_fusion.9
  330.0 8.3 fusion.680
  338.3 4.8 fusion.681
  343.1 10.3 fusion.699
  353.5 8.7 fusion.700
  370.9 5.7 fusion.103
  381.1 4.2 all-to-all-start.6
  385.3 5.6 fusion.98
  401.4 4.2 all-to-all-start.4
  438.5 3.9 convolution_add_fusion.12
  446.1 20.4 %subtract_add_fusion = (f32[192,32,128]{2,1,0:T(8,128)}, f32[192,32,128]{2,1,0:T(8,128)}, f32[192,32,128]{2,1,0:T(8,128)}, f32[192,32,128]{2,1,0:T(8,128)}, f32[192,32,128]{2,1,0:T(8,128)}, /*index=5*/f32[192,32,128]{2,1,0:T(8,128)}) fusion(f32[192,32,128]{2,1,0:T(8,128)} %convolution_subtract_fusion.6, f32[192,32,128]{2,1,0:T(8,128)} %convolution_subtract_fusion.2, ...), kind=kOutput, calls=%fused_computation.93 | convolution fusion | flops 628588544 | bytes 56655872 | tf_op jit(solution)/shard_map/ckm,mj->ckj/dot_general | solution.py:115
  497.0 4.2 all-to-all-start.5
  501.3 3.7 convolution_subtract_fusion.1
  518.4 4.0 convolution_multiply_fusion.3
  532.5 4.2 all-to-all-start.7
  554.0 4.6 slice_multiply_fusion.5
  562.7 10.0 multiply_reduce_fusion.5
  573.5 9.1 multiply_reduce_fusion.2
  582.6 4.9 fusion.166
  600.2 5.6 convolution_dynamic-update-slice_fusion
  605.9 5.0 convolution_add_fusion.18
  611.0 4.1 fusion.168
  615.1 5.4 convolution_add_fusion
  621.2 5.3 fusion.116
  626.6 5.4 convolution_add_fusion.2
  632.7 6.5 fusion.238
  639.3 10.0 convolution_add_fusion.1
  649.9 8.8 fusion.154
  658.7 8.2 fusion.158
  671.7 79.6 %all-reduce.26.cloned.1.call-done = (f32[768]{0:T(1024)}, f32[768]{0:T(1024)}, f32[2304]{0:T(1024)}, f32[3,2304]{1,0:T(4,128)}, f32[2304]{0:T(1024)}, /*index=5*...) async-done(((f32[768]{0:T(1024)}, f32[768]{0:T(1024)}, ...) | async-done | bytes 122128
  765.2 87.9 %reduce-scatter.17.cloned.1.call-done = f32[64,24]{0,1:T(8,128)} async-done(((f32[64,768]{0,1:T(8,128)}), f32[64,24]{0,1:T(8,128)}) %reduce-scatter.17.cloned.1.call-update) | async-done | bytes 6160
  853.1 104.8 %reduce-scatter.11.cloned.1.call-done = f32[768,24]{0,1:T(8,128)} async-done(((f32[768,768]{0,1:T(8,128)}), f32[768,24]{0,1:T(8,128)}) %reduce-scatter.11.cloned.1.call-update) | async-done | bytes 73744 | tf_op jit(solution)/shard_map/reduce_scatter | solution.py:490
  957.9 124.5 %reduce-scatter.9.cloned.1.call-done = f32[768,72]{0,1:T(8,128)} async-done(((f32[768,2304]{0,1:T(8,128)}), f32[768,72]{0,1:T(8,128)}) %reduce-scatter.9.cloned.1.call-update) | async-done | bytes 221200 | tf_op jit(solution)/shard_map/reduce_scatter | solution.py:484
  1082.5 142.3 %reduce-scatter.13.cloned.1.call-done = f32[768,96]{0,1:T(8,128)} async-done(((f32[768,3072]{0,1:T(8,128)}), f32[768,96]{0,1:T(8,128)}) %reduce-scatter.13.cloned.1.call-update) | async-done | bytes 294928 | tf_op jit(solution)/shard_map/reduce_scatter | solution.py:494
  1224.7 141.0 %reduce-scatter.15.cloned.1.call-done = f32[3072,24]{0,1:T(8,128)} async-done(((f32[3072,768]{0,1:T(8,128)}), f32[3072,24]{0,1:T(8,128)}) %reduce-scatter.15.cloned.1.call-update) | async-done | bytes 294928 | tf_op jit(solution)/shard_map/reduce_scatter | solution.py:496
  (554 shorter events, 309.8 us)
Async XLA Ops:
  7.2 50.7 %copy-start = (f32[64,64]{1,0:T(8,128)S(1)}, f32[64,64]{1,0:T(8,128)}, u32[]{:S(2)}) copy-start(f32[64,64]{1,0:T(8,128)} %param.47) | copy-start | bytes 49156
  7.2 57.7 %copy-start.104 = (f32[64]{0:T(128)S(1)}, f32[64]{0:T(128)}, u32[]{:S(2)}) copy-start(f32[64]{0:T(128)} %param.51) | copy-start | bytes 772
  7.2 166.3 %all-gather.6.cloned.1.call-start = ((), (), s32[]{:S(2)}) async-start(), calls=%async_computation.13 | async-start | bytes 3649536 | tf_op jit(solution)/shard_map/all_gather | solution.py:218
  8.0 316.9 %all-gather.8.cloned.1.call-start = ((), (), s32[]{:S(2)}) async-start(), calls=%async_computation.14 | async-start | bytes 1216512 | tf_op jit(solution)/shard_map/all_gather | solution.py:224
  8.7 321.2 %all-gather.10.cloned.1.call-start = ((), (), s32[]{:S(2)}) async-start(), calls=%async_computation.15 | async-start | bytes 4866048 | tf_op jit(solution)/shard_map/all_gather | solution.py:228
  9.4 333.7 %all-gather.12.cloned.1.call-start = ((), (), s32[]{:S(2)}) async-start(), calls=%async_computation.16 | async-start | bytes 4866048 | tf_op jit(solution)/shard_map/all_gather | solution.py:230
  10.2 57.7 %copy-start.100 = (f32[2048,1]{0,1:T(1,128)}, f32[2048,1]{0,1:T(1,128)S(1)}, u32[]{:S(2)}) copy-start(f32[2048,1]{0,1:T(1,128)S(1)} %convert_multiply_fusion.7) | copy-start | bytes 24580
  10.2 57.7 %copy-start.98 = (f32[2048]{0:T(1024)}, f32[2048]{0:T(1024)S(1)}, u32[]{:S(2)}) copy-start(f32[2048]{0:T(1024)S(1)} %multiply_negate_fusion) | copy-start | bytes 24580
  10.2 57.6 %copy-start.126 = (f32[192]{0:T(256)}, f32[192]{0:T(256)S(1)}, u32[]{:S(2)}) copy-start(f32[192]{0:T(256)S(1)} %add_abs_fusion) | copy-start | bytes 2308
  54.5 13.4 copy-start.78
  74.8 44.0 %copy-start.128 = (s32[2,2]{1,0:T(2,128)S(1)}, s32[2,2]{1,0:T(2,128)}, u32[]{:S(2)}) copy-start(s32[2,2]{1,0:T(2,128)} %param.27) | copy-start | bytes 52
  78.3 48.6 %copy-start.130 = (bf16[3,72]{1,0:T(4,128)(2,1)S(1)}, bf16[3,72]{1,0:T(4,128)(2,1)}, u32[]{:S(2)}) copy-start(bf16[3,72]{1,0:T(4,128)(2,1)} %param.33) | copy-start | bytes 1300
  118.7 61.7 %copy-start.79 = (f32[768]{0:T(1024)}, f32[768]{0:T(1024)S(1)}, u32[]{:S(2)}) copy-start(f32[768]{0:T(1024)S(1)} %convert_element_type.510) | copy-start | bytes 9220
  118.7 61.8 %copy-start.90 = (f32[768]{0:T(1024)}, f32[768]{0:T(1024)S(1)}, u32[]{:S(2)}) copy-start(f32[768]{0:T(1024)S(1)} %convert_element_type.511) | copy-start | bytes 9220
  121.0 52.5 %copy-start.102 = (f32[512]{0:T(512)}, f32[512]{0:T(512)S(1)}, u32[]{:S(2)}) copy-start(f32[512]{0:T(512)S(1)} %get-tuple-element.168) | copy-start | bytes 6148
  121.0 59.5 %copy-start.110 = (f32[512]{0:T(512)}, f32[512]{0:T(512)S(1)}, u32[]{:S(2)}) copy-start(f32[512]{0:T(512)S(1)} %get-tuple-element.169) | copy-start | bytes 6148
  123.0 50.5 %copy-start.106 = (f32[512]{0:T(512)}, f32[512]{0:T(512)S(1)}, u32[]{:S(2)}) copy-start(f32[512]{0:T(512)S(1)} %fusion.426) | copy-start | bytes 6148
  126.9 53.6 %copy-start.114 = (f32[512]{0:T(512)}, f32[512]{0:T(512)S(1)}, u32[]{:S(2)}) copy-start(f32[512]{0:T(512)S(1)} %fusion.424) | copy-start | bytes 6148
  178.3 6.5 collective-permute-start.1
  182.7 2.8 collective-permute-start
  195.8 17.0 %all-to-all-start.2 = ((bf16[4,192,512]{2,1,0:T(8,128)(2,1)}), bf16[4,192,512]{2,1,0:T(8,128)(2,1)}, u32[]{:S(2)}, u32[]{:S(2)}) async-start(bf16[4,192,512]{2,1,0:T(8,128)(2,1)} %bitcast.542), calls=%async_computation.2 | async-start | bytes 1572864 | tf_op jit(solution)/shard_map/all_to_all | solution.py:277
  212.7 20.3 %all-to-all-start = ((bf16[4,192,512]{2,1,0:T(8,128)(2,1)}), bf16[4,192,512]{2,1,0:T(8,128)(2,1)}, u32[]{:S(2)}, u32[]{:S(2)}) async-start(bf16[4,192,512]{2,1,0:T(8,128)(2,1)} %bitcast.7), calls=%async_computation | async-start | bytes 1572864 | tf_op jit(solution)/shard_map/all_to_all | solution.py:277
  286.2 16.1 %all-to-all-start.3 = ((bf16[192,4,512]{2,0,1:T(8,128)(2,1)}), bf16[192,4,512]{2,0,1:T(8,128)(2,1)}, u32[]{:S(2)}, u32[]{:S(2)}) async-start(bf16[192,4,512]{2,0,1:T(8,128)(2,1)} %copy.103), calls=%async_computation.3 | async-start | bytes 1572864 | tf_op jit(solution)/shard_map/all_to_all | solution.py:287
  302.2 15.3 %all-to-all-start.1 = ((bf16[192,4,512]{2,0,1:T(8,128)(2,1)}), bf16[192,4,512]{2,0,1:T(8,128)(2,1)S(1)}, u32[]{:S(2)}, u32[]{:S(2)}) async-start(bf16[192,4,512]{2,0,1:T(8,128)(2,1)} %copy.99), calls=%async_computation.1 | async-start | bytes 1572864 | tf_op jit(solution)/shard_map/all_to_all | solution.py:287
  306.0 62.2 %copy-start.87 = (f32[768]{0:T(1024)}, f32[768]{0:T(1024)S(1)}, u32[]{:S(2)}) copy-start(f32[768]{0:T(1024)S(1)} %convert_element_type.533) | copy-start | bytes 9220
  306.0 32.3 %copy-start.92 = (f32[768]{0:T(1024)}, f32[768]{0:T(1024)S(1)}, u32[]{:S(2)}) copy-start(f32[768]{0:T(1024)S(1)} %convert_element_type.534) | copy-start | bytes 9220
  306.0 47.5 %copy-start.122 = (f32[3072]{0:T(1024)}, f32[3072]{0:T(1024)S(1)}, u32[]{:S(2)}) copy-start(f32[3072]{0:T(1024)S(1)} %convert_element_type.536) | copy-start | bytes 36868
  327.5 40.7 %copy-start.116 = (f32[512]{0:T(512)}, f32[512]{0:T(512)S(1)}, u32[]{:S(2)}) copy-start(f32[512]{0:T(512)S(1)} %broadcast_multiply_fusion.2) | copy-start | bytes 6148
  329.6 35.4 %copy-start.41 = (f32[512,768]{1,0:T(8,128)}, f32[512,768]{1,0:T(8,128)S(1)}, u32[]{:S(2)}) copy-start(f32[512,768]{1,0:T(8,128)S(1)} %get-tuple-element.158) | copy-start | bytes 4718596
  329.6 38.6 %copy-start.108 = (f32[512]{0:T(512)}, f32[512]{0:T(512)S(1)}, u32[]{:S(2)}) copy-start(f32[512]{0:T(512)S(1)} %broadcast_multiply_fusion) | copy-start | bytes 6148
  329.9 38.3 %copy-start.124 = (f32[512]{0:T(512)}, f32[512]{0:T(512)S(1)}, u32[]{:S(2)}) copy-start(f32[512]{0:T(512)S(1)} %fusion.425) | copy-start | bytes 6148
  329.9 38.3 %copy-start.112 = (f32[512]{0:T(512)}, f32[512]{0:T(512)S(1)}, u32[]{:S(2)}) copy-start(f32[512]{0:T(512)S(1)} %fusion.427) | copy-start | bytes 6148
  343.1 10.4 copy-start.146
  343.1 19.2 %slice-start = ((s8[4718592]{0:T(1024)(128)(4,1)}), s8[4194304]{0:T(1024)(128)(4,1)S(1)}, s32[]{:S(2)}) async-start(s8[4718592]{0:T(1024)(128)(4,1)} %bitcast.545), calls=%async_computation.23 | async-start | bytes 8388608
  370.9 14.4 %copy-start.25 = (f32[512,768]{1,0:T(8,128)}, f32[512,768]{1,0:T(8,128)S(1)}, u32[]{:S(2)}) copy-start(f32[512,768]{1,0:T(8,128)S(1)} %get-tuple-element.142) | copy-start | bytes 4718596
  370.9 26.9 %copy-start.6 = (f32[512,768]{1,0:T(8,128)}, f32[512,768]{1,0:T(8,128)S(1)}, u32[]{:S(2)}) copy-start(f32[512,768]{1,0:T(8,128)S(1)} %get-tuple-element.105) | copy-start | bytes 4718596
  381.1 20.2 %all-to-all-start.6 = ((bf16[4,192,512]{2,1,0:T(8,128)(2,1)}), bf16[4,192,512]{2,1,0:T(8,128)(2,1)}, u32[]{:S(2)}, u32[]{:S(2)}) async-start(bf16[4,192,512]{2,1,0:T(8,128)(2,1)} %bitcast.541), calls=%async_computation.6 | async-start | bytes 1572864 | tf_op jit(solution)/shard_map/all_to_all | solution.py:352
  401.4 15.9 %all-to-all-start.4 = ((bf16[4,192,512]{2,1,0:T(8,128)(2,1)}), bf16[4,192,512]{2,1,0:T(8,128)(2,1)}, u32[]{:S(2)}, u32[]{:S(2)}) async-start(bf16[4,192,512]{2,1,0:T(8,128)(2,1)} %bitcast.540), calls=%async_computation.4 | async-start | bytes 1572864 | tf_op jit(solution)/shard_map/all_to_all | solution.py:352
  497.0 35.4 %all-to-all-start.5 = ((bf16[192,4,512]{2,0,1:T(8,128)(2,1)}), bf16[192,4,512]{2,0,1:T(8,128)(2,1)}, u32[]{:S(2)}, u32[]{:S(2)}) async-start(bf16[192,4,512]{2,0,1:T(8,128)(2,1)} %copy.107), calls=%async_computation.5 | async-start | bytes 1572864 | tf_op jit(solution)/shard_map/all_to_all | solution.py:375
  532.5 15.9 %all-to-all-start.7 = ((bf16[192,4,512]{2,0,1:T(8,128)(2,1)}), bf16[192,4,512]{2,0,1:T(8,128)(2,1)}, u32[]{:S(2)}, u32[]{:S(2)}) async-start(bf16[192,4,512]{2,0,1:T(8,128)(2,1)} %copy.111), calls=%async_computation.7 | async-start | bytes 1572864 | tf_op jit(solution)/shard_map/all_to_all | solution.py:375
  536.7 214.6 %all-reduce.26.cloned.1.call-start = ((), (), s32[]{:S(2)}) async-start(), calls=%async_computation.22 | async-start | bytes 380928
  558.9 3.4 collective-permute-start.2
  560.7 12.0 collective-permute-start.3
  599.0 254.1 %reduce-scatter.17.cloned.1.call-start = ((), (), s32[]{:S(2)}) async-start(), calls=%async_computation.21 | async-start | bytes 405504
  605.8 352.1 %reduce-scatter.11.cloned.1.call-start = ((), (), s32[]{:S(2)}) async-start(), calls=%async_computation.18 | async-start | bytes 2433024 | tf_op jit(solution)/shard_map/reduce_scatter | solution.py:490
  610.9 471.5 %reduce-scatter.9.cloned.1.call-start = ((), (), s32[]{:S(2)}) async-start(), calls=%async_computation.17 | async-start | bytes 7299072 | tf_op jit(solution)/shard_map/reduce_scatter | solution.py:484
  620.6 604.1 %reduce-scatter.13.cloned.1.call-start = ((), (), s32[]{:S(2)}) async-start(), calls=%async_computation.19 | async-start | bytes 9732096 | tf_op jit(solution)/shard_map/reduce_scatter | solution.py:494
  632.1 733.6 %reduce-scatter.15.cloned.1.call-start = ((), (), s32[]{:S(2)}) async-start(), calls=%async_computation.20 | async-start | bytes 9732096 | tf_op jit(solution)/shard_map/reduce_scatter | solution.py:496
  (123 other events, 486.1 us)
Sparse Core Ops, SparseCore 0:
  11.0 62.9 all-gather.5
  76.8 52.9 all-gather.7
  132.7 62.5 all-gather.9
  198.0 63.0 all-gather.11
  599.1 152.1 all-reduce.25
  756.6 96.4 reduce-scatter.16
  859.8 98.0 reduce-scatter.10
  964.2 118.2 reduce-scatter.8
  1089.9 134.7 reduce-scatter.12
  1231.0 134.6 reduce-scatter.14
where the time goes:
time: 1390 us; the launch traced here: 1380 us
  waiting for transfers between devices  704 us (51%)
  matrix products  336 us (24%)
  blocking collectives  122 us (9%)
  local copies, waits for them, and re-layouts  88.3 us (6%)
  other arithmetic  70 us (5%)
  starting transfers between devices  41.8 us (3%)
  between operations  19.5 us (1%)
    unnamed x12, waiting for transfers between devices  170 us
    reduce_scatter x1, waiting for transfers between devices, per_device(): lax.psum_scatter(trailing_sums[4], ('dp', 'seq'), scatter_dimension=1, ti...  142 us
    reduce_scatter x1, waiting for transfers between devices, per_device(): lax.psum_scatter(trailing_sums[6], ('dp', 'seq'), scatter_dimension=1, ti...  141 us
    dot_general x40, matrix products, lane_mul(): jnp.einsum('ckm,mj->ckj', values, table, precision=lax.Precision.HIGH)  141 us
    reduce_scatter x1, waiting for transfers between devices, per_device(): lax.psum_scatter(leading_sums[2], ('dp', 'seq'), scatter_dimension=1, til...  125 us
    reduce_scatter x1, waiting for transfers between devices, per_device(): lax.psum_scatter(trailing_sums[0], ('dp', 'seq'), scatter_dimension=1, ti...  105 us
    all_gather x1, blocking collectives, per_device(): lax.all_gather(filter_final_coefficients, ('dp', 'seq'), axis=1, tiled=True)  44.2 us
    unnamed x337, local copies, waits for them, and re-layouts  41.5 us
  transfers between devices with their start and end apart: 22, of which 13 were waited for; matrix products, arithmetic and copies ran while one was open for 23% of the time, Pallas kernels for 0%

commit v1 on v0

v1 whole, which is shorter than its diff:
```python
import math

import jax
import jax.numpy as jnp
import ml_dtypes
import numpy as np
from jax import lax
from jax.experimental import pallas as pl
from jax.experimental.pallas import tpu as pltpu
from jax.sharding import PartitionSpec as P

AXES = ("dp", "seq")

F32=jnp.float32; BF=jnp.bfloat16
RADIX=16

def dft_tables(length):
    padded = 2*length
    inner = padded//RADIX
    pairs = RADIX//4
    half = RADIX//2
    m = np.arange(inner)
    mats=[]
    for p in range(pairs):
        for s in (p, half-1-p):
            k2 = 2*(RADIX*m+s)+1
            ang = np.pi*((k2[:,None]*m[None,:])%(2*padded))/padded
            c,sn=np.cos(ang),np.sin(ang)
            mats.append(np.block([[c,sn],[-sn,c]]))
    fwd=np.stack(mats).reshape(pairs,2,2*inner,2*inner)
    inv=np.swapaxes(fwd,-1,-2)/length
    r=np.arange(half)
    th=np.pi*(r[None,:]*(2*np.arange(pairs)[:,None]+1))/RADIX
    coef=np.concatenate([np.cos(th),np.sin(th)],axis=1).astype(np.float32)
    return fwd.astype(ml_dtypes.bfloat16),inv.astype(ml_dtypes.bfloat16),coef

def split_rows(x_ref,coef_ref,p,z_ref,inner):
    step=16
    @pl.loop(0,inner//step)
    def _(i):
        lo=pl.multiple_of(i*step,step)
        rows=pl.ds(lo,step); low=pl.ds(pl.multiple_of(inner+i*step,step),step)
        xs=[x_ref[r,rows,:].astype(F32) for r in range(8)]
        c=[coef_ref[p,r] for r in range(8)]; s=[coef_ref[p,8+r] for r in range(8)]
        ce=xs[0]+c[2]*xs[2]+c[4]*xs[4]+c[6]*xs[6]
        co=c[1]*xs[1]+c[3]*xs[3]+c[5]*xs[5]+c[7]*xs[7]
        se=s[2]*xs[2]+s[4]*xs[4]+s[6]*xs[6]
        so=s[1]*xs[1]+s[3]*xs[3]+s[5]*xs[5]+s[7]*xs[7]
        z_ref[0,rows,:]=(ce+co).astype(BF)
        z_ref[1,rows,:]=(ce-co).astype(BF)
        z_ref[0,low,:]=(-(se+so)).astype(BF)
        z_ref[1,low,:]=(se-so).astype(BF)

def join_rows(w_ref,coef_ref,p,acc_ref,inner,lanes):
    step=16
    @pl.loop(0,inner//step)
    def _(i):
        lo=pl.multiple_of(i*step,step)
        rows=pl.ds(lo,step); low=pl.ds(pl.multiple_of(inner+i*step,step),step)
        r0=w_ref[0,rows,lanes]; r1=w_ref[1,rows,lanes]
        i0=w_ref[0,low,lanes]; i1=w_ref[1,low,lanes]
        rs=(r0+r1,r0-r1); im=(i0-i1,i0+i1)
        for r in range(8):
            if r==0: term=rs[0]
            else: term=coef_ref[p,r]*rs[r%2]-coef_ref[p,8+r]*im[r%2]
            acc_ref[r,rows,:]=jnp.where(p==0,0.0,acc_ref[r,rows,:])+term

def spec_kernel(coef_ref,x_ref,f_ref,o_ref,z_ref):
    p=pl.program_id(0); inner=x_ref.shape[1]
    split_rows(x_ref,coef_ref,p,z_ref,inner)
    for j in range(2):
        o_ref[0,j]=jnp.dot(f_ref[0,j],z_ref[j],preferred_element_type=F32).astype(o_ref.dtype)

def conv_kernel(coef_ref,x_ref,k_ref,f_ref,b_ref,s_ref,y_ref,z_ref,w_ref,acc_ref):
    p=pl.program_id(0); inner=x_ref.shape[1]
    split_rows(x_ref,coef_ref,p,z_ref,inner)
    for j in range(2):
        w_ref[j]=jnp.dot(f_ref[0,j],z_ref[j],preferred_element_type=F32)
    step=16
    for j in range(2):
        @pl.loop(0,inner//step)
        def _(i):
            rows=pl.ds(pl.multiple_of(i*step,step),step); low=pl.ds(pl.multiple_of(inner+i*step,step),step)
            xr=w_ref[j,rows,:]; xi=w_ref[j,low,:]
            kr=k_ref[0,j,rows,:].astype(F32); ki=k_ref[0,j,low,:].astype(F32)
            s_ref[0,j,rows,:]=xr.astype(BF); s_ref[0,j,low,:]=xi.astype(BF)
            z_ref[j,rows,:]=(xr*kr-xi*ki).astype(BF)
            z_ref[j,low,:]=(xr*ki+xi*kr).astype(BF)
    for j in range(2):
        w_ref[j]=jnp.dot(b_ref[0,j],z_ref[j],preferred_element_type=F32)
    join_rows(w_ref,coef_ref,p,acc_ref,inner,slice(None))
    @pl.when(p==pl.num_programs(0)-1)
    def _():
        @pl.loop(0,inner//step)
        def _(i):
            rows=pl.ds(pl.multiple_of(i*step,step),step)
            for r in range(8):
                y_ref[r,rows,:]=acc_ref[r,rows,:].astype(y_ref.dtype)

def back_kernel(coef_ref,g_ref,k_ref,s_ref,f_ref,b_ref,y_ref,kg_ref,z_ref,w_ref,q_ref,v_ref,acc_ref):
    p=pl.program_id(0); inner=g_ref.shape[1]; chans=g_ref.shape[2]
    split_rows(g_ref,coef_ref,p,z_ref,inner)
    for j in range(2):
        w_ref[j]=jnp.dot(f_ref[0,j],z_ref[j],preferred_element_type=F32)
    step=16
    for j in range(2):
        @pl.loop(0,inner//step)
        def _(i):
            rows=pl.ds(pl.multiple_of(i*step,step),step); low=pl.ds(pl.multiple_of(inner+i*step,step),step)
            gr=w_ref[j,rows,:]; gi=w_ref[j,low,:]
            kr=k_ref[0,j,rows,:].astype(F32); ki=k_ref[0,j,low,:].astype(F32)
            q_ref[j,rows,0:chans]=(gr*kr+gi*ki).astype(BF)
            q_ref[j,low,0:chans]=(gi*kr-gr*ki).astype(BF)
            kr=s_ref[0,j,rows,:].astype(F32); ki=s_ref[0,j,low,:].astype(F32)
            q_ref[j,rows,chans:2*chans]=(gr*kr+gi*ki).astype(BF)
            q_ref[j,low,chans:2*chans]=(gi*kr-gr*ki).astype(BF)
    for j in range(2):
        v_ref[j]=jnp.dot(b_ref[0,j],q_ref[j],preferred_element_type=F32)
    join_rows(v_ref,coef_ref,p,acc_ref,inner,slice(0,chans))
    join_rows(v_ref,coef_ref,p,kg_ref,inner,slice(chans,2*chans))
    @pl.when(p==pl.num_programs(0)-1)
    def _():
        @pl.loop(0,inner//step)
        def _(i):
            rows=pl.ds(pl.multiple_of(i*step,step),step)
            for r in range(8):
                y_ref[r,rows,:]=acc_ref[r,rows,:].astype(y_ref.dtype)

PAR=pltpu.CompilerParams(vmem_limit_bytes=52<<20)
SM=pl.BlockSpec(memory_space=pltpu.SMEM)
def whole(shape): return pl.BlockSpec(shape,lambda p:(0,)*len(shape))
def step_of(shape): return pl.BlockSpec((1,)+shape,lambda p:(p,)+(0,)*len(shape))

def spectrum(x,tables):
    fwd,inv,coef=tables
    length,ch=x.shape; inner=2*length//RADIX
    return pl.pallas_call(spec_kernel,grid=(RADIX//4,),
        in_specs=[SM,whole((8,inner,ch)),step_of((2,2*inner,2*inner))],
        out_specs=step_of((2,2*inner,ch)),
        out_shape=jax.ShapeDtypeStruct((RADIX//4,2,2*inner,ch),F32),
        scratch_shapes=[pltpu.VMEM((2,2*inner,ch),BF)],compiler_params=PAR)(coef,x.reshape(8,inner,ch),fwd)

def long_conv(x,kspec,tables):
    fwd,inv,coef=tables
    length,ch=x.shape; inner=2*length//RADIX
    s,y=pl.pallas_call(conv_kernel,grid=(RADIX//4,),
        in_specs=[SM,whole((8,inner,ch)),step_of((2,2*inner,ch)),step_of((2,2*inner,2*inner)),step_of((2,2*inner,2*inner))],
        out_specs=[step_of((2,2*inner,ch)),whole((8,inner,ch))],
        out_shape=[jax.ShapeDtypeStruct((RADIX//4,2,2*inner,ch),BF),jax.ShapeDtypeStruct((8,inner,ch),F32)],
        scratch_shapes=[pltpu.VMEM((2,2*inner,ch),BF),pltpu.VMEM((2,2*inner,ch),F32),pltpu.VMEM((8,inner,ch),F32)],compiler_params=PAR)(coef,x.reshape(8,inner,ch),kspec,fwd,inv)
    return s,y.reshape(length,ch)

def long_back(g,kspec,sspec,tables):
    fwd,inv,coef=tables
    length,ch=g.shape; inner=2*length//RADIX
    y,kg=pl.pallas_call(back_kernel,grid=(RADIX//4,),
        in_specs=[SM,whole((8,inner,ch)),step_of((2,2*inner,ch)),step_of((2,2*inner,ch)),step_of((2,2*inner,2*inner)),step_of((2,2*inner,2*inner))],
        out_specs=[whole((8,inner,ch)),whole((8,inner,ch))],
        out_shape=[jax.ShapeDtypeStruct((8,inner,ch),F32),jax.ShapeDtypeStruct((8,inner,ch),F32)],
        scratch_shapes=[pltpu.VMEM((2,2*inner,ch),BF),pltpu.VMEM((2,2*inner,ch),F32),pltpu.VMEM((2,2*inner,2*ch),BF),pltpu.VMEM((2,2*inner,2*ch),F32),pltpu.VMEM((8,inner,ch),F32)],compiler_params=PAR)(coef,g.reshape(8,inner,ch),kspec,sspec,fwd,inv)
    return y.reshape(length,ch),kg.reshape(length,ch)

def product(left, right):
    return jnp.dot(left, right, precision=lax.Precision.HIGHEST, preferred_element_type=jnp.float32)

def gelu_tanh(values):
    return jax.nn.gelu(values, approximate=True)

def filter_hidden(
    features,
    filter_entry_coefficients,
    filter_entry_offset,
    filter_second_coefficients,
    filter_second_offset,
    filter_third_coefficients,
    filter_third_offset,
    periodic_frequency,
):
    first = jnp.sin(
        periodic_frequency * (product(features, filter_entry_coefficients) + filter_entry_offset)
    )
    middle = jnp.sin(
        periodic_frequency * (product(first, filter_second_coefficients) + filter_second_offset)
    )
    return jnp.sin(
        periodic_frequency * (product(middle, filter_third_coefficients) + filter_third_offset)
    )

def modulation(length, model_width, offset, channels):
    standardized_values = jnp.arange(length).astype(jnp.float32) / (length - 1)
    slowest = math.log(0.01) / 1.5
    fastest = math.log(0.01) / 0.3
    columns = (offset + jnp.arange(channels)).astype(jnp.float32)
    decays = slowest + (fastest - slowest) * columns / (model_width - 1)
    return jnp.exp(-standardized_values[:, None] * jnp.abs(decays)[None, :]) + 0.05

def position_features(length, emb_width):
    band_count = (emb_width - 1) // 2
    places = np.arange(length, dtype=np.float64)
    band_rates = 0.0001 + (band_count - 1 - 0.0001) * np.arange(band_count) / (band_count - 1)
    phases = (2.0 * math.pi * places / length)[:, None] * band_rates[None, :]
    return np.concatenate(
        [(places / (length - 1))[:, None], np.cos(phases), -np.sin(phases)], axis=1
    ).astype(np.float32)


def swap_bit(value, me, bit, count):
    return lax.ppermute(value, AXES, [(i, i ^ (1 << bit)) for i in range(count)])


def bit_of(me, bit):
    return (me >> bit) & 1


def gather_shards(value, me, count, order):
    held = value
    for bit in order[:-1]:
        held = jnp.concatenate([held, swap_bit(held, me, bit, count)], axis=0)
    other = swap_bit(held, me, order[-1], count)
    return place_shards(held, other, me, count, order)


def place_shards(near, other, me, count, order):
    rows = near.shape[0] * 2 // count
    half = count // 2

    def spread(i):
        return sum(((i >> p) & 1) << bit for p, bit in enumerate(order[:-1]))

    def kernel(me_ref, near_ref, other_ref, out_ref, sems):
        own = me_ref[0]
        copies = []
        for i in range(half):
            at = jnp.bitwise_xor(own, spread(i))
            copies.append(pltpu.make_async_copy(near_ref.at[i], out_ref.at[at], sems.at[i]))
            flip = jnp.bitwise_xor(own, spread(i) | (1 << order[-1]))
            copies.append(
                pltpu.make_async_copy(other_ref.at[i], out_ref.at[flip], sems.at[half + i])
            )
        for copy in copies:
            copy.start()
        for copy in copies:
            copy.wait()

    hbm = pl.BlockSpec(memory_space=pl.ANY)
    shape = (count, rows) + near.shape[1:]
    return pl.pallas_call(
        kernel,
        in_specs=[SM, hbm, hbm],
        out_specs=hbm,
        out_shape=jax.ShapeDtypeStruct(shape, near.dtype),
        scratch_shapes=[pltpu.SemaphoreType.DMA((count,))],
    )(
        me.reshape(1).astype(jnp.int32),
        near.reshape((half, rows) + near.shape[1:]),
        other.reshape((half, rows) + near.shape[1:]),
    )


def scatter_sum(value, me, count, order, keep):
    rows, columns = value.shape[1:]
    left = list(range(count.bit_length() - 1))
    for place, bit in enumerate(order):
        low = 1 << sum(1 for b in left if b < bit)
        cut = value.reshape(-1, 2, low * rows, columns)
        mine = lax.dynamic_index_in_dim(cut, bit_of(me, bit), 1, keepdims=False)
        given = lax.dynamic_index_in_dim(cut, 1 - bit_of(me, bit), 1, keepdims=False)
        value = mine.astype(F32) + swap_bit(given, me, bit, count).astype(F32)
        if place < len(order) - 1:
            value = value.astype(keep)
        left.remove(bit)
    return value.reshape(rows, columns)


def sum_everywhere(value, me, count):
    for bit in range(count.bit_length() - 1):
        value = value + swap_bit(value, me, bit, count)
    return value


def orders_of(count):
    bits = count.bit_length() - 1
    first = list(range(bits))
    second = list(range(bits))
    second[1], second[2] = second[2], second[1]
    return first, second


def normalise(values):
    centre = values - jnp.mean(values, axis=-1, keepdims=True)
    spread = jnp.mean(centre * centre, axis=-1, keepdims=True)
    rstd = lax.rsqrt(spread + 1e-05)
    return centre * rstd, rstd


def normalise_back(unit, rstd, incoming):
    return rstd * (
        incoming
        - jnp.mean(incoming, axis=-1, keepdims=True)
        - unit * jnp.mean(incoming * unit, axis=-1, keepdims=True)
    )


def dot_nt(left, right):
    return lax.dot_general(left, right, (((1,), (1,)), ((), ())), preferred_element_type=F32)


def dot_nn(left, right):
    return lax.dot_general(left, right, (((1,), (0,)), ((), ())), preferred_element_type=F32)


def dot_tn(left, right):
    return lax.dot_general(left, right, (((0,), (0,)), ((), ())), preferred_element_type=F32)


def per_device(
    block_input,
    slot_spans,
    output_adjoint,
    opening_scale_factor,
    opening_offset_vector,
    intake_coefficients,
    intake_offset,
    brief_filter_coefficients,
    brief_filter_offset,
    direct_path_factor,
    filter_final_coefficients,
    mixer_output_coefficients,
    mixer_output_offset,
    closing_scale_factor,
    closing_offset_vector,
    expand_coefficients,
    expand_offset,
    contract_coefficients,
    contract_offset,
    filter_entry_coefficients,
    filter_entry_offset,
    filter_second_coefficients,
    filter_second_offset,
    filter_third_coefficients,
    filter_third_offset,
    periodic_frequency,
):
    width = block_input.shape[2]
    local = block_input.shape[1]
    seq_count = lax.axis_size("seq")
    count = lax.axis_size("dp") * seq_count
    seq_index = lax.axis_index("seq")
    me = lax.axis_index("dp") * seq_count + seq_index
    half = seq_count // 2
    group_bits = half.bit_length() - 1
    rank = seq_index % half
    side = seq_index // half
    length = local * seq_count
    channels = width // half
    chan_start = rank * channels
    up, across = orders_of(count)
    down, back = up[::-1], across[::-1]
    tables = tuple(jnp.asarray(t) for t in dft_tables(length))

    vectors = (
        opening_scale_factor,
        opening_offset_vector,
        direct_path_factor,
        mixer_output_offset,
        closing_scale_factor,
        closing_offset_vector,
        contract_offset,
        intake_offset,
        brief_filter_offset,
        brief_filter_coefficients,
        expand_offset,
        filter_final_coefficients,
    )
    pack = jnp.concatenate([v.reshape(-1) for v in vectors])
    pad = -pack.size % 1024
    pack = jnp.concatenate([pack, jnp.zeros((pad,), pack.dtype)]).reshape(8, -1).astype(F32)
    pack_full = gather_shards(pack, me, count, down).reshape(count, -1)
    fields = []
    at = 0
    for v in vectors:
        part = pack_full[:, at : at + v.size]
        at += v.size
        if v.ndim == 1:
            fields.append(part.reshape(-1).astype(F32))
        else:
            rows = v.shape[0]
            fields.append(
                part.reshape(count, rows, -1).transpose(1, 0, 2).reshape(rows, -1).astype(F32)
            )
    (
        gain_one,
        shift_one,
        skip_gain,
        mix_bias,
        gain_two,
        shift_two,
        down_bias,
        intake_bias,
        conv_bias,
        conv_taps,
        up_bias,
        filter_final,
    ) = fields

    intake_shard = intake_coefficients.T
    middle = width // 2
    intake_t = jnp.concatenate(
        [
            gather_shards(intake_shard[:, :middle], me, count, down).reshape(-1, middle),
            gather_shards(intake_shard[:, middle:], me, count, back).reshape(-1, middle),
        ],
        axis=1,
    )

    far = half.bit_length() - 1
    own_rows = lax.dynamic_index_in_dim(block_input, side, 0, keepdims=False)
    far_rows = swap_bit(
        lax.dynamic_index_in_dim(block_input, 1 - side, 0, keepdims=False), me, far, count
    )
    tokens_low = jnp.concatenate([own_rows, far_rows], axis=0)

    intake_t, mix_own, up_own, down_own = lax.optimization_barrier(
        (
            intake_t,
            mixer_output_coefficients.T,
            expand_coefficients.T,
            contract_coefficients.T,
        )
    )
    mix_t = gather_shards(mix_own, me, count, down).reshape(-1, width)
    up_t = gather_shards(up_own, me, count, back).reshape(-1, width)
    down_t = gather_shards(down_own, me, count, down).reshape(width, -1)

    own_adj = lax.dynamic_index_in_dim(output_adjoint, side, 0, keepdims=False)
    far_adj = swap_bit(
        lax.dynamic_index_in_dim(output_adjoint, 1 - side, 0, keepdims=False), me, far, count
    )
    adjoint = jnp.concatenate([own_adj, far_adj], axis=0)

    features = jnp.asarray(position_features(length, filter_entry_coefficients.shape[0]))
    net = (
        filter_entry_coefficients,
        filter_entry_offset,
        filter_second_coefficients,
        filter_second_offset,
        filter_third_coefficients,
        filter_third_offset,
        periodic_frequency,
    )
    hidden, filter_pull = jax.vjp(lambda *w: filter_hidden(features, *w), *net)
    shaping = modulation(length, width, chan_start, channels)
    columns = lax.dynamic_slice_in_dim(filter_final, chan_start, channels, 1)
    kernel_spec = spectrum(product(hidden, columns) * shaping, tables)

    own_base = seq_index * local
    far_base = ((1 - side) * half + rank) * local
    places = jnp.concatenate(
        [own_base + jnp.arange(local), far_base + jnp.arange(local)]
    ).astype(jnp.int32)
    span = lax.dynamic_index_in_dim(slot_spans, side, 0, keepdims=False)
    row_mask = ((places >= span[0]) & (places < span[0] + span[1])).astype(F32)[:, None]
    tokens = tokens_low.astype(F32)
    unit_one, rstd_one = normalise(tokens)
    normed_low = (unit_one * gain_one + shift_one).astype(BF)
    projected = row_mask * (dot_nt(normed_low, intake_t) + intake_bias)
    blocks = projected.reshape(2, local, -1)

    def ring(value, by):
        pairs = []
        for i in range(count):
            group, r = divmod(i, half)
            pairs.append((i, group * half + (r + by) % half))
        return lax.ppermute(value, AXES, pairs)

    ends = ring(blocks[:, local - 2 :], 1)
    wrapped = jnp.stack(
        [jnp.where(side == 1, ends[1], 0.0), jnp.where(side == 0, ends[0], 0.0)]
    )
    before = jnp.where(rank == 0, wrapped, ends)
    extended = jnp.concatenate([before, blocks], axis=1)
    rows = 2 * local

    def shifted(by):
        return extended[:, by : by + local].reshape(rows, -1)

    conv_out = (
        conv_bias
        + conv_taps[0] * shifted(0)
        + conv_taps[1] * shifted(1)
        + conv_taps[2] * shifted(2)
    )
    outer_gate = conv_out[:, :width]
    inner_gate = conv_out[:, width : 2 * width]
    values = conv_out[:, 2 * width :]
    signal = (row_mask * inner_gate * values).astype(BF)

    def traded(near, give):
        got = [near]
        for k in range(1, half):
            got.append(lax.ppermute(give(k), AXES, [(i, i ^ k) for i in range(count)]))
        if half == 2:
            return jnp.where(rank == 0, got[0], got[1]), jnp.where(rank == 0, got[1], got[0])
        stacked = jnp.take(jnp.stack(got), jnp.arange(half) ^ rank, axis=0)
        return tuple(stacked[k] for k in range(half))

    def to_channels(value):
        def give(k):
            return lax.dynamic_slice_in_dim(value, (rank ^ k) * channels, channels, 1)

        pieces = traded(give(0), give)
        first = [jnp.where(side == 0, p[:local], p[local:]) for p in pieces]
        second = [jnp.where(side == 0, p[local:], p[:local]) for p in pieces]
        return jnp.concatenate(first + second, axis=0)

    def to_rows(value):
        def give(k):
            first = lax.dynamic_slice_in_dim(value, (rank ^ k) * local, local, 0)
            second = lax.dynamic_slice_in_dim(value, (half + (rank ^ k)) * local, local, 0)
            return jnp.concatenate(
                [jnp.where(side == 0, first, second), jnp.where(side == 0, second, first)], axis=0
            )

        return jnp.concatenate(traded(give(0), give), axis=1)

    sig_spec, carried_cols = long_conv(to_channels(signal), kernel_spec, tables)
    carried = to_rows(carried_cols.astype(BF)).astype(F32)
    signal_wide = signal.astype(F32)
    joined = carried + skip_gain * signal_wide
    gated_mix = (joined * outer_gate).astype(BF)
    residual = tokens + dot_nt(gated_mix, mix_t) + mix_bias
    unit_two, rstd_two = normalise(residual)
    second_low = (unit_two * gain_two + shift_two).astype(BF)
    up_proj = dot_nt(second_low, up_t) + up_bias
    active_low, gelu_pull = jax.vjp(gelu_tanh, up_proj)
    active_low = active_low.astype(BF)
    output = (row_mask * (residual + dot_nt(active_low, down_t) + down_bias)).astype(BF)

    def to_home(value):
        far_part = swap_bit(value[local:], me, far, count)
        near = value[:local]
        return jnp.where(side == 0, jnp.stack([near, far_part]), jnp.stack([far_part, near]))

    output_home = to_home(output)

    grad_out = row_mask * adjoint.astype(F32)
    grad_low = grad_out.astype(BF)
    down_bias_grad = jnp.sum(grad_out, axis=0)
    down_grad = dot_tn(grad_low, active_low).astype(BF)
    grad_up = gelu_pull(dot_nn(grad_low, down_t))[0]
    up_bias_grad = jnp.sum(grad_up, axis=0)
    grad_up_low = grad_up.astype(BF)
    up_grad = dot_tn(grad_up_low, second_low).astype(BF)
    grad_second = dot_nn(grad_up_low, up_t)
    gain_two_grad = jnp.sum(grad_second * unit_two, axis=0)
    shift_two_grad = jnp.sum(grad_second, axis=0)
    grad_residual = grad_out + normalise_back(unit_two, rstd_two, grad_second * gain_two)
    mix_bias_grad = jnp.sum(grad_residual, axis=0)
    resid_low = grad_residual.astype(BF)
    mix_grad = dot_tn(resid_low, gated_mix).astype(BF)
    down_shard = scatter_sum(down_grad.reshape(count, -1, down_grad.shape[1]), me, count, up, BF)
    up_shard = scatter_sum(up_grad.reshape(count, -1, width), me, count, across, BF)
    mix_shard = scatter_sum(mix_grad.reshape(count, -1, width), me, count, up, BF)

    grad_gated = dot_nn(resid_low, mix_t)
    grad_joined = grad_gated * outer_gate
    skip_grad = jnp.sum(grad_joined * signal_wide, axis=0)
    conv_back_cols, kernel_grad = long_back(
        to_channels(grad_joined.astype(BF)), kernel_spec, sig_spec, tables
    )
    conv_back = to_rows(conv_back_cols.astype(BF)).astype(F32)
    grad_signal = row_mask * (conv_back + skip_gain * grad_joined)
    grad_conv = jnp.concatenate(
        [grad_gated * joined, grad_signal * values, grad_signal * inner_gate], axis=1
    )
    conv_bias_grad = jnp.sum(grad_conv, axis=0)
    taps_grad = jnp.stack([jnp.sum(grad_conv * shifted(k), axis=0) for k in range(3)])
    conv_blocks = grad_conv.reshape(2, local, -1)
    starts = ring(conv_blocks[:, :2], -1)
    wrapped_after = jnp.stack(
        [jnp.where(side == 0, starts[1], 0.0), jnp.where(side == 1, starts[0], 0.0)]
    )
    after = jnp.where(rank == half - 1, wrapped_after, starts)
    grad_extended = jnp.concatenate([conv_blocks, after], axis=1)

    def ahead(by):
        return grad_extended[:, by : by + local].reshape(rows, -1)

    grad_projected = row_mask * (
        conv_taps[2] * ahead(0) + conv_taps[1] * ahead(1) + conv_taps[0] * ahead(2)
    )
    intake_bias_grad = jnp.sum(grad_projected, axis=0)
    projected_low = grad_projected.astype(BF)
    intake_grad = dot_tn(projected_low, normed_low).astype(BF).reshape(count, -1, width)
    intake_shard_grad = jnp.concatenate(
        [
            scatter_sum(intake_grad[:, :, :middle], me, count, up, BF),
            scatter_sum(intake_grad[:, :, middle:], me, count, across, BF),
        ],
        axis=1,
    )
    grad_normed = dot_nn(projected_low, intake_t)
    gain_one_grad = jnp.sum(grad_normed * unit_one, axis=0)
    shift_one_grad = jnp.sum(grad_normed, axis=0)
    tokens_grad = (
        grad_residual + normalise_back(unit_one, rstd_one, grad_normed * gain_one)
    ).astype(BF)
    tokens_home = to_home(tokens_grad)

    shaped_grad = kernel_grad * shaping
    column_grad = product(hidden.T, shaped_grad)
    filter_full = lax.dynamic_update_slice_in_dim(
        jnp.zeros((hidden.shape[1], width), F32), column_grad, chan_start, 1
    )
    net_grads = filter_pull(product(shaped_grad, columns.T))

    vector_grads = (
        gain_one_grad,
        shift_one_grad,
        skip_grad,
        mix_bias_grad,
        gain_two_grad,
        shift_two_grad,
        down_bias_grad,
        intake_bias_grad,
        conv_bias_grad,
        taps_grad,
        up_bias_grad,
        filter_full,
    )
    pieces = []
    for g in vector_grads:
        if g.ndim == 1:
            pieces.append(g.reshape(count, -1))
        else:
            pieces.append(
                g.reshape(g.shape[0], count, -1).transpose(1, 0, 2).reshape(count, -1)
            )
    packed = jnp.concatenate(pieces + [jnp.zeros((count, pad), F32)], axis=1)
    summed = scatter_sum(packed.reshape(count, 8, -1), me, count, up, F32).reshape(-1)
    small = []
    at = 0
    for v in vectors:
        small.append(summed[at : at + v.size].reshape(v.shape))
        at += v.size
    net_flat = sum_everywhere(
        jnp.concatenate([g.reshape(-1) for g in net_grads]), me, count
    )
    net_out = []
    at = 0
    for g in net_grads:
        net_out.append(net_flat[at : at + g.size].reshape(g.shape))
        at += g.size
    return (
        output_home,
        tokens_home,
        small[0],
        small[1],
        intake_shard_grad.T,
        small[7],
        small[9],
        small[8],
        small[2],
        small[11],
        mix_shard.T,
        small[3],
        small[4],
        small[5],
        up_shard.T,
        small[10],
        down_shard.T,
        small[6],
    ) + tuple(net_out)

def solution(mesh):
    in_specs = (
        P("dp", "seq", None),
        P("dp", None),
        P("dp", "seq", None),
        P(("dp", "seq")),
        P(("dp", "seq")),
        P(None, ("dp", "seq")),
        P(("dp", "seq")),
        P(None, ("dp", "seq")),
        P(("dp", "seq")),
        P(("dp", "seq")),
        P(None, ("dp", "seq")),
        P(None, ("dp", "seq")),
        P(("dp", "seq")),
        P(("dp", "seq")),
        P(("dp", "seq")),
        P(None, ("dp", "seq")),
        P(("dp", "seq")),
        P(None, ("dp", "seq")),
        P(("dp", "seq")),
        P(),
        P(),
        P(),
        P(),
        P(),
        P(),
        P(),
    )
    out_specs = (
        P("dp", "seq", None),
        P("dp", "seq", None),
        P(("dp", "seq")),
        P(("dp", "seq")),
        P(None, ("dp", "seq")),
        P(("dp", "seq")),
        P(None, ("dp", "seq")),
        P(("dp", "seq")),
        P(("dp", "seq")),
        P(None, ("dp", "seq")),
        P(None, ("dp", "seq")),
        P(("dp", "seq")),
        P(("dp", "seq")),
        P(("dp", "seq")),
        P(None, ("dp", "seq")),
        P(("dp", "seq")),
        P(None, ("dp", "seq")),
        P(("dp", "seq")),
        P(),
        P(),
        P(),
        P(),
        P(),
        P(),
        P(),
    )
    return jax.shard_map(
        per_device, mesh=mesh, in_specs=in_specs, out_specs=out_specs, check_vma=False
    )
```

time: 1390 us -> 1040 us (0.75)
  waiting for transfers between devices: 704 us -> 113 us
  Pallas kernels: 0 us -> 498 us
  matrix products: 336 us -> 138 us
  blocking collectives: 122 us -> 0 us
  other arithmetic: 70 us -> 125 us
  starting transfers between devices: 41.8 us -> 72.3 us
  between operations: 19.5 us -> 4.76 us
    reduce_scatter x4 -> x0, waiting for transfers between devices: 513 us -> none  [the longest x1 142 us: per_device(): lax.psum_scatter(trailing_sums[4], ('dp', 'seq'), scatter_dimension=1, ti...]
    pallas_call x0 -> x9, Pallas kernels: none -> 498 us  [the longest x6 449 us: place_shards(): pl.pallas_call(kernel, in_specs=[SM, hbm, hbm], out_specs=hbm, out_shape=...]
    dot_general x84 -> x12, matrix products: 303 us -> 96.4 us  [the longest x4 41.8 us: dot_nn(): lax.dot_general(left, right, (((1,), (0,)), ((), ())), preferred_element_...]
    unnamed x12 -> x0, waiting for transfers between devices: 170 us -> none
    ppermute x4 -> x75, waiting for transfers between devices: 0.68 us -> 113 us  [the longest x69 113 us: swap_bit(): return lax.ppermute(value, AXES, [(i, i ^ 1 << bit) for i in range(count)])]
    all_gather x2 -> x0, blocking collectives: 84.3 us -> none  [the longest x1 44.2 us: per_device(): lax.all_gather(filter_final_coefficients, ('dp', 'seq'), axis=1, tiled=True)]
    ppermute x4 -> x75, starting transfers between devices: 7.15 us -> 72.3 us  [the longest x69 71.5 us: swap_bit(): return lax.ppermute(value, AXES, [(i, i ^ 1 << bit) for i in range(count)])]
    unnamed x1 -> x0, blocking collectives: 38 us -> none
  transfers between devices with their start and end apart: 22 -> 75, of which waited for: 13 -> 36; matrix products, arithmetic and copies ran while one was open for 23% -> 26% of each run, Pallas kernels for 0% -> 43%
where the time goes in v1:
time: 1040 us
  Pallas kernels  498 us (48%)
  matrix products  138 us (13%)
  other arithmetic  125 us (12%)
  waiting for transfers between devices  113 us (11%)
  local copies, waits for them, and re-layouts  85.6 us (8%)
  starting transfers between devices  72.3 us (7%)
    pallas_call x6, Pallas kernels, place_shards(): pl.pallas_call(kernel, in_specs=[SM, hbm, hbm], out_specs=hbm, out_shape=...  449 us
    ppermute x69, waiting for transfers between devices, swap_bit(): return lax.ppermute(value, AXES, [(i, i ^ 1 << bit) for i in range(count)])  113 us
    ppermute x69, starting transfers between devices, swap_bit(): return lax.ppermute(value, AXES, [(i, i ^ 1 << bit) for i in range(count)])  71.5 us
    dot_general x4, matrix products, dot_nn(): lax.dot_general(left, right, (((1,), (0,)), ((), ())), preferred_element_...  41.8 us
    dot_general x11, matrix products, product(): jnp.dot(left, right, precision=lax.Precision.HIGHEST, preferred_element_t...  41.3 us
    reduce_sum x2, other arithmetic, per_device(): jnp.sum(grad_conv * shifted(k), axis=0)  40.9 us
    dot_general x4, matrix products, dot_nt(): lax.dot_general(left, right, (((1,), (1,)), ((), ())), preferred_element_...  27.7 us
    dot_general x4, matrix products, dot_tn(): lax.dot_general(left, right, (((0,), (0,)), ((), ())), preferred_element_...  26.9 us
  transfers between devices with their start and end apart: 75, of which 36 were waited for; matrix products, arithmetic and copies ran while one was open for 26% of the time, Pallas kernels for 43%

profile of v1, /device:TPU:0, one launch (start us, length us, event | category | flops | bytes accessed | tf_op | source)
XLA Modules:
  0.0 1035.2 jit_solution(11627031078134355174)
XLA Ops:
  2.5 6.8 concatenate.170
  9.3 4.1 collective-permute-start.1
  49.9 13.3 %shard_map.477 = f32[32,8,384]{2,1,0:T(8,128)} custom-call(s32[1]{0:T(128)} %bitcast.4.me_ref, f32[16,8,384]{2,1,0:T(8,128)} %bitcast.378, f32[16,8,384]{2,1,0:T(8,128)} %bitcast.380), custom_call_target="tpu_custom_call" | custom-call | tf_op jit(solution)/shard_map/pallas_call | solution.py:247
  67.1 8.1 fusion.40
  83.4 5.6 collective-permute-done.9
  94.0 9.3 shard_map.480.k_ref
  104.3 55.0 %shard_map.478 = bf16[32,72,384]{2,1,0:T(8,128)(2,1)} custom-call(s32[1]{0:T(128)} %bitcast.4.me_ref, bf16[16,72,384]{2,1,0:T(8,128)(2,1)} %bitcast.362, bf16[16,72,384]{2,1,0:T(8,128)(2,1)} %bitcast.10.other_ref), custom_call_target="tpu_custom_call" | custom-call | tf_op jit(solution)/shard_map/pallas_call | solution.py:247
  159.3 55.0 %shard_map.479 = bf16[32,72,384]{2,1,0:T(8,128)(2,1)} custom-call(s32[1]{0:T(128)} %bitcast.4.me_ref, bf16[16,72,384]{2,1,0:T(8,128)(2,1)} %bitcast.12.near_ref, bf16[16,72,384]{2,1,0:T(8,128)(2,1)} %bitcast.13.other_ref), custom_call_target="tpu_custom_call" | custom-call | tf_op jit(solution)/shard_map/pallas_call | solution.py:247
  221.3 4.2 add_multiply_fusion
  226.3 8.2 collective-permute-done.19
  234.6 4.5 fusion.7
  239.1 8.7 fusion.13
  258.1 3.3 collective-permute-done.25
  262.9 4.2 collective-permute-done.30
  270.9 10.9 %collective-permute-done.31 = bf16[96,3072]{1,0:T(8,128)(2,1)S(1)} collective-permute-done((bf16[96,3072]{1,0:T(8,128)(2,1)S(1)}, bf16[96,3072]{1,0:T(8,128)(2,1)S(1)}, u32[]{:S(2)}, u32[]{:S(2)}) %collective-permute-start.31) | collective-permute-done | bytes 589856 | tf_op jit(solution)/shard_map/ppermute | solution.py:208
  285.1 17.0 %shard_map.481 = (bf16[4,2,512,384]{3,2,1,0:T(8,128)(2,1)}, f32[8,256,384]{2,1,0:T(8,128)}) custom-call(f32[4,16]{1,0:T(4,128)S(1)} %copy-done.1, bf16[8,256,384]{2,1,0:T(8,128)(2,1)S(1)} %bitcast.279, f32[4,2,512,384]{3,2,1,0:T(8,128)} %shard_map.480.k_ref, bf16[4,2,512,512]{3,2,1,0:T(8,128)(2,1)} %constant.289.clone.f_ref, ...), custom_call_target="tpu_custom_call" | custom-call | tf_op jit(solution)/shard_map/pallas_call | solution.py:146
  316.9 37.1 %shard_map.482 = bf16[32,24,768]{2,1,0:T(8,128)(2,1)} custom-call(s32[1]{0:T(128)} %bitcast.4.me_ref, bf16[16,24,768]{2,1,0:T(8,128)(2,1)} %bitcast.26.near_ref, bf16[16,24,768]{2,1,0:T(8,128)(2,1)} %bitcast.27.other_ref), custom_call_target="tpu_custom_call" | custom-call | tf_op jit(solution)/shard_map/pallas_call | solution.py:247
  355.5 4.9 multiply_convert_fusion.2
  364.3 144.3 %shard_map.484 = bf16[32,24,3072]{2,1,0:T(8,128)(2,1)} custom-call(s32[1]{0:T(128)} %bitcast.4.me_ref, bf16[16,24,3072]{2,1,0:T(8,128)(2,1)} %bitcast.32.near_ref, bf16[16,24,3072]{2,1,0:T(8,128)(2,1)} %bitcast.33.other_ref), custom_call_target="tpu_custom_call" | custom-call | tf_op jit(solution)/shard_map/pallas_call | solution.py:247
  508.6 144.3 %shard_map.483 = bf16[32,96,768]{2,1,0:T(8,128)(2,1)} custom-call(s32[1]{0:T(128)} %bitcast.4.me_ref, bf16[16,96,768]{2,1,0:T(8,128)(2,1)} %bitcast.29.near_ref, bf16[16,96,768]{2,1,0:T(8,128)(2,1)} %bitcast.30.other_ref), custom_call_target="tpu_custom_call" | custom-call | tf_op jit(solution)/shard_map/pallas_call | solution.py:247
  653.0 10.8 %fusion.90 = f32[1024,3072]{1,0:T(8,128)} fusion(bf16[3072,768]{1,0:T(8,128)(2,1)} %bitcast.310, f32[1024,768]{1,0:T(8,128)S(1)} %copy-done.18, f32[768]{0:T(1024)S(1)} %add.535, f32[768]{0:T(1024)S(1)} %mul.454, f32[1024]{0:T(1024)S(1)} %add_rsqrt_fusion, f32[1024]{0:T(1024)S(1)} %broadcast_multiply_fusion.4), kind=kOutput, calls=%fused_computation.332 | convolution fusion | flops 4835770368 | bytes 20461568 | tf_op jit(solution)/shard_map/dot_general | solution.py:305
  663.9 17.9 %fusion.104 = (f32[3072]{0:T(1024)S(1)}, bf16[1024,3072]{1,0:T(8,128)(2,1)}) fusion(f32[1024,3072]{1,0:T(8,128)} %fusion.90, f32[3072]{0:T(1024)S(1)} %add.538, bf16[768,3072]{1,0:T(8,128)(2,1)S(1)} %bitcast.308, f32[1024]{0:T(1024)S(1)} %and_convert_fusion.1, bf16[512,768]{1,0:T(8,128)(2,1)} %collective-permute-done.35, bf16[512,768]{1,0:T(8,128)(2,1)S(1)} %copy-done.43), kind=kOutput, calls=%fused_computation.345 | convolution fusion | flops 4905759744 | bytes 25194496 | tf_op jit(solution)/shard_map/dot_general | solution.py:309
  681.8 8.6 multiply_reduce_fusion.4
  690.4 7.7 convolution_convert_fusion.1
  698.1 3.0 fusion.93
  704.9 5.5 fusion.33
  710.5 11.1 %multiply_convert_fusion.1 = bf16[1024,768]{1,0:T(8,128)(2,1)S(1)} fusion(f32[1024,768]{1,0:T(8,128)S(1)} %copy-done.19, bf16[768,3072]{1,0:T(8,128)(2,1)S(1)} %bitcast.309, f32[768]{0:T(1024)S(1)} %add.544, f32[1024]{0:T(1024)S(1)} %and_convert_fusion.1, f32[1024,3072]{1,0:T(8,128)} %fusion.90, f32[3072]{0:T(1024)S(1)} %add.538), kind=kOutput, calls=%fused_computation.77 | convolution fusion | flops 4866441216 | bytes 22039552 | tf_op jit(solution)/shard_map/dot_general | solution.py:305
  731.4 9.8 convolution_convert_fusion
  749.6 22.1 %shard_map.485 = (f32[8,256,384]{2,1,0:T(8,128)}, f32[8,256,384]{2,1,0:T(8,128)}) custom-call(f32[4,16]{1,0:T(4,128)S(1)} %copy-done.1, bf16[8,256,384]{2,1,0:T(8,128)(2,1)S(1)} %bitcast.278, f32[4,2,512,384]{3,2,1,0:T(8,128)} %shard_map.480.k_ref, bf16[4,2,512,384]{3,2,1,0:T(8,128)(2,1)} %get-tuple-element.38.s_ref, ...), custom_call_target="tpu_custom_call" | custom-call | tf_op jit(solution)/shard_map/pallas_call | solution.py:156
  774.4 4.8 convolution_multiply_fusion.2
  783.9 3.7 multiply_reduce_fusion.11
  791.5 3.2 fusion.59
  795.0 8.4 convolution_dynamic-update-slice_fusion
  839.5 5.1 slice_multiply_fusion.1
  844.6 7.2 pad_maximum_fusion.2
  854.4 25.4 %multiply_reduce_fusion.2 = (f32[2304]{0:T(1024)S(1)}, f32[2304]{0:T(1024)}, f32[2304]{0:T(1024)}, f32[2,512,2304]{2,1,0:T(8,128)}, f32[2,512,2304]{2,1,0:T(8,128)}) fusion(f32[2,512,2304]{2,1,0:T(8,128)} %copy-done.4, f32[2,512,768]{2,1,0:T(8,128)} %bitcast.284, f32[2,512,768]{2,1,0:T(8,128)} %bitcast.283, f32[2,512,768]{2,1,0:T(8,128)S(1)} %bitcast.282, ...), kind=kLoop, calls=%fused_computation.32 | loop fusion | flops 35382528 | bytes 56719360 | tf_op jit(solution)/shard_map/reduce_sum | solution.py:577
  879.9 15.5 %multiply_reduce_fusion = (f32[2304]{0:T(1024)S(1)}, f32[2304]{0:T(1024)}, bf16[1024,2304]{1,0:T(8,128)(2,1)}) fusion(f32[1024,2304]{1,0:T(8,128)} %copy-done.3, f32[1024,768]{1,0:T(8,128)} %get-tuple-element.170, f32[1024,768]{1,0:T(8,128)} %get-tuple-element.169, f32[1024,768]{1,0:T(8,128)S(1)} %get-tuple-element.174, ...), kind=kLoop, calls=%fused_computation.30 | loop fusion | flops 28306944 | bytes 42517504 | tf_op jit(solution)/shard_map/reduce_sum | solution.py:577
  895.7 9.8 fusion.30
  907.2 6.8 convolution_convert_fusion.2
  916.9 3.9 collective-permute-done.41
  930.5 3.0 collective-permute-done.44
  940.0 3.3 fusion.15
  952.0 2.8 maximum_select_fusion.1
  954.8 26.5 %collective-permute-done.46 = bf16[8,72,384]{2,1,0:T(8,128)(2,1)S(1)} collective-permute-done((bf16[8,72,384]{2,1,0:T(8,128)(2,1)S(1)}, bf16[8,72,384]{2,1,0:T(8,128)(2,1)S(1)}, u32[]{:S(2)}, u32[]{:S(2)}) %collective-permute-start.46) | collective-permute-done | bytes 442400 | tf_op jit(solution)/shard_map/ppermute | solution.py:208
  1005.0 6.5 collective-permute-done.67
  1016.1 5.1 collective-permute-done.68
  1024.5 3.9 collective-permute-start.64
  1028.3 4.3 collective-permute-done.69
  (622 shorter events, 235.8 us)
Async XLA Ops:
  9.3 22.4 %collective-permute-start.1 = (f32[8,384]{1,0:T(8,128)S(1)}, f32[8,384]{1,0:T(8,128)S(1)}, u32[]{:S(2)}, u32[]{:S(2)}) collective-permute-start(f32[8,384]{1,0:T(8,128)S(1)} %reshape.655), channel_id=1, source_target_pairs={{0,16},{1,17},{2,18},{3,19},{4,20},{5,21},{6,22},{7,23},{8,24},{9,... | collective-permute-start | bytes 36872 | tf_op jit(solution)/shard_map/ppermute | solution.py:208
  15.8 87.5 %collective-permute-start = (bf16[512,768]{1,0:T(8,128)(2,1)}, bf16[512,768]{1,0:T(8,128)(2,1)S(1)}, u32[]{:S(2)}, u32[]{:S(2)}) collective-permute-start(bf16[512,768]{1,0:T(8,128)(2,1)} %get-tuple-element.201), channel_id=1, source_target_pairs={{0,2},{1,3},{2,0},{3,1},{4,6},{5,7},{6,4},{7,5},{8,10},{9,11},{10,... | collective-permute-start | bytes 2359304 | tf_op jit(solution)/shard_map/ppermute | solution.py:208
  17.9 19.8 %collective-permute-start.6 = (bf16[72,384]{1,0:T(8,128)(2,1)S(1)}, bf16[72,384]{1,0:T(8,128)(2,1)S(1)}, u32[]{:S(2)}, u32[]{:S(2)}) collective-permute-start(bf16[72,384]{1,0:T(8,128)(2,1)S(1)} %get-tuple-element.219), channel_id=1, source_target_pairs={{0,16},{1,17},{2,18},{3,19},{4,20},{5,21},{6,22},{7,23},{8,24},{9,... | collective-permute-start | bytes 165896 | tf_op jit(solution)/shard_map/ppermute | solution.py:208
  18.3 21.1 %collective-permute-start.11 = (bf16[72,384]{1,0:T(8,128)(2,1)S(1)}, bf16[72,384]{1,0:T(8,128)(2,1)S(1)}, u32[]{:S(2)}, u32[]{:S(2)}) collective-permute-start(bf16[72,384]{1,0:T(8,128)(2,1)S(1)} %get-tuple-element.222), channel_id=1, source_target_pairs={{0,16},{1,17},{2,18},{3,19},{4,20},{5,21},{6,22},{7,23},{8,24},{9,... | collective-permute-start | bytes 165896 | tf_op jit(solution)/shard_map/ppermute | solution.py:208
  43.3 32.2 %collective-permute-start.8 = (bf16[288,384]{1,0:T(8,128)(2,1)}, bf16[288,384]{1,0:T(8,128)(2,1)}, u32[]{:S(2)}, u32[]{:S(2)}) collective-permute-start(bf16[288,384]{1,0:T(8,128)(2,1)} %pad_maximum_fusion.24), channel_id=1, source_target_pairs={{0,4},{1,5},{2,6},{3,7},{4,0},{5,1},{6,2},{7,3},{8,12},{9,13},{10,... | collective-permute-start | bytes 663560 | tf_op jit(solution)/shard_map/ppermute | solution.py:208
  44.9 32.2 %collective-permute-start.13 = (bf16[288,384]{1,0:T(8,128)(2,1)}, bf16[288,384]{1,0:T(8,128)(2,1)}, u32[]{:S(2)}, u32[]{:S(2)}) collective-permute-start(bf16[288,384]{1,0:T(8,128)(2,1)} %pad_maximum_fusion.25), channel_id=1, source_target_pairs={{0,2},{1,3},{2,0},{3,1},{4,6},{5,7},{6,4},{7,5},{8,10},{9,11},{10,... | collective-permute-start | bytes 663560 | tf_op jit(solution)/shard_map/ppermute | solution.py:208
  76.5 12.4 %collective-permute-start.9 = (bf16[576,384]{1,0:T(8,128)(2,1)S(1)}, bf16[576,384]{1,0:T(8,128)(2,1)}, u32[]{:S(2)}, u32[]{:S(2)}) collective-permute-start(bf16[576,384]{1,0:T(8,128)(2,1)S(1)} %pad_maximum_fusion.19), channel_id=1, source_target_pairs={{0,2},{1,3},{2,0},{3,1},{4,6},{5,7},{6,4},{7,5},{8,10},{9,11},{10,... | collective-permute-start | bytes 1327112 | tf_op jit(solution)/shard_map/ppermute | solution.py:208
  79.0 12.3 %collective-permute-start.14 = (bf16[576,384]{1,0:T(8,128)(2,1)}, bf16[576,384]{1,0:T(8,128)(2,1)}, u32[]{:S(2)}, u32[]{:S(2)}) collective-permute-start(bf16[576,384]{1,0:T(8,128)(2,1)} %pad_maximum_fusion.20), channel_id=1, source_target_pairs={{0,4},{1,5},{2,6},{3,7},{4,0},{5,1},{6,2},{7,3},{8,12},{9,13},{10,... | collective-permute-start | bytes 1327112 | tf_op jit(solution)/shard_map/ppermute | solution.py:208
  90.1 14.2 %collective-permute-start.10 = (bf16[1152,384]{1,0:T(8,128)(2,1)S(1)}, bf16[1152,384]{1,0:T(8,128)(2,1)}, u32[]{:S(2)}, u32[]{:S(2)}) collective-permute-start(bf16[1152,384]{1,0:T(8,128)(2,1)S(1)} %constant_dynamic-update-slice_fusion.5), channel_id=1, source_target_pairs={{0,1},{1,0},{2,3},{3,2},{4,5},{5,4},{6,7},{7,6},{8,9},{9,8},{10,11... | collective-permute-start | bytes 2654216 | tf_op jit(solution)/shard_map/ppermute | solution.py:208
  93.1 66.2 %collective-permute-start.15 = (bf16[1152,384]{1,0:T(8,128)(2,1)}, bf16[1152,384]{1,0:T(8,128)(2,1)}, u32[]{:S(2)}, u32[]{:S(2)}) collective-permute-start(bf16[1152,384]{1,0:T(8,128)(2,1)} %constant_dynamic-update-slice_fusion.10), channel_id=1, source_target_pairs={{0,1},{1,0},{2,3},{3,2},{4,5},{5,4},{6,7},{7,6},{8,9},{9,8},{10,11... | collective-permute-start | bytes 2654216 | tf_op jit(solution)/shard_map/ppermute | solution.py:208
  216.2 35.3 %collective-permute-start.24 = (bf16[96,768]{1,0:T(8,128)(2,1)S(1)}, bf16[96,768]{1,0:T(8,128)(2,1)S(1)}, u32[]{:S(2)}, u32[]{:S(2)}) collective-permute-start(bf16[96,768]{1,0:T(8,128)(2,1)S(1)} %bitcast.331), channel_id=1, source_target_pairs={{0,16},{1,17},{2,18},{3,19},{4,20},{5,21},{6,22},{7,23},{8,24},{9,... | collective-permute-start | bytes 442376 | tf_op jit(solution)/shard_map/ppermute | solution.py:208
  217.7 35.9 %collective-permute-start.29 = (bf16[24,3072]{1,0:T(8,128)(2,1)S(1)}, bf16[24,3072]{1,0:T(8,128)(2,1)S(1)}, u32[]{:S(2)}, u32[]{:S(2)}) collective-permute-start(bf16[24,3072]{1,0:T(8,128)(2,1)S(1)} %bitcast.326), channel_id=1, source_target_pairs={{0,16},{1,17},{2,18},{3,19},{4,20},{5,21},{6,22},{7,23},{8,24},{9,... | collective-permute-start | bytes 442376 | tf_op jit(solution)/shard_map/ppermute | solution.py:208
  220.5 14.0 %collective-permute-start.19 = (bf16[24,768]{1,0:T(8,128)(2,1)S(1)}, bf16[24,768]{1,0:T(8,128)(2,1)S(1)}, u32[]{:S(2)}, u32[]{:S(2)}) collective-permute-start(bf16[24,768]{1,0:T(8,128)(2,1)S(1)} %bitcast.369), channel_id=1, source_target_pairs={{0,16},{1,17},{2,18},{3,19},{4,20},{5,21},{6,22},{7,23},{8,24},{9,... | collective-permute-start | bytes 110600 | tf_op jit(solution)/shard_map/ppermute | solution.py:208
  234.5 15.0 %collective-permute-start.20 = (bf16[48,768]{1,0:T(8,128)(2,1)S(1)}, bf16[48,768]{1,0:T(8,128)(2,1)S(1)}, u32[]{:S(2)}, u32[]{:S(2)}) collective-permute-start(bf16[48,768]{1,0:T(8,128)(2,1)S(1)} %pad_maximum_fusion.30), channel_id=1, source_target_pairs={{0,8},{1,9},{2,10},{3,11},{4,12},{5,13},{6,14},{7,15},{8,0},{9,1},... | collective-permute-start | bytes 221192 | tf_op jit(solution)/shard_map/ppermute | solution.py:208
  248.3 22.1 %collective-permute-start.17 = (bf16[1024,384]{1,0:T(8,128)(2,1)S(1)}, bf16[1024,384]{1,0:T(8,128)(2,1)S(1)}, u32[]{:S(2)}, u32[]{:S(2)}) collective-permute-start(bf16[1024,384]{1,0:T(8,128)(2,1)S(1)} %constant_dynamic-slice_fusion.8), channel_id=1, source_target_pairs={{0,1},{1,0},{2,3},{3,2},{4,5},{5,4},{6,7},{7,6},{8,9},{9,8},{10,11... | collective-permute-start | bytes 2359304 | tf_op jit(solution)/shard_map/ppermute | solution.py:501
  251.5 9.9 collective-permute-start.25
  253.6 13.4 %collective-permute-start.30 = (bf16[48,3072]{1,0:T(8,128)(2,1)S(1)}, bf16[48,3072]{1,0:T(8,128)(2,1)S(1)}, u32[]{:S(2)}, u32[]{:S(2)}) collective-permute-start(bf16[48,3072]{1,0:T(8,128)(2,1)S(1)} %pad_maximum_fusion.23), channel_id=1, source_target_pairs={{0,8},{1,9},{2,10},{3,11},{4,12},{5,13},{6,14},{7,15},{8,0},{9,1},... | collective-permute-start | bytes 884744 | tf_op jit(solution)/shard_map/ppermute | solution.py:208
  255.9 13.8 %collective-permute-start.22 = (bf16[192,768]{1,0:T(8,128)(2,1)S(1)}, bf16[192,768]{1,0:T(8,128)(2,1)S(1)}, u32[]{:S(2)}, u32[]{:S(2)}) collective-permute-start(bf16[192,768]{1,0:T(8,128)(2,1)S(1)} %pad_maximum_fusion.21), channel_id=1, source_target_pairs={{0,2},{1,3},{2,0},{3,1},{4,6},{5,7},{6,4},{7,5},{8,10},{9,11},{10,... | collective-permute-start | bytes 884744 | tf_op jit(solution)/shard_map/ppermute | solution.py:208
  261.4 22.2 %collective-permute-start.26 = (bf16[384,768]{1,0:T(8,128)(2,1)S(1)}, bf16[384,768]{1,0:T(8,128)(2,1)S(1)}, u32[]{:S(2)}, u32[]{:S(2)}) collective-permute-start(bf16[384,768]{1,0:T(8,128)(2,1)S(1)} %pad_maximum_fusion.17), channel_id=1, source_target_pairs={{0,2},{1,3},{2,0},{3,1},{4,6},{5,7},{6,4},{7,5},{8,10},{9,11},{10,... | collective-permute-start | bytes 1769480 | tf_op jit(solution)/shard_map/ppermute | solution.py:208
  267.1 14.7 %collective-permute-start.31 = (bf16[96,3072]{1,0:T(8,128)(2,1)S(1)}, bf16[96,3072]{1,0:T(8,128)(2,1)S(1)}, u32[]{:S(2)}, u32[]{:S(2)}) collective-permute-start(bf16[96,3072]{1,0:T(8,128)(2,1)S(1)} %pad_maximum_fusion.18), channel_id=1, source_target_pairs={{0,4},{1,5},{2,6},{3,7},{4,0},{5,1},{6,2},{7,3},{8,12},{9,13},{10,... | collective-permute-start | bytes 1769480 | tf_op jit(solution)/shard_map/ppermute | solution.py:208
  270.5 46.4 %collective-permute-start.23 = (bf16[384,768]{1,0:T(8,128)(2,1)}, bf16[384,768]{1,0:T(8,128)(2,1)}, u32[]{:S(2)}, u32[]{:S(2)}) collective-permute-start(bf16[384,768]{1,0:T(8,128)(2,1)} %constant_dynamic-update-slice_fusion.15), channel_id=1, source_target_pairs={{0,1},{1,0},{2,3},{3,2},{4,5},{5,4},{6,7},{7,6},{8,9},{9,8},{10,11... | collective-permute-start | bytes 1769480 | tf_op jit(solution)/shard_map/ppermute | solution.py:208
  281.9 26.5 %collective-permute-start.32 = (bf16[192,3072]{1,0:T(8,128)(2,1)S(1)}, bf16[192,3072]{1,0:T(8,128)(2,1)S(1)}, u32[]{:S(2)}, u32[]{:S(2)}) collective-permute-start(bf16[192,3072]{1,0:T(8,128)(2,1)S(1)} %pad_maximum_fusion.12), channel_id=1, source_target_pairs={{0,2},{1,3},{2,0},{3,1},{4,6},{5,7},{6,4},{7,5},{8,10},{9,11},{10,... | collective-permute-start | bytes 3538952 | tf_op jit(solution)/shard_map/ppermute | solution.py:208
  283.7 26.4 %collective-permute-start.27 = (bf16[768,768]{1,0:T(8,128)(2,1)S(1)}, bf16[768,768]{1,0:T(8,128)(2,1)}, u32[]{:S(2)}, u32[]{:S(2)}) collective-permute-start(bf16[768,768]{1,0:T(8,128)(2,1)S(1)} %pad_maximum_fusion.11), channel_id=1, source_target_pairs={{0,4},{1,5},{2,6},{3,7},{4,0},{5,1},{6,2},{7,3},{8,12},{9,13},{10,... | collective-permute-start | bytes 3538952 | tf_op jit(solution)/shard_map/ppermute | solution.py:208
  305.4 48.6 %collective-permute-start.18 = (bf16[1024,384]{1,0:T(8,128)(2,1)}, bf16[1024,384]{1,0:T(8,128)(2,1)}, u32[]{:S(2)}, u32[]{:S(2)}) collective-permute-start(bf16[1024,384]{1,0:T(8,128)(2,1)} %pad_maximum_fusion.14), channel_id=1, source_target_pairs={{0,1},{1,0},{2,3},{3,2},{4,5},{5,4},{6,7},{7,6},{8,9},{9,8},{10,11... | collective-permute-start | bytes 2359304 | tf_op jit(solution)/shard_map/ppermute | solution.py:501
  309.6 54.7 %collective-permute-start.33 = (bf16[384,3072]{1,0:T(8,128)(2,1)}, bf16[384,3072]{1,0:T(8,128)(2,1)}, u32[]{:S(2)}, u32[]{:S(2)}) collective-permute-start(bf16[384,3072]{1,0:T(8,128)(2,1)} %constant_dynamic-update-slice_fusion.25), channel_id=1, source_target_pairs={{0,1},{1,0},{2,3},{3,2},{4,5},{5,4},{6,7},{7,6},{8,9},{9,8},{10,11... | collective-permute-start | bytes 7077896 | tf_op jit(solution)/shard_map/ppermute | solution.py:208
  312.5 196.1 %collective-permute-start.28 = (bf16[1536,768]{1,0:T(8,128)(2,1)}, bf16[1536,768]{1,0:T(8,128)(2,1)}, u32[]{:S(2)}, u32[]{:S(2)}) collective-permute-start(bf16[1536,768]{1,0:T(8,128)(2,1)} %constant_dynamic-update-slice_fusion.20), channel_id=1, source_target_pairs={{0,1},{1,0},{2,3},{3,2},{4,5},{5,4},{6,7},{7,6},{8,9},{9,8},{10,11... | collective-permute-start | bytes 7077896 | tf_op jit(solution)/shard_map/ppermute | solution.py:208
  313.9 350.0 %collective-permute-start.35 = (bf16[512,768]{1,0:T(8,128)(2,1)}, bf16[512,768]{1,0:T(8,128)(2,1)}, u32[]{:S(2)}, u32[]{:S(2)}) collective-permute-start(bf16[512,768]{1,0:T(8,128)(2,1)} %get-tuple-element.191), channel_id=1, source_target_pairs={{0,2},{1,3},{2,0},{3,1},{4,6},{5,7},{6,4},{7,5},{8,10},{9,11},{10,... | collective-permute-start | bytes 2359304 | tf_op jit(solution)/shard_map/ppermute | solution.py:208
  722.8 85.9 %collective-permute-start.34 = (bf16[512,768]{1,0:T(8,128)(2,1)}, bf16[512,768]{1,0:T(8,128)(2,1)}, u32[]{:S(2)}, u32[]{:S(2)}) collective-permute-start(bf16[512,768]{1,0:T(8,128)(2,1)} %get-tuple-element.193), channel_id=1, source_target_pairs={{0,2},{1,3},{2,0},{3,1},{4,6},{5,7},{6,4},{7,5},{8,10},{9,11},{10,... | collective-permute-start | bytes 2359304 | tf_op jit(solution)/shard_map/ppermute | solution.py:208
  727.9 17.2 %collective-permute-start.55 = (bf16[16,24,768]{2,1,0:T(8,128)(2,1)}, bf16[16,24,768]{2,1,0:T(8,128)(2,1)}, u32[]{:S(2)}, u32[]{:S(2)}) collective-permute-start(bf16[16,24,768]{2,1,0:T(8,128)(2,1)} %dynamic-slice_bitcast_fusion.12), channel_id=1, source_target_pairs={{0,1},{1,0},{2,3},{3,2},{4,5},{5,4},{6,7},{7,6},{8,9},{9,8},{10,11... | collective-permute-start | bytes 1769480 | tf_op jit(solution)/shard_map/ppermute | solution.py:208
  730.8 18.0 %collective-permute-start.36 = (bf16[1024,384]{1,0:T(8,128)(2,1)S(1)}, bf16[1024,384]{1,0:T(8,128)(2,1)S(1)}, u32[]{:S(2)}, u32[]{:S(2)}) collective-permute-start(bf16[1024,384]{1,0:T(8,128)(2,1)S(1)} %constant_dynamic-slice_fusion.7), channel_id=1, source_target_pairs={{0,1},{1,0},{2,3},{3,2},{4,5},{5,4},{6,7},{7,6},{8,9},{9,8},{10,11... | collective-permute-start | bytes 2359304 | tf_op jit(solution)/shard_map/ppermute | solution.py:501
  743.0 197.0 %collective-permute-start.65 = (bf16[16,24,3072]{2,1,0:T(8,128)(2,1)}, bf16[16,24,3072]{2,1,0:T(8,128)(2,1)}, u32[]{:S(2)}, u32[]{:S(2)}) collective-permute-start(bf16[16,24,3072]{2,1,0:T(8,128)(2,1)} %dynamic-slice_bitcast_fusion), channel_id=1, source_target_pairs={{0,1},{1,0},{2,3},{3,2},{4,5},{5,4},{6,7},{7,6},{8,9},{9,8},{10,11... | collective-permute-start | bytes 7077896 | tf_op jit(solution)/shard_map/ppermute | solution.py:208
  744.8 199.0 %collective-permute-start.60 = (bf16[16,96,768]{2,1,0:T(8,128)(2,1)}, bf16[16,96,768]{2,1,0:T(8,128)(2,1)}, u32[]{:S(2)}, u32[]{:S(2)}) collective-permute-start(bf16[16,96,768]{2,1,0:T(8,128)(2,1)} %dynamic-slice_bitcast_fusion.1), channel_id=1, source_target_pairs={{0,1},{1,0},{2,3},{3,2},{4,5},{5,4},{6,7},{7,6},{8,9},{9,8},{10,11... | collective-permute-start | bytes 7077896 | tf_op jit(solution)/shard_map/ppermute | solution.py:208
  747.1 71.2 %collective-permute-start.56 = (bf16[8,24,768]{2,1,0:T(8,128)(2,1)}, bf16[8,24,768]{2,1,0:T(8,128)(2,1)}, u32[]{:S(2)}, u32[]{:S(2)}) collective-permute-start(bf16[8,24,768]{2,1,0:T(8,128)(2,1)} %dynamic-slice_bitcast_fusion.17), channel_id=1, source_target_pairs={{0,2},{1,3},{2,0},{3,1},{4,6},{5,7},{6,4},{7,5},{8,10},{9,11},{10,... | collective-permute-start | bytes 884744 | tf_op jit(solution)/shard_map/ppermute | solution.py:208
  794.9 9.8 collective-permute-start.70
  808.8 29.1 %collective-permute-start.37 = (bf16[1024,384]{1,0:T(8,128)(2,1)}, bf16[1024,384]{1,0:T(8,128)(2,1)}, u32[]{:S(2)}, u32[]{:S(2)}) collective-permute-start(bf16[1024,384]{1,0:T(8,128)(2,1)} %pad_maximum_fusion.16), channel_id=1, source_target_pairs={{0,1},{1,0},{2,3},{3,2},{4,5},{5,4},{6,7},{7,6},{8,9},{9,8},{10,11... | collective-permute-start | bytes 2359304 | tf_op jit(solution)/shard_map/ppermute | solution.py:501
  835.4 17.5 %collective-permute-start.59 = (bf16[1,24,768]{2,1,0:T(8,128)(2,1)S(1)}, bf16[1,24,768]{2,1,0:T(8,128)(2,1)}, u32[]{:S(2)}, u32[]{:S(2)}) collective-permute-start(bf16[1,24,768]{2,1,0:T(8,128)(2,1)S(1)} %constant_dynamic-slice_fusion.2), channel_id=1, source_target_pairs={{0,16},{1,17},{2,18},{3,19},{4,20},{5,21},{6,22},{7,23},{8,24},{9,... | collective-permute-start | bytes 110600 | tf_op jit(solution)/shard_map/ppermute | solution.py:208
  922.9 29.0 %collective-permute-start.39 = (bf16[512,768]{1,0:T(8,128)(2,1)}, bf16[512,768]{1,0:T(8,128)(2,1)}, u32[]{:S(2)}, u32[]{:S(2)}) collective-permute-start(bf16[512,768]{1,0:T(8,128)(2,1)} %get-tuple-element.183), channel_id=1, source_target_pairs={{0,2},{1,3},{2,0},{3,1},{4,6},{5,7},{6,4},{7,5},{8,10},{9,11},{10,... | collective-permute-start | bytes 2359304 | tf_op jit(solution)/shard_map/ppermute | solution.py:208
  930.5 16.9 %collective-permute-start.45 = (bf16[16,72,384]{2,1,0:T(8,128)(2,1)}, bf16[16,72,384]{2,1,0:T(8,128)(2,1)}, u32[]{:S(2)}, u32[]{:S(2)}) collective-permute-start(bf16[16,72,384]{2,1,0:T(8,128)(2,1)} %dynamic-slice_bitcast_fusion.5), channel_id=1, source_target_pairs={{0,1},{1,0},{2,3},{3,2},{4,5},{5,4},{6,7},{7,6},{8,9},{9,8},{10,11... | collective-permute-start | bytes 2654216 | tf_op jit(solution)/shard_map/ppermute | solution.py:208
  933.6 17.0 %collective-permute-start.50 = (bf16[16,72,384]{2,1,0:T(8,128)(2,1)}, bf16[16,72,384]{2,1,0:T(8,128)(2,1)S(1)}, u32[]{:S(2)}, u32[]{:S(2)}) collective-permute-start(bf16[16,72,384]{2,1,0:T(8,128)(2,1)} %dynamic-slice_bitcast_fusion.4), channel_id=1, source_target_pairs={{0,1},{1,0},{2,3},{3,2},{4,5},{5,4},{6,7},{7,6},{8,9},{9,8},{10,11... | collective-permute-start | bytes 2654216 | tf_op jit(solution)/shard_map/ppermute | solution.py:208
  943.4 56.2 %collective-permute-start.66 = (bf16[8,24,3072]{2,1,0:T(8,128)(2,1)S(1)}, bf16[8,24,3072]{2,1,0:T(8,128)(2,1)S(1)}, u32[]{:S(2)}, u32[]{:S(2)}) collective-permute-start(bf16[8,24,3072]{2,1,0:T(8,128)(2,1)S(1)} %dynamic-slice_bitcast_fusion.2), channel_id=1, source_target_pairs={{0,2},{1,3},{2,0},{3,1},{4,6},{5,7},{6,4},{7,5},{8,10},{9,11},{10,... | collective-permute-start | bytes 3538952 | tf_op jit(solution)/shard_map/ppermute | solution.py:208
  946.4 56.6 %collective-permute-start.61 = (bf16[4,192,768]{2,1,0:T(8,128)(2,1)S(1)}, bf16[4,192,768]{2,1,0:T(8,128)(2,1)S(1)}, u32[]{:S(2)}, u32[]{:S(2)}) collective-permute-start(bf16[4,192,768]{2,1,0:T(8,128)(2,1)S(1)} %dynamic-slice_bitcast_fusion.3), channel_id=1, source_target_pairs={{0,4},{1,5},{2,6},{3,7},{4,0},{5,1},{6,2},{7,3},{8,12},{9,13},{10,... | collective-permute-start | bytes 3538952 | tf_op jit(solution)/shard_map/ppermute | solution.py:208
  948.9 32.4 %collective-permute-start.46 = (bf16[8,72,384]{2,1,0:T(8,128)(2,1)S(1)}, bf16[8,72,384]{2,1,0:T(8,128)(2,1)S(1)}, u32[]{:S(2)}, u32[]{:S(2)}) collective-permute-start(bf16[8,72,384]{2,1,0:T(8,128)(2,1)S(1)} %dynamic-slice_bitcast_fusion.14), channel_id=1, source_target_pairs={{0,2},{1,3},{2,0},{3,1},{4,6},{5,7},{6,4},{7,5},{8,10},{9,11},{10,... | collective-permute-start | bytes 1327112 | tf_op jit(solution)/shard_map/ppermute | solution.py:208
  950.9 33.3 %collective-permute-start.51 = (bf16[4,144,384]{2,1,0:T(8,128)(2,1)S(1)}, bf16[4,144,384]{2,1,0:T(8,128)(2,1)S(1)}, u32[]{:S(2)}, u32[]{:S(2)}) collective-permute-start(bf16[4,144,384]{2,1,0:T(8,128)(2,1)S(1)} %dynamic-slice_bitcast_fusion.13), channel_id=1, source_target_pairs={{0,4},{1,5},{2,6},{3,7},{4,0},{5,1},{6,2},{7,3},{8,12},{9,13},{10,... | collective-permute-start | bytes 1327112 | tf_op jit(solution)/shard_map/ppermute | solution.py:208
  1000.1 11.4 %collective-permute-start.67 = (bf16[4,24,3072]{2,1,0:T(8,128)(2,1)S(1)}, bf16[4,24,3072]{2,1,0:T(8,128)(2,1)S(1)}, u32[]{:S(2)}, u32[]{:S(2)}) collective-permute-start(bf16[4,24,3072]{2,1,0:T(8,128)(2,1)S(1)} %dynamic-slice_bitcast_fusion.10), channel_id=1, source_target_pairs={{0,4},{1,5},{2,6},{3,7},{4,0},{5,1},{6,2},{7,3},{8,12},{9,13},{10,... | collective-permute-start | bytes 1769480 | tf_op jit(solution)/shard_map/ppermute | solution.py:208
  1003.4 11.6 %collective-permute-start.62 = (bf16[4,96,768]{2,1,0:T(8,128)(2,1)S(1)}, bf16[4,96,768]{2,1,0:T(8,128)(2,1)S(1)}, u32[]{:S(2)}, u32[]{:S(2)}) collective-permute-start(bf16[4,96,768]{2,1,0:T(8,128)(2,1)S(1)} %dynamic-slice_bitcast_fusion.11), channel_id=1, source_target_pairs={{0,2},{1,3},{2,0},{3,1},{4,6},{5,7},{6,4},{7,5},{8,10},{9,11},{10,... | collective-permute-start | bytes 1769480 | tf_op jit(solution)/shard_map/ppermute | solution.py:208
  1011.8 9.4 collective-permute-start.68
  1021.3 11.3 %collective-permute-start.69 = (bf16[1,24,3072]{2,1,0:T(8,128)(2,1)S(1)}, bf16[1,24,3072]{2,1,0:T(8,128)(2,1)S(1)}, u32[]{:S(2)}, u32[]{:S(2)}) collective-permute-start(bf16[1,24,3072]{2,1,0:T(8,128)(2,1)S(1)} %constant_dynamic-slice_fusion), channel_id=1, source_target_pairs={{0,16},{1,17},{2,18},{3,19},{4,20},{5,21},{6,22},{7,23},{8,24},{9,... | collective-permute-start | bytes 442376 | tf_op jit(solution)/shard_map/ppermute | solution.py:208
  1024.5 9.7 collective-permute-start.64
  (146 other events, 2826.8 us)

commit v2 on v1

--- a/solution.py
+++ b/solution.py
@@ -160,6 +160,107 @@
         scratch_shapes=[pltpu.VMEM((2,2*inner,ch),BF),pltpu.VMEM((2,2*inner,ch),F32),pltpu.VMEM((2,2*inner,2*ch),BF),pltpu.VMEM((2,2*inner,2*ch),F32),pltpu.VMEM((8,inner,ch),F32)],compiler_params=PAR)(coef,g.reshape(8,inner,ch),kspec,sspec,fwd,inv)
     return y.reshape(length,ch),kg.reshape(length,ch)
 
+def ff_kernel(x_ref,g_ref,wu_ref,wd_ref,bu_ref,down_ref,gsec_ref,dwu_ref,dwd_ref,dbu_ref,a_ref,gu_ref):
+    f=pl.program_id(0); rows=x_ref.shape[0]; step=256 if rows%256==0 else rows
+    wu=wu_ref[...]; wd=wd_ref[...]
+    total=jnp.zeros(dbu_ref.shape[1:],F32)
+    for r in range(rows//step):
+        at=pl.ds(r*step,step)
+        up=lax.dot_general(x_ref[at,:],wu,(((1,),(1,)),((),())),preferred_element_type=F32)+bu_ref[0]
+        ga=jnp.dot(g_ref[at,:],wd,preferred_element_type=F32)
+        sq=up*up
+        th=jnp.tanh(up*(GELU_A+(GELU_A*GELU_B)*sq))
+        half_one=0.5+0.5*th
+        a_ref[at,:]=(up*half_one).astype(BF)
+        slope=half_one+(up*half_one*(1.0-th))*(GELU_A+(3.0*GELU_A*GELU_B)*sq)
+        gu=ga*slope
+        total=total+jnp.sum(gu,axis=0,keepdims=True)
+        gu_ref[at,:]=gu.astype(BF)
+        down=lax.dot_general(a_ref[at,:],wd,(((1,),(1,)),((),())),preferred_element_type=F32)
+        gsec=jnp.dot(gu_ref[at,:],wu,preferred_element_type=F32)
+        @pl.when(f==0)
+        def _():
+            down_ref[at,:]=down
+            gsec_ref[at,:]=gsec
+        @pl.when(f>0)
+        def _():
+            down_ref[at,:]+=down
+            gsec_ref[at,:]+=gsec
+    dbu_ref[0]=total
+    dwu_ref[...]=lax.dot_general(gu_ref[...],x_ref[...],(((0,),(0,)),((),())),preferred_element_type=F32).astype(BF)
+    dwd_ref[...]=lax.dot_general(g_ref[...],a_ref[...],(((0,),(0,)),((),())),preferred_element_type=F32).astype(BF)
+
+GELU_A=0.7978845608
+GELU_B=0.044715
+
+def feed_forward(x,g,wu,wd,bu):
+    rows,width=x.shape; hid=wu.shape[0]; blk=512 if hid%512==0 else hid
+    n=hid//blk
+    return pl.pallas_call(ff_kernel,grid=(n,),
+        in_specs=[whole((rows,width)),whole((rows,width)),pl.BlockSpec((blk,width),lambda f:(f,0)),pl.BlockSpec((width,blk),lambda f:(0,f)),pl.BlockSpec((1,1,blk),lambda f:(f,0,0))],
+        out_specs=[whole((rows,width)),whole((rows,width)),pl.BlockSpec((blk,width),lambda f:(f,0)),pl.BlockSpec((width,blk),lambda f:(0,f)),pl.BlockSpec((1,1,blk),lambda f:(f,0,0))],
+        out_shape=[jax.ShapeDtypeStruct((rows,width),F32),jax.ShapeDtypeStruct((rows,width),F32),jax.ShapeDtypeStruct((hid,width),BF),jax.ShapeDtypeStruct((width,hid),BF),jax.ShapeDtypeStruct((n,1,blk),F32)],
+        scratch_shapes=[pltpu.VMEM((rows,blk),BF),pltpu.VMEM((rows,blk),BF)],
+        cost_estimate=pl.CostEstimate(flops=12*rows*width*hid,bytes_accessed=8*width*hid+12*rows*width,transcendentals=rows*hid),
+        compiler_params=PAR)(x,g,wu,wd,bu.reshape(n,1,blk))
+
+def tail_kernel(p_ref,gg_ref,jo_ref,cb_ref,gj_ref,af_ref,mk_ref,tap_ref,cbias_ref,skip_ref,
+                gp_ref,sums_ref,pw_ref,gc_ref):
+    b=pl.program_id(0); local=gg_ref.shape[1]; width=gg_ref.shape[2]; wide=3*width
+    step=64 if local%64==0 else local; lanes=128
+    @pl.when(b==0)
+    def _():
+        sums_ref[...]=jnp.zeros_like(sums_ref)
+    @pl.loop(0,width//lanes)
+    def _(j):
+        def cols(s): return pl.ds(pl.multiple_of(s*width+j*lanes,lanes),lanes)
+        c0=cols(0)
+        for s in range(3):
+            for r in range(-1,local//step):
+                if r<0: pw_ref[s,0:16,:]=p_ref[0,0:16,cols(s)].astype(F32)
+                else: pw_ref[s,16+r*step:16+(r+1)*step,:]=p_ref[0,16+r*step:16+(r+1)*step,cols(s)].astype(F32)
+        tap=[[tap_ref[k:k+1,cols(s)] for k in range(3)] for s in range(3)]
+        cbias=[cbias_ref[0:1,cols(s)] for s in range(3)]
+        skip=skip_ref[0:1,c0]
+        acc=[[jnp.zeros((8,lanes),F32) for _ in range(5)] for s in range(3)]
+        def fold(v): return jnp.sum(v.reshape(-1,8,lanes),axis=0)
+        for r in range(local//step):
+            lo=r*step
+            at=pl.ds(lo,step)
+            sh=[[pw_ref[s,14+lo+k:14+lo+k+step,:] for k in range(3)] for s in range(3)]
+            gate=[None]+[cbias[s]+tap[s][0]*sh[s][0]+tap[s][1]*sh[s][1]+tap[s][2]*sh[s][2] for s in (1,2)]
+            gg=gg_ref[0,at,c0]
+            gs=mk_ref[0,at,:]*(cb_ref[0,at,c0].astype(F32)+skip*gj_ref[0,at,c0].astype(F32))
+            gc=[gg*jo_ref[0,at,c0].astype(F32),gs*gate[2],gs*gate[1]]
+            for s in range(3):
+                gc_ref[s,at,:]=gc[s]
+                acc[s][0]=acc[s][0]+fold(gc[s])
+                for k in range(3):
+                    acc[s][1+k]=acc[s][1+k]+fold(gc[s]*sh[s][k])
+        for s in range(3):
+            gc_ref[s,local:local+8,:]=af_ref[0,:,cols(s)]
+        for r in range(local//step):
+            lo=r*step
+            at=pl.ds(lo,step)
+            mk=mk_ref[0,at,:]
+            for s in range(3):
+                gp=mk*(tap[s][2]*gc_ref[s,at,:]+tap[s][1]*gc_ref[s,lo+1:lo+1+step,:]+tap[s][0]*gc_ref[s,lo+2:lo+2+step,:])
+                acc[s][4]=acc[s][4]+fold(gp)
+                gp_ref[0,at,cols(s)]=gp.astype(BF)
+        for s in range(3):
+            for q in range(5):
+                sums_ref[q:q+1,cols(s)]+=jnp.sum(acc[s][q],axis=0,keepdims=True)
+
+def tail_back(p,gg,jo,cb,gj,af,mk,taps,cbias,skip):
+    blocks,local,width=gg.shape; wide=3*width
+    def blk(rows,cols): return pl.BlockSpec((1,rows,cols),lambda b:(b,0,0))
+    return pl.pallas_call(tail_kernel,grid=(blocks,),
+        in_specs=[blk(local+16,wide),blk(local,width),blk(local,width),blk(local,width),blk(local,width),blk(8,wide),blk(local,1),whole((3,wide)),whole((1,wide)),whole((1,width))],
+        out_specs=[blk(local,wide),whole((8,wide))],
+        out_shape=[jax.ShapeDtypeStruct((blocks,local,wide),BF),jax.ShapeDtypeStruct((8,wide),F32)],
+        scratch_shapes=[pltpu.VMEM((3,local+16,128),F32),pltpu.VMEM((3,local+8,128),F32)],
+        compiler_params=PAR)(p,gg,jo,cb,gj,af,mk,taps,cbias,skip)
+
 def product(left, right):
     return jnp.dot(left, right, precision=lax.Precision.HIGHEST, preferred_element_type=jnp.float32)
 
@@ -227,29 +328,20 @@
     def spread(i):
         return sum(((i >> p) & 1) << bit for p, bit in enumerate(order[:-1]))
 
-    def kernel(me_ref, near_ref, other_ref, out_ref, sems):
+    def kernel(me_ref, near_ref, other_ref, out_ref):
         own = me_ref[0]
-        copies = []
         for i in range(half):
-            at = jnp.bitwise_xor(own, spread(i))
-            copies.append(pltpu.make_async_copy(near_ref.at[i], out_ref.at[at], sems.at[i]))
-            flip = jnp.bitwise_xor(own, spread(i) | (1 << order[-1]))
-            copies.append(
-                pltpu.make_async_copy(other_ref.at[i], out_ref.at[flip], sems.at[half + i])
-            )
-        for copy in copies:
-            copy.start()
-        for copy in copies:
-            copy.wait()
-
-    hbm = pl.BlockSpec(memory_space=pl.ANY)
+            out_ref[jnp.bitwise_xor(own, spread(i))] = near_ref[i]
+            out_ref[jnp.bitwise_xor(own, spread(i) | (1 << order[-1]))] = other_ref[i]
+
+    vmem = pl.BlockSpec(memory_space=pltpu.VMEM)
     shape = (count, rows) + near.shape[1:]
     return pl.pallas_call(
         kernel,
-        in_specs=[SM, hbm, hbm],
-        out_specs=hbm,
+        in_specs=[SM, vmem, vmem],
+        out_specs=vmem,
         out_shape=jax.ShapeDtypeStruct(shape, near.dtype),
-        scratch_shapes=[pltpu.SemaphoreType.DMA((count,))],
+        compiler_params=PAR,
     )(
         me.reshape(1).astype(jnp.int32),
         near.reshape((half, rows) + near.shape[1:]),
@@ -523,18 +615,28 @@
 
         return jnp.concatenate(traded(give(0), give), axis=1)
 
+    def blocks_of(value):
+        return value.reshape(2, local, -1)
+
+    projected_low_all = jnp.concatenate(
+        [jnp.zeros((2, 14, before.shape[2]), BF), before.astype(BF), blocks.astype(BF)], axis=1
+    )
     sig_spec, carried_cols = long_conv(to_channels(signal), kernel_spec, tables)
     carried = to_rows(carried_cols.astype(BF)).astype(F32)
     signal_wide = signal.astype(F32)
     joined = carried + skip_gain * signal_wide
+    joined_low = joined.astype(BF)
     gated_mix = (joined * outer_gate).astype(BF)
     residual = tokens + dot_nt(gated_mix, mix_t) + mix_bias
     unit_two, rstd_two = normalise(residual)
     second_low = (unit_two * gain_two + shift_two).astype(BF)
-    up_proj = dot_nt(second_low, up_t) + up_bias
-    active_low, gelu_pull = jax.vjp(gelu_tanh, up_proj)
-    active_low = active_low.astype(BF)
-    output = (row_mask * (residual + dot_nt(active_low, down_t) + down_bias)).astype(BF)
+    grad_out = row_mask * adjoint.astype(F32)
+    grad_low = grad_out.astype(BF)
+    down_proj, grad_second, up_grad, down_grad, up_bias_grad = feed_forward(
+        second_low, grad_low, up_t, down_t, up_bias
+    )
+    up_bias_grad = up_bias_grad.reshape(-1)
+    output = (row_mask * (residual + down_proj + down_bias)).astype(BF)
 
     def to_home(value):
         far_part = swap_bit(value[local:], me, far, count)
@@ -543,15 +645,7 @@
 
     output_home = to_home(output)
 
-    grad_out = row_mask * adjoint.astype(F32)
-    grad_low = grad_out.astype(BF)
     down_bias_grad = jnp.sum(grad_out, axis=0)
-    down_grad = dot_tn(grad_low, active_low).astype(BF)
-    grad_up = gelu_pull(dot_nn(grad_low, down_t))[0]
-    up_bias_grad = jnp.sum(grad_up, axis=0)
-    grad_up_low = grad_up.astype(BF)
-    up_grad = dot_tn(grad_up_low, second_low).astype(BF)
-    grad_second = dot_nn(grad_up_low, up_t)
     gain_two_grad = jnp.sum(grad_second * unit_two, axis=0)
     shift_two_grad = jnp.sum(grad_second, axis=0)
     grad_residual = grad_out + normalise_back(unit_two, rstd_two, grad_second * gain_two)
@@ -564,33 +658,49 @@
 
     grad_gated = dot_nn(resid_low, mix_t)
     grad_joined = grad_gated * outer_gate
+    grad_joined_low = grad_joined.astype(BF)
     skip_grad = jnp.sum(grad_joined * signal_wide, axis=0)
     conv_back_cols, kernel_grad = long_back(
-        to_channels(grad_joined.astype(BF)), kernel_spec, sig_spec, tables
-    )
-    conv_back = to_rows(conv_back_cols.astype(BF)).astype(F32)
-    grad_signal = row_mask * (conv_back + skip_gain * grad_joined)
-    grad_conv = jnp.concatenate(
-        [grad_gated * joined, grad_signal * values, grad_signal * inner_gate], axis=1
-    )
-    conv_bias_grad = jnp.sum(grad_conv, axis=0)
-    taps_grad = jnp.stack([jnp.sum(grad_conv * shifted(k), axis=0) for k in range(3)])
-    conv_blocks = grad_conv.reshape(2, local, -1)
-    starts = ring(conv_blocks[:, :2], -1)
+        to_channels(grad_joined_low), kernel_spec, sig_spec, tables
+    )
+    conv_back_low = to_rows(conv_back_cols.astype(BF))
+    conv_back = conv_back_low.astype(F32)
+    first = blocks_of(grad_gated)[:, :2]
+    first_signal = blocks_of(row_mask)[:, :2] * (
+        blocks_of(conv_back)[:, :2] + skip_gain * blocks_of(grad_joined_low)[:, :2].astype(F32)
+    )
+    starts = ring(
+        jnp.concatenate(
+            [
+                first * blocks_of(joined_low)[:, :2].astype(F32),
+                first_signal * blocks_of(values)[:, :2],
+                first_signal * blocks_of(inner_gate)[:, :2],
+            ],
+            axis=2,
+        ),
+        -1,
+    )
     wrapped_after = jnp.stack(
         [jnp.where(side == 0, starts[1], 0.0), jnp.where(side == 1, starts[0], 0.0)]
     )
     after = jnp.where(rank == half - 1, wrapped_after, starts)
-    grad_extended = jnp.concatenate([conv_blocks, after], axis=1)
-
-    def ahead(by):
-        return grad_extended[:, by : by + local].reshape(rows, -1)
-
-    grad_projected = row_mask * (
-        conv_taps[2] * ahead(0) + conv_taps[1] * ahead(1) + conv_taps[0] * ahead(2)
-    )
-    intake_bias_grad = jnp.sum(grad_projected, axis=0)
-    projected_low = grad_projected.astype(BF)
+    after = jnp.concatenate([after, jnp.zeros((2, 6, after.shape[2]), F32)], axis=1)
+    grad_projected, sums = tail_back(
+        projected_low_all,
+        blocks_of(grad_gated),
+        blocks_of(joined_low),
+        blocks_of(conv_back_low),
+        blocks_of(grad_joined_low),
+        after,
+        blocks_of(row_mask),
+        conv_taps,
+        conv_bias.reshape(1, -1),
+        skip_gain.reshape(1, -1),
+    )
+    conv_bias_grad = sums[0]
+    taps_grad = sums[1:4]
+    intake_bias_grad = sums[4]
+    projected_low = grad_projected.reshape(rows, -1)
     intake_grad = dot_tn(projected_low, normed_low).astype(BF).reshape(count, -1, width)
     intake_shard_grad = jnp.concatenate(
         [

time: 1040 us -> 599 us (0.58)
  Pallas kernels: 498 us -> 122 us
  matrix products: 138 us -> 70.2 us
  other arithmetic: 125 us -> 101 us
  local copies, waits for them, and re-layouts: 85.6 us -> 97.7 us
    pallas_call x6 -> x8, Pallas kernels: 449 us -> 73.7 us  [the longest x1 44.6 us: feed_forward(): pl.pallas_call(ff_kernel, grid=(n,), in_specs=[whole((rows, width)), whol...]
    dot_general x4 -> x2, matrix products: 41.8 us -> 11.5 us  [dot_nn(): lax.dot_general(left, right, (((1,), (0,)), ((), ())), preferred_element_...]
    reduce_sum x2 -> x3, other arithmetic: 40.9 us -> 12.8 us  [the longest x1 5.45 us: per_device(): skip_grad = jnp.sum(grad_joined * signal_wide, axis=0)]
    dot_general x4 -> x2, matrix products: 27.7 us -> 8.61 us  [dot_nt(): lax.dot_general(left, right, (((1,), (1,)), ((), ())), preferred_element_...]
    dot_general x4 -> x2, matrix products: 26.9 us -> 8.45 us  [dot_tn(): lax.dot_general(left, right, (((0,), (0,)), ((), ())), preferred_element_...]
    unnamed x264 -> x240, local copies, waits for them, and re-layouts: 26.8 us -> 15.1 us
  transfers between devices with their start and end apart: 75 -> 75, of which waited for: 36 -> 29; matrix products, arithmetic and copies ran while one was open for 26% -> 41% of each run, Pallas kernels for 43% -> 12%
where the time goes in v2:
time: 599 us; the launch traced here: 589 us
  Pallas kernels  122 us (20%)
  waiting for transfers between devices  120 us (20%)
  other arithmetic  101 us (17%)
  local copies, waits for them, and re-layouts  97.7 us (16%)
  starting transfers between devices  72.9 us (12%)
  matrix products  70.2 us (12%)
    ppermute x69, waiting for transfers between devices, swap_bit(): return lax.ppermute(value, AXES, [(i, i ^ 1 << bit) for i in range(count)])  120 us
    ppermute x69, starting transfers between devices, swap_bit(): return lax.ppermute(value, AXES, [(i, i ^ 1 << bit) for i in range(count)])  72.5 us
    pallas_call x1, Pallas kernels, feed_forward(): pl.pallas_call(ff_kernel, grid=(n,), in_specs=[whole((rows, width)), whol...  44.6 us
    dot_general x11, matrix products, product(): jnp.dot(left, right, precision=lax.Precision.HIGHEST, preferred_element_t...  41.7 us
    pallas_call x1, Pallas kernels, long_back(): pl.pallas_call(back_kernel, grid=(RADIX // 4,), in_specs=[SM, whole((8, i...  22.5 us
    pallas_call x1, Pallas kernels, long_conv(): pl.pallas_call(conv_kernel, grid=(RADIX // 4,), in_specs=[SM, whole((8, i...  17.1 us
    unnamed x240, local copies, waits for them, and re-layouts  15.1 us
    pallas_call x6, Pallas kernels, place_shards(): pl.pallas_call(kernel, in_specs=[SM, vmem, vmem], out_specs=vmem, out_sha...  15 us
  transfers between devices with their start and end apart: 75, of which 29 were waited for; matrix products, arithmetic and copies ran while one was open for 41% of the time, Pallas kernels for 12%

profile of v2, /device:TPU:0, one launch (start us, length us, event | category | flops | bytes accessed | tf_op | source)
XLA Modules:
  0.0 589.2 jit_solution(2562008158253006640)
XLA Ops:
  2.5 6.8 %concatenate.185 = bf16[3072]{0:T(1024)(128)(2,1)S(1)} concatenate(bf16[24]{0:T(256)(128)(2,1)} %param.33, bf16[24]{0:T(256)(128)(2,1)} %param.34, bf16[24]{0:T(256)(128)(2,1)} %param.39, bf16[24]{0:T(256)(128)(2,1)} %param.42, bf16[24]{0:T(256)(128)(2,1)} %param.43, bf16[24]{0:T(256)(128)(2,1)} %param.44, bf16[24]{0:T(256)(128)(2,1)} %param.48, bf16[72]{0:T(256)(128)(2,1)} %param.36, ...), dimensions={0} | concatenate | bytes 12288 | tf_op jit(solution)/shard_map/concatenate | solution.py:469
  9.3 4.1 collective-permute-start.1
  19.8 2.9 collective-permute-start.11
  32.2 3.0 convolution_add_fusion.1
  36.0 3.0 convolution_add_fusion
  63.8 8.0 %fusion.26 = f32[2048,384]{1,0:T(8,128)} fusion(f32[384]{0:T(512)S(1)} %add_abs_fusion, f32[2048]{0:T(1024)S(1)} %copy-done.68, f32[2048,64]{0,1:T(8,128)S(1)} %convolution_add_fusion, f32[64]{0:T(128)S(1)} %copy-done.66, f32[64,768]{0,1:T(8,128)} %bitcast.349, s32[]{:T(128)S(6)} %select_n.323), kind=kOutput, calls=%fused_computation.52 | convolution fusion | flops 606470144 | bytes 3876612 | tf_op jit(solution)/shard_map/dot_general | solution.py:265
  79.0 7.9 %collective-permute-done.9 = bf16[576,384]{1,0:T(8,128)(2,1)S(1)} collective-permute-done((bf16[576,384]{1,0:T(8,128)(2,1)S(1)}, bf16[576,384]{1,0:T(8,128)(2,1)S(1)}, u32[]{:S(2)}, u32[]{:S(2)}) %collective-permute-start.9) | collective-permute-done | bytes 442400 | tf_op jit(solution)/shard_map/ppermute | solution.py:309
  111.0 9.2 %shard_map.480.k_ref = f32[4,2,512,384]{3,2,1,0:T(8,128)} custom-call(f32[4,16]{1,0:T(4,128)S(1)} %copy-done.3, f32[8,256,384]{2,1,0:T(8,128)} %bitcast.291, bf16[4,2,512,512]{3,2,1,0:T(8,128)(2,1)} %constant.279.clone.f_ref), custom_call_target="tpu_custom_call" | custom-call | tf_op jit(solution)/shard_map/pallas_call | solution.py:137
  134.6 5.3 add_multiply_fusion
  140.5 6.8 %collective-permute-done.19 = bf16[24,768]{1,0:T(8,128)(2,1)S(1)} collective-permute-done((bf16[24,768]{1,0:T(8,128)(2,1)S(1)}, bf16[24,768]{1,0:T(8,128)(2,1)S(1)}, u32[]{:S(2)}, u32[]{:S(2)}) %collective-permute-start.19) | collective-permute-done | bytes 36896 | tf_op jit(solution)/shard_map/ppermute | solution.py:309
  147.4 7.1 %fusion = (f32[2,512,2304]{2,1,0:T(8,128)}, f32[2,512,2304]{2,1,0:T(8,128)}) fusion(f32[2,2,2304]{2,1,0:T(2,128)S(1)} %get-tuple-element.229, f32[2,512,2304]{2,1,0:T(8,128)S(1)} %bitcast.284), kind=kLoop, calls=%fused_computation.2 | loop fusion | flops 4718592 | bytes 28348416 | tf_op jit(solution)/shard_map/concatenate | solution.py:573
  154.5 8.3 %fusion.2 = f32[1024,2304]{1,0:T(8,128)S(1)} fusion(f32[2,512,2304]{2,1,0:T(8,128)} %get-tuple-element.233, f32[2,512,2304]{2,1,0:T(8,128)} %get-tuple-element.232, f32[1024,2304]{1,0:T(8,128)S(1)} %add_multiply_fusion, f32[2304]{0:T(1024)S(1)} %copy-done.77, f32[2304]{0:T(1024)S(1)} %copy-done.78, f32[2304]{0:T(1024)S(1)} %copy-done.76, f32[2304]{0:T(1024)S(1)} %copy-done.75), kind=kLoop, calls=%fused_computation.6 | loop fusion | flops 14155776 | bytes 37785600 | tf_op jit(solution)/shard_map/add | solution.py:580
  162.8 4.2 fusion.24
  175.0 3.2 collective-permute-done.26
  179.4 4.7 collective-permute-done.31
  187.4 11.7 %collective-permute-done.32 = bf16[96,3072]{1,0:T(8,128)(2,1)S(1)} collective-permute-done((bf16[96,3072]{1,0:T(8,128)(2,1)S(1)}, bf16[96,3072]{1,0:T(8,128)(2,1)S(1)}, u32[]{:S(2)}, u32[]{:S(2)}) %collective-permute-start.32) | collective-permute-done | bytes 589856 | tf_op jit(solution)/shard_map/ppermute | solution.py:309
  204.0 17.1 %shard_map.481 = (bf16[4,2,512,384]{3,2,1,0:T(8,128)(2,1)}, f32[8,256,384]{2,1,0:T(8,128)}) custom-call(f32[4,16]{1,0:T(4,128)S(1)} %copy-done.3, bf16[8,256,384]{2,1,0:T(8,128)(2,1)S(1)} %bitcast.273, f32[4,2,512,384]{3,2,1,0:T(8,128)} %shard_map.480.k_ref, bf16[4,2,512,512]{3,2,1,0:T(8,128)(2,1)} %constant.279.clone.f_ref, ...), custom_call_target="tpu_custom_call" | custom-call | tf_op jit(solution)/shard_map/pallas_call | solution.py:146
  232.5 3.6 pad_maximum_fusion.1.p_ref
  239.7 3.9 fusion.27
  243.6 3.3 fusion.85
  248.1 4.9 shard_map.484
  253.1 4.8 shard_map.483
  257.9 44.6 %shard_map.485 = (f32[1024,768]{1,0:T(8,128)}, f32[1024,768]{1,0:T(8,128)}, bf16[3072,768]{1,0:T(8,128)(2,1)}, bf16[768,3072]{1,0:T(8,128)(2,1)}, f32[6,1,512]{2,1,0:T(1,128)S(1)}) custom-call(bf16[1024,768]{1,0:T(8,128)(2,1)S(1)} %add_convert_fusion.x_ref, bf16[1024,768]{1,0:T(8,128)(2,1)} %get-tuple-element.246.g_ref, bf16[3072,768]{1,0:T(8,128)(2,1)} %bitcast.316, ...), custom_call_target="tpu_custom_call" | custom-call | flops 28991029248 | bytes 28311552 | tf_op jit(solution)/shard_map/pallas_call | solution.py:199
  302.5 3.2 multiply_reduce_fusion
  305.7 4.4 fusion.74
  312.4 3.0 fusion.39
  318.6 5.5 fusion.22
  325.3 3.3 dynamic-slice_bitcast_fusion
  332.3 3.3 dynamic-slice_bitcast_fusion.1
  342.2 22.5 %shard_map.486 = (f32[8,256,384]{2,1,0:T(8,128)}, f32[8,256,384]{2,1,0:T(8,128)}) custom-call(f32[4,16]{1,0:T(4,128)S(1)} %copy-done.3, bf16[8,256,384]{2,1,0:T(8,128)(2,1)S(1)} %bitcast.272, f32[4,2,512,384]{3,2,1,0:T(8,128)} %shard_map.480.k_ref, bf16[4,2,512,384]{3,2,1,0:T(8,128)(2,1)} %get-tuple-element.47.s_ref, ...), custom_call_target="tpu_custom_call" | custom-call | tf_op jit(solution)/shard_map/pallas_call | solution.py:156
  367.4 4.8 convolution_multiply_fusion.2
  372.3 3.0 fusion.47
  377.6 3.1 multiply_reduce_fusion.7
  380.7 3.2 fusion.46
  383.9 6.3 %convolution_dynamic-update-slice_fusion = f32[64,768]{0,1:T(8,128)S(1)} fusion(f32[64,768]{0,1:T(8,128)S(1)} %broadcast_in_dim.18, s32[]{:T(128)S(6)} %select_n.323, f32[2048,384]{1,0:T(8,128)S(1)} %bitcast_multiply_fusion.2, f32[2048,64]{0,1:T(8,128)S(1)} %copy-done.7, f32[64]{0:T(128)S(1)} %copy-done.67), kind=kOutput, calls=%fused_computation.95 | convolution fusion | flops 604110848 | bytes 3867140 | tf_op jit(solution)/shard_map/dot_general | solution.py:265
  404.5 3.2 collective-permute-done.72
  421.0 3.0 collective-permute-done.58
  434.5 14.2 %shard_map.487 = (bf16[2,512,2304]{2,1,0:T(8,128)(2,1)}, f32[8,2304]{1,0:T(8,128)S(1)}) custom-call(bf16[2,528,2304]{2,1,0:T(8,128)(2,1)} %pad_maximum_fusion.1.p_ref, f32[2,512,768]{2,1,0:T(8,128)} %bitcast.290, bf16[2,512,768]{2,1,0:T(8,128)(2,1)} %bitcast.305, bf16[2,512,768]{2,1,0:T(8,128)(2,1)} %bitcast.306, bf16[2,512,768]{2,1,0:T(8,128)(2,1)} %bitcast.288, ...), custom_call_target="tpu_custom_call" | custom-call | tf_op jit(solution)/shard_map/pallas_call | solution.py:257
  448.8 8.5 %fusion.19 = (f32[768]{0:T(1024)S(1)}, f32[1024]{0:T(1024)S(1)}, f32[1024]{0:T(1024)S(1)}, f32[768]{0:T(1024)S(1)}, f32[1024,768]{1,0:T(8,128)}) fusion(f32[1024]{0:T(1024)S(1)} %copy-done.93, f32[1024]{0:T(1024)S(1)} %copy-done.83, bf16[512,768]{1,0:T(8,128)(2,1)} %collective-permute-done, bf16[512,768]{1,0:T(8,128)(2,1)S(1)} %copy-done.12, ...), kind=kOutput, calls=%fused_computation.35 | convolution fusion | flops 3634098688 | bytes 13001728 | tf_op jit(solution)/shard_map/dot_general | solution.py:401
  458.9 7.0 %convolution_convert_fusion = bf16[2304,768]{1,0:T(8,128)(2,1)S(1)} fusion(bf16[1024,2304]{1,0:T(8,128)(2,1)} %bitcast.388, f32[768]{0:T(1024)S(1)} %copy-done.98, f32[768]{0:T(1024)S(1)} %copy-done.90, f32[1024]{0:T(1024)S(1)} %copy-done.93, f32[1024]{0:T(1024)S(1)} %copy-done.83, bf16[512,768]{1,0:T(8,128)(2,1)} %collective-permute-done, ...), kind=kOutput, calls=%fused_computation.10 | convolution fusion | flops 3632726016 | bytes 9844736 | tf_op jit(solution)/shard_map/dot_general | solution.py:405
  470.1 2.9 collective-permute-done.41
  492.2 3.3 fusion.4
  507.0 26.6 %collective-permute-done.46 = bf16[8,72,384]{2,1,0:T(8,128)(2,1)S(1)} collective-permute-done((bf16[8,72,384]{2,1,0:T(8,128)(2,1)S(1)}, bf16[8,72,384]{2,1,0:T(8,128)(2,1)S(1)}, u32[]{:S(2)}, u32[]{:S(2)}) %collective-permute-start.46) | collective-permute-done | bytes 442400 | tf_op jit(solution)/shard_map/ppermute | solution.py:309
  538.5 3.4 collective-permute-done.47
  556.9 8.2 %collective-permute-done.67 = bf16[4,24,3072]{2,1,0:T(8,128)(2,1)S(1)} collective-permute-done((bf16[4,24,3072]{2,1,0:T(8,128)(2,1)S(1)}, bf16[4,24,3072]{2,1,0:T(8,128)(2,1)S(1)}, u32[]{:S(2)}, u32[]{:S(2)}) %collective-permute-start.67) | collective-permute-done | bytes 589856 | tf_op jit(solution)/shard_map/ppermute | solution.py:309
  569.1 5.5 collective-permute-done.68
  577.1 3.9 collective-permute-done.63
  582.3 5.7 collective-permute-done.64
  (607 shorter events, 245.3 us)
Async XLA Ops:
  9.3 30.5 %collective-permute-start.1 = (f32[8,384]{1,0:T(8,128)S(1)}, f32[8,384]{1,0:T(8,128)S(1)}, u32[]{:S(2)}, u32[]{:S(2)}) collective-permute-start(f32[8,384]{1,0:T(8,128)S(1)} %reshape.675), channel_id=1, source_target_pairs={{0,16},{1,17},{2,18},{3,19},{4,20},{5,21},{6,22},{7,23},{8,24},{9,... | collective-permute-start | bytes 36872 | tf_op jit(solution)/shard_map/ppermute | solution.py:309
  15.8 104.5 %collective-permute-start = (bf16[512,768]{1,0:T(8,128)(2,1)}, bf16[512,768]{1,0:T(8,128)(2,1)}, u32[]{:S(2)}, u32[]{:S(2)}) collective-permute-start(bf16[512,768]{1,0:T(8,128)(2,1)} %get-tuple-element.266), channel_id=1, source_target_pairs={{0,2},{1,3},{2,0},{3,1},{4,6},{5,7},{6,4},{7,5},{8,10},{9,11},{10,... | collective-permute-start | bytes 2359304 | tf_op jit(solution)/shard_map/ppermute | solution.py:309
  18.5 144.3 %collective-permute-start.24 = (bf16[512,768]{1,0:T(8,128)(2,1)}, bf16[512,768]{1,0:T(8,128)(2,1)}, u32[]{:S(2)}, u32[]{:S(2)}) collective-permute-start(bf16[512,768]{1,0:T(8,128)(2,1)} %get-tuple-element.258), channel_id=1, source_target_pairs={{0,2},{1,3},{2,0},{3,1},{4,6},{5,7},{6,4},{7,5},{8,10},{9,11},{10,... | collective-permute-start | bytes 2359304 | tf_op jit(solution)/shard_map/ppermute | solution.py:309
  19.7 25.5 %collective-permute-start.6 = (bf16[72,384]{1,0:T(8,128)(2,1)S(1)}, bf16[72,384]{1,0:T(8,128)(2,1)S(1)}, u32[]{:S(2)}, u32[]{:S(2)}) collective-permute-start(bf16[72,384]{1,0:T(8,128)(2,1)S(1)} %get-tuple-element.284), channel_id=1, source_target_pairs={{0,16},{1,17},{2,18},{3,19},{4,20},{5,21},{6,22},{7,23},{8,24},{9,... | collective-permute-start | bytes 165896 | tf_op jit(solution)/shard_map/ppermute | solution.py:309
  19.8 27.1 %collective-permute-start.11 = (bf16[72,384]{1,0:T(8,128)(2,1)}, bf16[72,384]{1,0:T(8,128)(2,1)S(1)}, u32[]{:S(2)}, u32[]{:S(2)}) collective-permute-start(bf16[72,384]{1,0:T(8,128)(2,1)} %get-tuple-element.287), channel_id=1, source_target_pairs={{0,16},{1,17},{2,18},{3,19},{4,20},{5,21},{6,22},{7,23},{8,24},{9,... | collective-permute-start | bytes 165896 | tf_op jit(solution)/shard_map/ppermute | solution.py:309
  52.1 21.8 %collective-permute-start.8 = (bf16[288,384]{1,0:T(8,128)(2,1)}, bf16[288,384]{1,0:T(8,128)(2,1)}, u32[]{:S(2)}, u32[]{:S(2)}) collective-permute-start(bf16[288,384]{1,0:T(8,128)(2,1)} %pad_maximum_fusion.22), channel_id=1, source_target_pairs={{0,4},{1,5},{2,6},{3,7},{4,0},{5,1},{6,2},{7,3},{8,12},{9,13},{10,... | collective-permute-start | bytes 663560 | tf_op jit(solution)/shard_map/ppermute | solution.py:309
  54.7 17.1 %collective-permute-start.13 = (bf16[288,384]{1,0:T(8,128)(2,1)}, bf16[288,384]{1,0:T(8,128)(2,1)}, u32[]{:S(2)}, u32[]{:S(2)}) collective-permute-start(bf16[288,384]{1,0:T(8,128)(2,1)} %pad_maximum_fusion.23), channel_id=1, source_target_pairs={{0,2},{1,3},{2,0},{3,1},{4,6},{5,7},{6,4},{7,5},{8,10},{9,11},{10,... | collective-permute-start | bytes 663560 | tf_op jit(solution)/shard_map/ppermute | solution.py:309
  72.8 14.3 %collective-permute-start.14 = (bf16[576,384]{1,0:T(8,128)(2,1)S(1)}, bf16[576,384]{1,0:T(8,128)(2,1)S(1)}, u32[]{:S(2)}, u32[]{:S(2)}) collective-permute-start(bf16[576,384]{1,0:T(8,128)(2,1)S(1)} %pad_maximum_fusion.18), channel_id=1, source_target_pairs={{0,4},{1,5},{2,6},{3,7},{4,0},{5,1},{6,2},{7,3},{8,12},{9,13},{10,... | collective-permute-start | bytes 1327112 | tf_op jit(solution)/shard_map/ppermute | solution.py:309
  74.9 12.0 %collective-permute-start.9 = (bf16[576,384]{1,0:T(8,128)(2,1)S(1)}, bf16[576,384]{1,0:T(8,128)(2,1)S(1)}, u32[]{:S(2)}, u32[]{:S(2)}) collective-permute-start(bf16[576,384]{1,0:T(8,128)(2,1)S(1)} %pad_maximum_fusion.17), channel_id=1, source_target_pairs={{0,2},{1,3},{2,0},{3,1},{4,6},{5,7},{6,4},{7,5},{8,10},{9,11},{10,... | collective-permute-start | bytes 1327112 | tf_op jit(solution)/shard_map/ppermute | solution.py:309
  87.0 36.5 %collective-permute-start.10 = (bf16[1152,384]{1,0:T(8,128)(2,1)S(1)}, bf16[1152,384]{1,0:T(8,128)(2,1)S(1)}, u32[]{:S(2)}, u32[]{:S(2)}) collective-permute-start(bf16[1152,384]{1,0:T(8,128)(2,1)S(1)} %constant_dynamic-update-slice_fusion.5), channel_id=1, source_target_pairs={{0,1},{1,0},{2,3},{3,2},{4,5},{5,4},{6,7},{7,6},{8,9},{9,8},{10,11... | collective-permute-start | bytes 2654216 | tf_op jit(solution)/shard_map/ppermute | solution.py:309
  87.2 37.7 %collective-permute-start.15 = (bf16[1152,384]{1,0:T(8,128)(2,1)S(1)}, bf16[1152,384]{1,0:T(8,128)(2,1)}, u32[]{:S(2)}, u32[]{:S(2)}) collective-permute-start(bf16[1152,384]{1,0:T(8,128)(2,1)S(1)} %constant_dynamic-update-slice_fusion.10), channel_id=1, source_target_pairs={{0,1},{1,0},{2,3},{3,2},{4,5},{5,4},{6,7},{7,6},{8,9},{9,8},{10,11... | collective-permute-start | bytes 2654216 | tf_op jit(solution)/shard_map/ppermute | solution.py:309
  129.5 38.8 %collective-permute-start.25 = (bf16[96,768]{1,0:T(8,128)(2,1)S(1)}, bf16[96,768]{1,0:T(8,128)(2,1)S(1)}, u32[]{:S(2)}, u32[]{:S(2)}) collective-permute-start(bf16[96,768]{1,0:T(8,128)(2,1)S(1)} %bitcast.334), channel_id=1, source_target_pairs={{0,16},{1,17},{2,18},{3,19},{4,20},{5,21},{6,22},{7,23},{8,24},{9,... | collective-permute-start | bytes 442376 | tf_op jit(solution)/shard_map/ppermute | solution.py:309
  130.9 39.5 %collective-permute-start.30 = (bf16[24,3072]{1,0:T(8,128)(2,1)S(1)}, bf16[24,3072]{1,0:T(8,128)(2,1)S(1)}, u32[]{:S(2)}, u32[]{:S(2)}) collective-permute-start(bf16[24,3072]{1,0:T(8,128)(2,1)S(1)} %bitcast.329), channel_id=1, source_target_pairs={{0,16},{1,17},{2,18},{3,19},{4,20},{5,21},{6,22},{7,23},{8,24},{9,... | collective-permute-start | bytes 442376 | tf_op jit(solution)/shard_map/ppermute | solution.py:309
  133.8 13.5 %collective-permute-start.19 = (bf16[24,768]{1,0:T(8,128)(2,1)S(1)}, bf16[24,768]{1,0:T(8,128)(2,1)S(1)}, u32[]{:S(2)}, u32[]{:S(2)}) collective-permute-start(bf16[24,768]{1,0:T(8,128)(2,1)S(1)} %bitcast.372), channel_id=1, source_target_pairs={{0,16},{1,17},{2,18},{3,19},{4,20},{5,21},{6,22},{7,23},{8,24},{9,... | collective-permute-start | bytes 110600 | tf_op jit(solution)/shard_map/ppermute | solution.py:309
  147.3 19.9 %collective-permute-start.20 = (bf16[48,768]{1,0:T(8,128)(2,1)S(1)}, bf16[48,768]{1,0:T(8,128)(2,1)S(1)}, u32[]{:S(2)}, u32[]{:S(2)}) collective-permute-start(bf16[48,768]{1,0:T(8,128)(2,1)S(1)} %pad_maximum_fusion.28), channel_id=1, source_target_pairs={{0,8},{1,9},{2,10},{3,11},{4,12},{5,13},{6,14},{7,15},{8,0},{9,1},... | collective-permute-start | bytes 221192 | tf_op jit(solution)/shard_map/ppermute | solution.py:309
  167.1 19.8 %collective-permute-start.17 = (bf16[1024,384]{1,0:T(8,128)(2,1)S(1)}, bf16[1024,384]{1,0:T(8,128)(2,1)S(1)}, u32[]{:S(2)}, u32[]{:S(2)}) collective-permute-start(bf16[1024,384]{1,0:T(8,128)(2,1)S(1)} %constant_dynamic-slice_fusion.8), channel_id=1, source_target_pairs={{0,1},{1,0},{2,3},{3,2},{4,5},{5,4},{6,7},{7,6},{8,9},{9,8},{10,11... | collective-permute-start | bytes 2359304 | tf_op jit(solution)/shard_map/ppermute | solution.py:593
  168.3 9.9 %collective-permute-start.26 = (bf16[192,768]{1,0:T(8,128)(2,1)S(1)}, bf16[192,768]{1,0:T(8,128)(2,1)S(1)}, u32[]{:S(2)}, u32[]{:S(2)}) collective-permute-start(bf16[192,768]{1,0:T(8,128)(2,1)S(1)} %pad_maximum_fusion.20), channel_id=1, source_target_pairs={{0,8},{1,9},{2,10},{3,11},{4,12},{5,13},{6,14},{7,15},{8,0},{9,1},... | collective-permute-start | bytes 884744 | tf_op jit(solution)/shard_map/ppermute | solution.py:309
  170.4 13.7 %collective-permute-start.31 = (bf16[48,3072]{1,0:T(8,128)(2,1)S(1)}, bf16[48,3072]{1,0:T(8,128)(2,1)S(1)}, u32[]{:S(2)}, u32[]{:S(2)}) collective-permute-start(bf16[48,3072]{1,0:T(8,128)(2,1)S(1)} %pad_maximum_fusion.21), channel_id=1, source_target_pairs={{0,8},{1,9},{2,10},{3,11},{4,12},{5,13},{6,14},{7,15},{8,0},{9,1},... | collective-permute-start | bytes 884744 | tf_op jit(solution)/shard_map/ppermute | solution.py:309
  173.6 13.2 %collective-permute-start.22 = (bf16[192,768]{1,0:T(8,128)(2,1)S(1)}, bf16[192,768]{1,0:T(8,128)(2,1)S(1)}, u32[]{:S(2)}, u32[]{:S(2)}) collective-permute-start(bf16[192,768]{1,0:T(8,128)(2,1)S(1)} %pad_maximum_fusion.19), channel_id=1, source_target_pairs={{0,2},{1,3},{2,0},{3,1},{4,6},{5,7},{6,4},{7,5},{8,10},{9,11},{10,... | collective-permute-start | bytes 884744 | tf_op jit(solution)/shard_map/ppermute | solution.py:309
  178.2 23.2 %collective-permute-start.27 = (bf16[384,768]{1,0:T(8,128)(2,1)S(1)}, bf16[384,768]{1,0:T(8,128)(2,1)S(1)}, u32[]{:S(2)}, u32[]{:S(2)}) collective-permute-start(bf16[384,768]{1,0:T(8,128)(2,1)S(1)} %pad_maximum_fusion.15), channel_id=1, source_target_pairs={{0,2},{1,3},{2,0},{3,1},{4,6},{5,7},{6,4},{7,5},{8,10},{9,11},{10,... | collective-permute-start | bytes 1769480 | tf_op jit(solution)/shard_map/ppermute | solution.py:309
  184.1 15.0 %collective-permute-start.32 = (bf16[96,3072]{1,0:T(8,128)(2,1)S(1)}, bf16[96,3072]{1,0:T(8,128)(2,1)S(1)}, u32[]{:S(2)}, u32[]{:S(2)}) collective-permute-start(bf16[96,3072]{1,0:T(8,128)(2,1)S(1)} %pad_maximum_fusion.16), channel_id=1, source_target_pairs={{0,4},{1,5},{2,6},{3,7},{4,0},{5,1},{6,2},{7,3},{8,12},{9,13},{10,... | collective-permute-start | bytes 1769480 | tf_op jit(solution)/shard_map/ppermute | solution.py:309
  186.8 50.1 %collective-permute-start.23 = (bf16[384,768]{1,0:T(8,128)(2,1)S(1)}, bf16[384,768]{1,0:T(8,128)(2,1)S(1)}, u32[]{:S(2)}, u32[]{:S(2)}) collective-permute-start(bf16[384,768]{1,0:T(8,128)(2,1)S(1)} %constant_dynamic-update-slice_fusion.15), channel_id=1, source_target_pairs={{0,1},{1,0},{2,3},{3,2},{4,5},{5,4},{6,7},{7,6},{8,9},{9,8},{10,11... | collective-permute-start | bytes 1769480 | tf_op jit(solution)/shard_map/ppermute | solution.py:309
  200.3 27.0 %collective-permute-start.33 = (bf16[192,3072]{1,0:T(8,128)(2,1)}, bf16[192,3072]{1,0:T(8,128)(2,1)}, u32[]{:S(2)}, u32[]{:S(2)}) collective-permute-start(bf16[192,3072]{1,0:T(8,128)(2,1)} %pad_maximum_fusion.10), channel_id=1, source_target_pairs={{0,2},{1,3},{2,0},{3,1},{4,6},{5,7},{6,4},{7,5},{8,10},{9,11},{10,... | collective-permute-start | bytes 3538952 | tf_op jit(solution)/shard_map/ppermute | solution.py:309
  202.6 27.5 %collective-permute-start.28 = (bf16[768,768]{1,0:T(8,128)(2,1)}, bf16[768,768]{1,0:T(8,128)(2,1)}, u32[]{:S(2)}, u32[]{:S(2)}) collective-permute-start(bf16[768,768]{1,0:T(8,128)(2,1)} %pad_maximum_fusion.9), channel_id=1, source_target_pairs={{0,4},{1,5},{2,6},{3,7},{4,0},{5,1},{6,2},{7,3},{8,12},{9,13},{10,... | collective-permute-start | bytes 3538952 | tf_op jit(solution)/shard_map/ppermute | solution.py:309
  225.4 12.6 %collective-permute-start.18 = (bf16[1024,384]{1,0:T(8,128)(2,1)}, bf16[1024,384]{1,0:T(8,128)(2,1)}, u32[]{:S(2)}, u32[]{:S(2)}) collective-permute-start(bf16[1024,384]{1,0:T(8,128)(2,1)} %pad_maximum_fusion.12), channel_id=1, source_target_pairs={{0,1},{1,0},{2,3},{3,2},{4,5},{5,4},{6,7},{7,6},{8,9},{9,8},{10,11... | collective-permute-start | bytes 2359304 | tf_op jit(solution)/shard_map/ppermute | solution.py:593
  229.6 18.5 %collective-permute-start.34 = (bf16[384,3072]{1,0:T(8,128)(2,1)}, bf16[384,3072]{1,0:T(8,128)(2,1)}, u32[]{:S(2)}, u32[]{:S(2)}) collective-permute-start(bf16[384,3072]{1,0:T(8,128)(2,1)} %constant_dynamic-update-slice_fusion.25), channel_id=1, source_target_pairs={{0,1},{1,0},{2,3},{3,2},{4,5},{5,4},{6,7},{7,6},{8,9},{9,8},{10,11... | collective-permute-start | bytes 7077896 | tf_op jit(solution)/shard_map/ppermute | solution.py:309
  232.4 20.7 %collective-permute-start.29 = (bf16[1536,768]{1,0:T(8,128)(2,1)}, bf16[1536,768]{1,0:T(8,128)(2,1)}, u32[]{:S(2)}, u32[]{:S(2)}) collective-permute-start(bf16[1536,768]{1,0:T(8,128)(2,1)} %constant_dynamic-update-slice_fusion.20), channel_id=1, source_target_pairs={{0,1},{1,0},{2,3},{3,2},{4,5},{5,4},{6,7},{7,6},{8,9},{9,8},{10,11... | collective-permute-start | bytes 7077896 | tf_op jit(solution)/shard_map/ppermute | solution.py:309
  316.2 21.0 %collective-permute-start.55 = (bf16[16,24,768]{2,1,0:T(8,128)(2,1)}, bf16[16,24,768]{2,1,0:T(8,128)(2,1)}, u32[]{:S(2)}, u32[]{:S(2)}) collective-permute-start(bf16[16,24,768]{2,1,0:T(8,128)(2,1)} %dynamic-slice_bitcast_fusion.12), channel_id=1, source_target_pairs={{0,1},{1,0},{2,3},{3,2},{4,5},{5,4},{6,7},{7,6},{8,9},{9,8},{10,11... | collective-permute-start | bytes 1769480 | tf_op jit(solution)/shard_map/ppermute | solution.py:309
  317.9 94.7 %collective-permute-start.35 = (bf16[512,768]{1,0:T(8,128)(2,1)}, bf16[512,768]{1,0:T(8,128)(2,1)}, u32[]{:S(2)}, u32[]{:S(2)}) collective-permute-start(bf16[512,768]{1,0:T(8,128)(2,1)} %get-tuple-element.256), channel_id=1, source_target_pairs={{0,2},{1,3},{2,0},{3,1},{4,6},{5,7},{6,4},{7,5},{8,10},{9,11},{10,... | collective-permute-start | bytes 2359304 | tf_op jit(solution)/shard_map/ppermute | solution.py:309
  325.1 15.3 %collective-permute-start.36 = (bf16[1024,384]{1,0:T(8,128)(2,1)}, bf16[1024,384]{1,0:T(8,128)(2,1)}, u32[]{:S(2)}, u32[]{:S(2)}) collective-permute-start(bf16[1024,384]{1,0:T(8,128)(2,1)} %constant_dynamic-slice_fusion.7), channel_id=1, source_target_pairs={{0,1},{1,0},{2,3},{3,2},{4,5},{5,4},{6,7},{7,6},{8,9},{9,8},{10,11... | collective-permute-start | bytes 2359304 | tf_op jit(solution)/shard_map/ppermute | solution.py:593
  332.1 160.1 %collective-permute-start.65 = (bf16[16,24,3072]{2,1,0:T(8,128)(2,1)}, bf16[16,24,3072]{2,1,0:T(8,128)(2,1)}, u32[]{:S(2)}, u32[]{:S(2)}) collective-permute-start(bf16[16,24,3072]{2,1,0:T(8,128)(2,1)} %dynamic-slice_bitcast_fusion), channel_id=1, source_target_pairs={{0,1},{1,0},{2,3},{3,2},{4,5},{5,4},{6,7},{7,6},{8,9},{9,8},{10,11... | collective-permute-start | bytes 7077896 | tf_op jit(solution)/shard_map/ppermute | solution.py:309
  335.6 161.4 %collective-permute-start.60 = (bf16[16,96,768]{2,1,0:T(8,128)(2,1)}, bf16[16,96,768]{2,1,0:T(8,128)(2,1)}, u32[]{:S(2)}, u32[]{:S(2)}) collective-permute-start(bf16[16,96,768]{2,1,0:T(8,128)(2,1)} %dynamic-slice_bitcast_fusion.1), channel_id=1, source_target_pairs={{0,1},{1,0},{2,3},{3,2},{4,5},{5,4},{6,7},{7,6},{8,9},{9,8},{10,11... | collective-permute-start | bytes 7077896 | tf_op jit(solution)/shard_map/ppermute | solution.py:309
  339.3 64.2 %collective-permute-start.56 = (bf16[8,24,768]{2,1,0:T(8,128)(2,1)}, bf16[8,24,768]{2,1,0:T(8,128)(2,1)S(1)}, u32[]{:S(2)}, u32[]{:S(2)}) collective-permute-start(bf16[8,24,768]{2,1,0:T(8,128)(2,1)} %dynamic-slice_bitcast_fusion.17), channel_id=1, source_target_pairs={{0,2},{1,3},{2,0},{3,1},{4,6},{5,7},{6,4},{7,5},{8,10},{9,11},{10,... | collective-permute-start | bytes 884744 | tf_op jit(solution)/shard_map/ppermute | solution.py:309
  403.5 26.1 %collective-permute-start.37 = (bf16[1024,384]{1,0:T(8,128)(2,1)}, bf16[1024,384]{1,0:T(8,128)(2,1)}, u32[]{:S(2)}, u32[]{:S(2)}) collective-permute-start(bf16[1024,384]{1,0:T(8,128)(2,1)} %pad_maximum_fusion.14), channel_id=1, source_target_pairs={{0,1},{1,0},{2,3},{3,2},{4,5},{5,4},{6,7},{7,6},{8,9},{9,8},{10,11... | collective-permute-start | bytes 2359304 | tf_op jit(solution)/shard_map/ppermute | solution.py:593
  458.4 9.9 %collective-permute-start.40 = (f32[16,8,384]{2,1,0:T(8,128)S(1)}, f32[16,8,384]{2,1,0:T(8,128)S(1)}, u32[]{:S(2)}, u32[]{:S(2)}) collective-permute-start(f32[16,8,384]{2,1,0:T(8,128)S(1)} %dynamic-slice_bitcast_fusion.20), channel_id=1, source_target_pairs={{0,1},{1,0},{2,3},{3,2},{4,5},{5,4},{6,7},{7,6},{8,9},{9,8},{10,11... | collective-permute-start | bytes 589832 | tf_op jit(solution)/shard_map/ppermute | solution.py:309
  475.4 28.8 %collective-permute-start.39 = (bf16[512,768]{1,0:T(8,128)(2,1)}, bf16[512,768]{1,0:T(8,128)(2,1)}, u32[]{:S(2)}, u32[]{:S(2)}) collective-permute-start(bf16[512,768]{1,0:T(8,128)(2,1)} %get-tuple-element.248), channel_id=1, source_target_pairs={{0,2},{1,3},{2,0},{3,1},{4,6},{5,7},{6,4},{7,5},{8,10},{9,11},{10,... | collective-permute-start | bytes 2359304 | tf_op jit(solution)/shard_map/ppermute | solution.py:309
  484.4 15.9 %collective-permute-start.45 = (bf16[16,72,384]{2,1,0:T(8,128)(2,1)}, bf16[16,72,384]{2,1,0:T(8,128)(2,1)}, u32[]{:S(2)}, u32[]{:S(2)}) collective-permute-start(bf16[16,72,384]{2,1,0:T(8,128)(2,1)} %dynamic-slice_bitcast_fusion.5), channel_id=1, source_target_pairs={{0,1},{1,0},{2,3},{3,2},{4,5},{5,4},{6,7},{7,6},{8,9},{9,8},{10,11... | collective-permute-start | bytes 2654216 | tf_op jit(solution)/shard_map/ppermute | solution.py:309
  485.8 17.3 %collective-permute-start.50 = (bf16[16,72,384]{2,1,0:T(8,128)(2,1)}, bf16[16,72,384]{2,1,0:T(8,128)(2,1)S(1)}, u32[]{:S(2)}, u32[]{:S(2)}) collective-permute-start(bf16[16,72,384]{2,1,0:T(8,128)(2,1)} %dynamic-slice_bitcast_fusion.4), channel_id=1, source_target_pairs={{0,1},{1,0},{2,3},{3,2},{4,5},{5,4},{6,7},{7,6},{8,9},{9,8},{10,11... | collective-permute-start | bytes 2654216 | tf_op jit(solution)/shard_map/ppermute | solution.py:309
  495.6 57.2 %collective-permute-start.66 = (bf16[8,24,3072]{2,1,0:T(8,128)(2,1)S(1)}, bf16[8,24,3072]{2,1,0:T(8,128)(2,1)S(1)}, u32[]{:S(2)}, u32[]{:S(2)}) collective-permute-start(bf16[8,24,3072]{2,1,0:T(8,128)(2,1)S(1)} %dynamic-slice_bitcast_fusion.2), channel_id=1, source_target_pairs={{0,2},{1,3},{2,0},{3,1},{4,6},{5,7},{6,4},{7,5},{8,10},{9,11},{10,... | collective-permute-start | bytes 3538952 | tf_op jit(solution)/shard_map/ppermute | solution.py:309
  499.5 56.9 %collective-permute-start.61 = (bf16[4,192,768]{2,1,0:T(8,128)(2,1)S(1)}, bf16[4,192,768]{2,1,0:T(8,128)(2,1)S(1)}, u32[]{:S(2)}, u32[]{:S(2)}) collective-permute-start(bf16[4,192,768]{2,1,0:T(8,128)(2,1)S(1)} %dynamic-slice_bitcast_fusion.3), channel_id=1, source_target_pairs={{0,4},{1,5},{2,6},{3,7},{4,0},{5,1},{6,2},{7,3},{8,12},{9,13},{10,... | collective-permute-start | bytes 3538952 | tf_op jit(solution)/shard_map/ppermute | solution.py:309
  501.8 31.8 %collective-permute-start.46 = (bf16[8,72,384]{2,1,0:T(8,128)(2,1)S(1)}, bf16[8,72,384]{2,1,0:T(8,128)(2,1)S(1)}, u32[]{:S(2)}, u32[]{:S(2)}) collective-permute-start(bf16[8,72,384]{2,1,0:T(8,128)(2,1)S(1)} %dynamic-slice_bitcast_fusion.14), channel_id=1, source_target_pairs={{0,2},{1,3},{2,0},{3,1},{4,6},{5,7},{6,4},{7,5},{8,10},{9,11},{10,... | collective-permute-start | bytes 1327112 | tf_op jit(solution)/shard_map/ppermute | solution.py:309
  503.4 34.5 %collective-permute-start.51 = (bf16[4,144,384]{2,1,0:T(8,128)(2,1)S(1)}, bf16[4,144,384]{2,1,0:T(8,128)(2,1)S(1)}, u32[]{:S(2)}, u32[]{:S(2)}) collective-permute-start(bf16[4,144,384]{2,1,0:T(8,128)(2,1)S(1)} %dynamic-slice_bitcast_fusion.13), channel_id=1, source_target_pairs={{0,4},{1,5},{2,6},{3,7},{4,0},{5,1},{6,2},{7,3},{8,12},{9,13},{10,... | collective-permute-start | bytes 1327112 | tf_op jit(solution)/shard_map/ppermute | solution.py:309
  533.7 8.2 %collective-permute-start.47 = (bf16[4,72,384]{2,1,0:T(8,128)(2,1)S(1)}, bf16[4,72,384]{2,1,0:T(8,128)(2,1)S(1)}, u32[]{:S(2)}, u32[]{:S(2)}) collective-permute-start(bf16[4,72,384]{2,1,0:T(8,128)(2,1)S(1)} %dynamic-slice_bitcast_fusion.19), channel_id=1, source_target_pairs={{0,4},{1,5},{2,6},{3,7},{4,0},{5,1},{6,2},{7,3},{8,12},{9,13},{10,... | collective-permute-start | bytes 663560 | tf_op jit(solution)/shard_map/ppermute | solution.py:309
  553.3 11.8 %collective-permute-start.67 = (bf16[4,24,3072]{2,1,0:T(8,128)(2,1)S(1)}, bf16[4,24,3072]{2,1,0:T(8,128)(2,1)S(1)}, u32[]{:S(2)}, u32[]{:S(2)}) collective-permute-start(bf16[4,24,3072]{2,1,0:T(8,128)(2,1)S(1)} %dynamic-slice_bitcast_fusion.10), channel_id=1, source_target_pairs={{0,4},{1,5},{2,6},{3,7},{4,0},{5,1},{6,2},{7,3},{8,12},{9,13},{10,... | collective-permute-start | bytes 1769480 | tf_op jit(solution)/shard_map/ppermute | solution.py:309
  556.9 10.9 %collective-permute-start.62 = (bf16[4,96,768]{2,1,0:T(8,128)(2,1)S(1)}, bf16[4,96,768]{2,1,0:T(8,128)(2,1)S(1)}, u32[]{:S(2)}, u32[]{:S(2)}) collective-permute-start(bf16[4,96,768]{2,1,0:T(8,128)(2,1)S(1)} %dynamic-slice_bitcast_fusion.11), channel_id=1, source_target_pairs={{0,2},{1,3},{2,0},{3,1},{4,6},{5,7},{6,4},{7,5},{8,10},{9,11},{10,... | collective-permute-start | bytes 1769480 | tf_op jit(solution)/shard_map/ppermute | solution.py:309
  565.4 9.3 %collective-permute-start.68 = (bf16[2,24,3072]{2,1,0:T(8,128)(2,1)S(1)}, bf16[2,24,3072]{2,1,0:T(8,128)(2,1)S(1)}, u32[]{:S(2)}, u32[]{:S(2)}) collective-permute-start(bf16[2,24,3072]{2,1,0:T(8,128)(2,1)S(1)} %dynamic-slice_bitcast_fusion.15), channel_id=1, source_target_pairs={{0,8},{1,9},{2,10},{3,11},{4,12},{5,13},{6,14},{7,15},{8,0},{9,1},... | collective-permute-start | bytes 884744 | tf_op jit(solution)/shard_map/ppermute | solution.py:309
  567.9 13.1 %collective-permute-start.63 = (bf16[2,96,768]{2,1,0:T(8,128)(2,1)S(1)}, bf16[2,96,768]{2,1,0:T(8,128)(2,1)S(1)}, u32[]{:S(2)}, u32[]{:S(2)}) collective-permute-start(bf16[2,96,768]{2,1,0:T(8,128)(2,1)S(1)} %dynamic-slice_bitcast_fusion.16), channel_id=1, source_target_pairs={{0,8},{1,9},{2,10},{3,11},{4,12},{5,13},{6,14},{7,15},{8,0},{9,1},... | collective-permute-start | bytes 884744 | tf_op jit(solution)/shard_map/ppermute | solution.py:309
  581.1 6.9 %collective-permute-start.64 = (bf16[1,96,768]{2,1,0:T(8,128)(2,1)S(1)}, bf16[1,96,768]{2,1,0:T(8,128)(2,1)S(1)}, u32[]{:S(2)}, u32[]{:S(2)}) collective-permute-start(bf16[1,96,768]{2,1,0:T(8,128)(2,1)S(1)} %constant_dynamic-slice_fusion.1), channel_id=1, source_target_pairs={{0,16},{1,17},{2,18},{3,19},{4,20},{5,21},{6,22},{7,23},{8,24},{9,... | collective-permute-start | bytes 442376 | tf_op jit(solution)/shard_map/ppermute | solution.py:309
  (134 other events, 1340.7 us)

commit v3 on v2

--- a/solution.py
+++ b/solution.py
@@ -162,7 +162,7 @@
 
 def ff_kernel(x_ref,g_ref,wu_ref,wd_ref,bu_ref,down_ref,gsec_ref,dwu_ref,dwd_ref,dbu_ref,a_ref,gu_ref):
     f=pl.program_id(0); rows=x_ref.shape[0]; step=256 if rows%256==0 else rows
-    wu=wu_ref[...]; wd=wd_ref[...]
+    wu=wu_ref[...]; wd=wd_ref[0]
     total=jnp.zeros(dbu_ref.shape[1:],F32)
     for r in range(rows//step):
         at=pl.ds(r*step,step)
@@ -194,10 +194,10 @@
 GELU_B=0.044715
 
 def feed_forward(x,g,wu,wd,bu):
-    rows,width=x.shape; hid=wu.shape[0]; blk=512 if hid%512==0 else hid
+    rows,width=x.shape; hid=wu.shape[0]; blk=width
     n=hid//blk
     return pl.pallas_call(ff_kernel,grid=(n,),
-        in_specs=[whole((rows,width)),whole((rows,width)),pl.BlockSpec((blk,width),lambda f:(f,0)),pl.BlockSpec((width,blk),lambda f:(0,f)),pl.BlockSpec((1,1,blk),lambda f:(f,0,0))],
+        in_specs=[whole((rows,width)),whole((rows,width)),pl.BlockSpec((blk,width),lambda f:(f,0)),pl.BlockSpec((1,width,blk),lambda f:(f,0,0)),pl.BlockSpec((1,1,blk),lambda f:(f,0,0))],
         out_specs=[whole((rows,width)),whole((rows,width)),pl.BlockSpec((blk,width),lambda f:(f,0)),pl.BlockSpec((width,blk),lambda f:(0,f)),pl.BlockSpec((1,1,blk),lambda f:(f,0,0))],
         out_shape=[jax.ShapeDtypeStruct((rows,width),F32),jax.ShapeDtypeStruct((rows,width),F32),jax.ShapeDtypeStruct((hid,width),BF),jax.ShapeDtypeStruct((width,hid),BF),jax.ShapeDtypeStruct((n,1,blk),F32)],
         scratch_shapes=[pltpu.VMEM((rows,blk),BF),pltpu.VMEM((rows,blk),BF)],
@@ -313,12 +313,124 @@
     return (me >> bit) & 1
 
 
-def gather_shards(value, me, count, order):
-    held = value
-    for bit in order[:-1]:
-        held = jnp.concatenate([held, swap_bit(held, me, bit, count)], axis=0)
-    other = swap_bit(held, me, order[-1], count)
-    return place_shards(held, other, me, count, order)
+class Gather:
+    flight = None
+
+    def __init__(self, value, me, count, order):
+        self.held, self.me, self.count, self.order = value, me, count, list(order)
+        self.at = 0
+
+    def send(self):
+        self.flight = [swap_bit(self.held, self.me, self.order[self.at], self.count)]
+
+    def receive(self, got):
+        self.at += 1
+        if self.at < len(self.order):
+            self.held = jnp.concatenate([self.held, got[0]], axis=0)
+        else:
+            self.held = place_shards(self.held, got[0], self.me, self.count, self.order)
+
+    @property
+    def open(self):
+        return self.at < len(self.order)
+
+
+class Scatter:
+    flight = None
+
+    def __init__(self, value, me, count, order, keep):
+        self.value, self.me, self.count, self.order, self.keep = value, me, count, list(order), keep
+        self.rows, self.columns = value.shape[1:]
+        self.left = list(range(len(self.order)))
+        self.at = 0
+
+    def send(self):
+        bit = self.order[self.at]
+        low = 1 << sum(1 for b in self.left if b < bit)
+        cut = self.value.reshape(-1, 2, low * self.rows, self.columns)
+        mine = bit_of(self.me, bit)
+        self.mine = lax.dynamic_index_in_dim(cut, mine, 1, keepdims=False)
+        given = lax.dynamic_index_in_dim(cut, 1 - mine, 1, keepdims=False)
+        self.flight = [swap_bit(given, self.me, bit, self.count)]
+        self.left.remove(bit)
+
+    def receive(self, got):
+        self.at += 1
+        self.value = self.mine.astype(F32) + got[0].astype(F32)
+        if self.open:
+            self.value = self.value.astype(self.keep)
+        else:
+            self.value = self.value.reshape(self.rows, self.columns)
+
+    @property
+    def open(self):
+        return self.at < len(self.order)
+
+
+class Swap:
+    flight = None
+
+    def __init__(self, value, me, count, bit):
+        self.value, self.me, self.count, self.bit = value, me, count, bit
+        self.open = True
+
+    def send(self):
+        self.flight = [swap_bit(self.value, self.me, self.bit, self.count)]
+
+    def receive(self, got):
+        self.value = got[0]
+        self.open = False
+
+
+class Total:
+    flight = None
+
+    def __init__(self, value, me, count):
+        self.value, self.me, self.count = value, me, count
+        bits = list(range(count.bit_length() - 1))
+        self.groups = [bits[i : i + 2] for i in range(0, len(bits), 2)]
+        self.at = 0
+
+    def send(self):
+        group = self.groups[self.at]
+        masks = [sum(1 << b for j, b in enumerate(group) if (m >> j) & 1) for m in range(1, 1 << len(group))]
+        self.flight = [
+            lax.ppermute(self.value, AXES, [(i, i ^ m) for i in range(self.count)]) for m in masks
+        ]
+
+    def receive(self, got):
+        self.at += 1
+        for v in got:
+            self.value = self.value + v
+
+    @property
+    def open(self):
+        return self.at < len(self.groups)
+
+
+def send(*chains):
+    for c in chains:
+        if c.open:
+            c.send()
+
+
+def meet(state, *chains):
+    chains = [c for c in chains if c.flight]
+    sizes = [len(c.flight) for c in chains]
+    tied = lax.optimization_barrier(tuple(state) + tuple(v for c in chains for v in c.flight))
+    at = len(state)
+    for c, n in zip(chains, sizes):
+        c.receive(tied[at : at + n])
+        c.flight = None
+        at += n
+    return tied[: len(state)]
+
+
+def drain(*chains):
+    meet((), *chains)
+    while any(c.open for c in chains):
+        send(*chains)
+        meet((), *chains)
 
 
 def place_shards(near, other, me, count, order):
@@ -347,27 +459,6 @@
         near.reshape((half, rows) + near.shape[1:]),
         other.reshape((half, rows) + near.shape[1:]),
     )
-
-
-def scatter_sum(value, me, count, order, keep):
-    rows, columns = value.shape[1:]
-    left = list(range(count.bit_length() - 1))
-    for place, bit in enumerate(order):
-        low = 1 << sum(1 for b in left if b < bit)
-        cut = value.reshape(-1, 2, low * rows, columns)
-        mine = lax.dynamic_index_in_dim(cut, bit_of(me, bit), 1, keepdims=False)
-        given = lax.dynamic_index_in_dim(cut, 1 - bit_of(me, bit), 1, keepdims=False)
-        value = mine.astype(F32) + swap_bit(given, me, bit, count).astype(F32)
-        if place < len(order) - 1:
-            value = value.astype(keep)
-        left.remove(bit)
-    return value.reshape(rows, columns)
-
-
-def sum_everywhere(value, me, count):
-    for bit in range(count.bit_length() - 1):
-        value = value + swap_bit(value, me, bit, count)
-    return value
 
 
 def orders_of(count):
@@ -462,23 +553,91 @@
         brief_filter_offset,
         brief_filter_coefficients,
         expand_offset,
-        filter_final_coefficients,
-    )
+    )
+    middle = width // 2
+    far = half.bit_length() - 1
+    intake_shard = intake_coefficients.T
+    front = Gather(intake_shard[:, :middle], me, count, down)
+    rear = Gather(intake_shard[:, middle:], me, count, back)
+    final = Gather(filter_final_coefficients.T.astype(F32), me, count, down)
+    trade = Swap(
+        lax.dynamic_index_in_dim(block_input, 1 - side, 0, keepdims=False), me, count, far
+    )
+    features = jnp.asarray(position_features(length, filter_entry_coefficients.shape[0]))
+    send(front, rear, final)
+    later = jnp.concatenate(
+        [expand_coefficients.T]
+        + [
+            contract_coefficients[q * width : (q + 1) * width].T
+            for q in range(contract_coefficients.shape[0] // width)
+        ]
+        + [mixer_output_coefficients.T],
+        axis=0,
+    )
+    later = lax.all_gather(later, AXES, axis=0, tiled=False)
+    frequency = periodic_frequency
+
+    def angle(values, weights, offset):
+        return product(values, weights) + offset
+
+    p1 = angle(features, filter_entry_coefficients, filter_entry_offset)
+    m1 = jnp.sin(frequency * p1)
+    (m1,) = meet((m1,), final)
+    send(final, trade)
+    p2 = angle(m1, filter_second_coefficients, filter_second_offset)
+    m2 = jnp.sin(frequency * p2)
+    (m2,) = meet((m2,), final, front, rear)
+    send(front, rear, final)
+    p3 = angle(m2, filter_third_coefficients, filter_third_offset)
+    hidden = jnp.sin(frequency * p3)
+    (hidden,) = meet((hidden,), final)
+    send(final)
     pack = jnp.concatenate([v.reshape(-1) for v in vectors])
-    pad = -pack.size % 1024
+    used = pack.size
+    pad = -used % 1024
     pack = jnp.concatenate([pack, jnp.zeros((pad,), pack.dtype)]).reshape(8, -1).astype(F32)
-    pack_full = gather_shards(pack, me, count, down).reshape(count, -1)
+    (pack,) = meet((pack,), final, front, rear)
+    bundle = Gather(pack, me, count, down)
+    send(front, rear, final, bundle)
+    shaping = modulation(length, width, chan_start, channels)
+    (shaping,) = meet((shaping,), final, bundle)
+    drain(final)
+    columns = lax.dynamic_slice_in_dim(final.held.reshape(width, -1), chan_start, channels, 0)
+    send(bundle)
+    filter_kernel = (
+        lax.dot_general(
+            hidden,
+            columns,
+            (((1,), (1,)), ((), ())),
+            precision=lax.Precision.HIGHEST,
+            preferred_element_type=F32,
+        )
+        * shaping
+    )
+    (filter_kernel,) = meet((filter_kernel,), front, rear, bundle)
+    send(front, rear, bundle)
+    kernel_spec = spectrum(filter_kernel, tables)
+    (kernel_spec,) = meet((kernel_spec,), bundle, trade)
+    send(bundle)
+    own_rows = lax.dynamic_index_in_dim(block_input, side, 0, keepdims=False)
+    tokens_low = jnp.concatenate([own_rows, trade.value], axis=0)
+    (tokens_low,) = meet((tokens_low,), bundle, front, rear)
+    send(front, rear, bundle)
+    tokens = tokens_low.astype(F32)
+    unit_one, rstd_one = normalise(tokens)
+    unit_one, rstd_one = meet((unit_one, rstd_one), bundle, front, rear)
+    drain(bundle, front, rear)
+    pack_full = bundle.held.reshape(count, -1)
     fields = []
     at = 0
     for v in vectors:
         part = pack_full[:, at : at + v.size]
         at += v.size
         if v.ndim == 1:
-            fields.append(part.reshape(-1).astype(F32))
+            fields.append(part.reshape(-1))
         else:
-            rows = v.shape[0]
             fields.append(
-                part.reshape(count, rows, -1).transpose(1, 0, 2).reshape(rows, -1).astype(F32)
+                part.reshape(count, v.shape[0], -1).transpose(1, 0, 2).reshape(v.shape[0], -1)
             )
     (
         gain_one,
@@ -492,58 +651,14 @@
         conv_bias,
         conv_taps,
         up_bias,
-        filter_final,
     ) = fields
-
-    intake_shard = intake_coefficients.T
-    middle = width // 2
     intake_t = jnp.concatenate(
-        [
-            gather_shards(intake_shard[:, :middle], me, count, down).reshape(-1, middle),
-            gather_shards(intake_shard[:, middle:], me, count, back).reshape(-1, middle),
-        ],
-        axis=1,
-    )
-
-    far = half.bit_length() - 1
-    own_rows = lax.dynamic_index_in_dim(block_input, side, 0, keepdims=False)
-    far_rows = swap_bit(
-        lax.dynamic_index_in_dim(block_input, 1 - side, 0, keepdims=False), me, far, count
-    )
-    tokens_low = jnp.concatenate([own_rows, far_rows], axis=0)
-
-    intake_t, mix_own, up_own, down_own = lax.optimization_barrier(
-        (
-            intake_t,
-            mixer_output_coefficients.T,
-            expand_coefficients.T,
-            contract_coefficients.T,
-        )
-    )
-    mix_t = gather_shards(mix_own, me, count, down).reshape(-1, width)
-    up_t = gather_shards(up_own, me, count, back).reshape(-1, width)
-    down_t = gather_shards(down_own, me, count, down).reshape(width, -1)
-
-    own_adj = lax.dynamic_index_in_dim(output_adjoint, side, 0, keepdims=False)
-    far_adj = swap_bit(
-        lax.dynamic_index_in_dim(output_adjoint, 1 - side, 0, keepdims=False), me, far, count
-    )
-    adjoint = jnp.concatenate([own_adj, far_adj], axis=0)
-
-    features = jnp.asarray(position_features(length, filter_entry_coefficients.shape[0]))
-    net = (
-        filter_entry_coefficients,
-        filter_entry_offset,
-        filter_second_coefficients,
-        filter_second_offset,
-        filter_third_coefficients,
-        filter_third_offset,
-        periodic_frequency,
-    )
-    hidden, filter_pull = jax.vjp(lambda *w: filter_hidden(features, *w), *net)
-    shaping = modulation(length, width, chan_start, channels)
-    columns = lax.dynamic_slice_in_dim(filter_final, chan_start, channels, 1)
-    kernel_spec = spectrum(product(hidden, columns) * shaping, tables)
+        [front.held.reshape(-1, middle), rear.held.reshape(-1, middle)], axis=1
+    )
+    trade_adj = Swap(
+        lax.dynamic_index_in_dim(output_adjoint, 1 - side, 0, keepdims=False), me, count, far
+    )
+    send(trade_adj)
 
     own_base = seq_index * local
     far_base = ((1 - side) * half + rank) * local
@@ -552,8 +667,6 @@
     ).astype(jnp.int32)
     span = lax.dynamic_index_in_dim(slot_spans, side, 0, keepdims=False)
     row_mask = ((places >= span[0]) & (places < span[0] + span[1])).astype(F32)[:, None]
-    tokens = tokens_low.astype(F32)
-    unit_one, rstd_one = normalise(tokens)
     normed_low = (unit_one * gain_one + shift_one).astype(BF)
     projected = row_mask * (dot_nt(normed_low, intake_t) + intake_bias)
     blocks = projected.reshape(2, local, -1)
@@ -627,6 +740,20 @@
     joined = carried + skip_gain * signal_wide
     joined_low = joined.astype(BF)
     gated_mix = (joined * outer_gate).astype(BF)
+    (gated_mix,) = meet((gated_mix,), trade_adj)
+    own_adj = lax.dynamic_index_in_dim(output_adjoint, side, 0, keepdims=False)
+    adjoint = jnp.concatenate([own_adj, trade_adj.value], axis=0)
+    ff_rows = expand_coefficients.shape[1]
+    mix_rows = mixer_output_coefficients.shape[1]
+    up_t = later[:, :ff_rows].reshape(-1, width)
+    mix_t = later[:, later.shape[1] - mix_rows :].reshape(-1, width)
+    folds = contract_coefficients.shape[0] // width
+    down_t = (
+        later[:, ff_rows : later.shape[1] - mix_rows]
+        .reshape(count, folds, -1, width)
+        .transpose(1, 0, 2, 3)
+        .reshape(folds, width, width)
+    )
     residual = tokens + dot_nt(gated_mix, mix_t) + mix_bias
     unit_two, rstd_two = normalise(residual)
     second_low = (unit_two * gain_two + shift_two).astype(BF)
@@ -638,13 +765,9 @@
     up_bias_grad = up_bias_grad.reshape(-1)
     output = (row_mask * (residual + down_proj + down_bias)).astype(BF)
 
-    def to_home(value):
-        far_part = swap_bit(value[local:], me, far, count)
-        near = value[:local]
-        return jnp.where(side == 0, jnp.stack([near, far_part]), jnp.stack([far_part, near]))
-
-    output_home = to_home(output)
-
+    up_sum = Scatter(up_grad.reshape(count, -1, width), me, count, across, BF)
+    down_sum = Scatter(down_grad.reshape(count, -1, down_grad.shape[1]), me, count, up, BF)
+    send(up_sum, down_sum)
     down_bias_grad = jnp.sum(grad_out, axis=0)
     gain_two_grad = jnp.sum(grad_second * unit_two, axis=0)
     shift_two_grad = jnp.sum(grad_second, axis=0)
@@ -652,17 +775,19 @@
     mix_bias_grad = jnp.sum(grad_residual, axis=0)
     resid_low = grad_residual.astype(BF)
     mix_grad = dot_tn(resid_low, gated_mix).astype(BF)
-    down_shard = scatter_sum(down_grad.reshape(count, -1, down_grad.shape[1]), me, count, up, BF)
-    up_shard = scatter_sum(up_grad.reshape(count, -1, width), me, count, across, BF)
-    mix_shard = scatter_sum(mix_grad.reshape(count, -1, width), me, count, up, BF)
-
+    mix_sum = Scatter(mix_grad.reshape(count, -1, width), me, count, up, BF)
     grad_gated = dot_nn(resid_low, mix_t)
     grad_joined = grad_gated * outer_gate
     grad_joined_low = grad_joined.astype(BF)
     skip_grad = jnp.sum(grad_joined * signal_wide, axis=0)
+    (grad_joined_low,) = meet((grad_joined_low,), up_sum, down_sum)
+    send(mix_sum, up_sum, down_sum)
     conv_back_cols, kernel_grad = long_back(
         to_channels(grad_joined_low), kernel_spec, sig_spec, tables
     )
+    conv_back_cols, kernel_grad = meet((conv_back_cols, kernel_grad), mix_sum, up_sum, down_sum)
+    send(mix_sum, up_sum, down_sum)
+    trade_out = Swap(output[local:], me, count, far)
     conv_back_low = to_rows(conv_back_cols.astype(BF))
     conv_back = conv_back_low.astype(F32)
     first = blocks_of(grad_gated)[:, :2]
@@ -701,28 +826,37 @@
     taps_grad = sums[1:4]
     intake_bias_grad = sums[4]
     projected_low = grad_projected.reshape(rows, -1)
+    (projected_low,) = meet((projected_low,), mix_sum, up_sum, down_sum)
+    send(mix_sum, up_sum, down_sum)
     intake_grad = dot_tn(projected_low, normed_low).astype(BF).reshape(count, -1, width)
-    intake_shard_grad = jnp.concatenate(
-        [
-            scatter_sum(intake_grad[:, :, :middle], me, count, up, BF),
-            scatter_sum(intake_grad[:, :, middle:], me, count, across, BF),
-        ],
-        axis=1,
-    )
+    (intake_grad,) = meet((intake_grad,), mix_sum, up_sum, down_sum)
+    front_sum = Scatter(intake_grad[:, :, :middle], me, count, up, BF)
+    rear_sum = Scatter(intake_grad[:, :, middle:], me, count, across, BF)
+    send(mix_sum, up_sum, down_sum, front_sum, rear_sum)
     grad_normed = dot_nn(projected_low, intake_t)
     gain_one_grad = jnp.sum(grad_normed * unit_one, axis=0)
     shift_one_grad = jnp.sum(grad_normed, axis=0)
     tokens_grad = (
         grad_residual + normalise_back(unit_one, rstd_one, grad_normed * gain_one)
     ).astype(BF)
-    tokens_home = to_home(tokens_grad)
+    (tokens_grad,) = meet((tokens_grad,), mix_sum, up_sum, down_sum, front_sum, rear_sum)
+    trade_tokens = Swap(tokens_grad[local:], me, count, far)
+    send(mix_sum, front_sum, rear_sum, trade_out)
 
     shaped_grad = kernel_grad * shaping
-    column_grad = product(hidden.T, shaped_grad)
+    (shaped_grad,) = meet((shaped_grad,), front_sum, rear_sum, mix_sum)
+    send(front_sum, rear_sum, trade_tokens)
+    column_grad = lax.dot_general(
+        shaped_grad,
+        hidden,
+        (((0,), (0,)), ((), ())),
+        precision=lax.Precision.HIGHEST,
+        preferred_element_type=F32,
+    )
+    hidden_grad = product(shaped_grad, columns)
     filter_full = lax.dynamic_update_slice_in_dim(
-        jnp.zeros((hidden.shape[1], width), F32), column_grad, chan_start, 1
-    )
-    net_grads = filter_pull(product(shaped_grad, columns.T))
+        jnp.zeros((width, hidden.shape[1]), F32), column_grad, chan_start, 0
+    )
 
     vector_grads = (
         gain_one_grad,
@@ -736,7 +870,6 @@
         conv_bias_grad,
         taps_grad,
         up_bias_grad,
-        filter_full,
     )
     pieces = []
     for g in vector_grads:
@@ -747,20 +880,58 @@
                 g.reshape(g.shape[0], count, -1).transpose(1, 0, 2).reshape(count, -1)
             )
     packed = jnp.concatenate(pieces + [jnp.zeros((count, pad), F32)], axis=1)
-    summed = scatter_sum(packed.reshape(count, 8, -1), me, count, up, F32).reshape(-1)
+    bundle_sum = Scatter(packed.reshape(count, 8, -1), me, count, up, F32)
+    final_sum = Scatter(filter_full.reshape(count, -1, hidden.shape[1]), me, count, up, F32)
+    send(bundle_sum, final_sum)
+
+    def layer_back(grad, p, inputs, weights):
+        turned = grad * jnp.cos(frequency * p)
+        grad_p = turned * frequency
+        rate = jnp.sum(turned * p, axis=0)
+        return product(inputs.T, grad_p), jnp.sum(grad_p, axis=0), rate, product(grad_p, weights.T)
+
+    third, third_bias, rate_3, grad_2 = layer_back(
+        hidden_grad, p3, m2, filter_third_coefficients
+    )
+    (grad_2,) = meet((grad_2,), front_sum, rear_sum, bundle_sum, final_sum, trade_out)
+    send(front_sum, rear_sum, bundle_sum, final_sum)
+    second, second_bias, rate_2, grad_1 = layer_back(grad_2, p2, m1, filter_second_coefficients)
+    (grad_1,) = meet((grad_1,), front_sum, rear_sum, bundle_sum, final_sum)
+    send(front_sum, rear_sum, bundle_sum, final_sum)
+    entry, entry_bias, rate_1, _ = layer_back(
+        grad_1, p1, features, filter_entry_coefficients
+    )
+    net_grads = (
+        entry,
+        entry_bias,
+        second,
+        second_bias,
+        third,
+        third_bias,
+        rate_1 + rate_2 + rate_3,
+    )
+    net_flat = jnp.concatenate([g.reshape(-1) for g in net_grads])
+    net_sum = Total(net_flat, me, count)
+    meet((net_flat,), front_sum, rear_sum, bundle_sum, final_sum, trade_tokens)
+    drain(bundle_sum, final_sum, net_sum, front_sum, rear_sum, mix_sum, up_sum, down_sum)
+    summed = bundle_sum.value.reshape(-1)
     small = []
     at = 0
     for v in vectors:
         small.append(summed[at : at + v.size].reshape(v.shape))
         at += v.size
-    net_flat = sum_everywhere(
-        jnp.concatenate([g.reshape(-1) for g in net_grads]), me, count
-    )
     net_out = []
     at = 0
     for g in net_grads:
-        net_out.append(net_flat[at : at + g.size].reshape(g.shape))
+        net_out.append(net_sum.value[at : at + g.size].reshape(g.shape))
         at += g.size
+    intake_shard_grad = jnp.concatenate([front_sum.value, rear_sum.value], axis=1)
+
+    def at_home(near, far_part):
+        return jnp.where(side == 0, jnp.stack([near, far_part]), jnp.stack([far_part, near]))
+
+    output_home = at_home(output[:local], trade_out.value)
+    tokens_home = at_home(tokens_grad[:local], trade_tokens.value)
     return (
         output_home,
         tokens_home,
@@ -771,14 +942,14 @@
         small[9],
         small[8],
         small[2],
-        small[11],
-        mix_shard.T,
+        final_sum.value.T,
+        mix_sum.value.T,
         small[3],
         small[4],
         small[5],
-        up_shard.T,
+        up_sum.value.T,
         small[10],
-        down_shard.T,
+        down_sum.value.T,
         small[6],
     ) + tuple(net_out)
 

time: 599 us -> 515 us (0.86)
  waiting for transfers between devices: 120 us -> 60.3 us
  local copies, waits for them, and re-layouts: 97.7 us -> 77 us
  other arithmetic: 101 us -> 118 us
  Pallas kernels: 122 us -> 106 us
  between operations: 4.65 us -> 18.2 us
  matrix products: 70.2 us -> 62.3 us
    ppermute x69 -> x59, waiting for transfers between devices: 120 us -> 58.2 us  [swap_bit(): return lax.ppermute(value, AXES, [(i, i ^ 1 << bit) for i in range(count)])]
    convert_element_type x20 -> x24, other arithmetic: 11.3 us -> 26.1 us  [the longest x20 22.4 us: receive(): self.value = self.value.astype(self.keep)]
    ppermute x69 -> x59, starting transfers between devices: 72.5 us -> 58.4 us  [swap_bit(): return lax.ppermute(value, AXES, [(i, i ^ 1 << bit) for i in range(count)])]
    dot_general x11 -> x9, matrix products: 41.7 us -> 29.2 us  [product(): jnp.dot(left, right, precision=lax.Precision.HIGHEST, preferred_element_t...]
    pallas_call x6 -> x4, Pallas kernels: 15 us -> 2.82 us  [place_shards(): pl.pallas_call(kernel, in_specs=[SM, vmem, vmem], out_specs=vmem, out_sha...]
    slice x8 -> x9, local copies, waits for them, and re-layouts: 3.71 us -> 14.8 us  [the longest x1 8.37 us: per_device(): later[:, ff_rows:later.shape[1] - mix_rows].reshape(count, folds, -1, width)]
    dot_general x0 -> x2, matrix products: none -> 10.3 us  [the longest x1 5.29 us: per_device(): lax.dot_general(hidden, columns, (((1,), (1,)), ((), ())), precision=lax....]
    ppermute x0 -> x7, starting transfers between devices: none -> 7.61 us  [send(): lax.ppermute(self.value, AXES, [(i, i ^ m) for i in range(self.count)])]
  transfers between devices with their start and end apart: 75 -> 73, of which waited for: 29 -> 18; matrix products, arithmetic and copies ran while one was open for 41% -> 36% of each run, Pallas kernels for 12% -> 13%
where the time goes in v3:
time: 515 us; the launch traced here: 509 us
  other arithmetic  118 us (23%)
  Pallas kernels  106 us (21%)
  local copies, waits for them, and re-layouts  77 us (15%)
  starting transfers between devices  67.4 us (13%)
  matrix products  62.3 us (12%)
  waiting for transfers between devices  60.3 us (12%)
  between operations  18.2 us (4%)
    ppermute x59, starting transfers between devices, swap_bit(): return lax.ppermute(value, AXES, [(i, i ^ 1 << bit) for i in range(count)])  58.4 us
    ppermute x59, waiting for transfers between devices, swap_bit(): return lax.ppermute(value, AXES, [(i, i ^ 1 << bit) for i in range(count)])  58.2 us
    pallas_call x1, Pallas kernels, feed_forward(): pl.pallas_call(ff_kernel, grid=(n,), in_specs=[whole((rows, width)), whol...  39.1 us
    dot_general x9, matrix products, product(): jnp.dot(left, right, precision=lax.Precision.HIGHEST, preferred_element_t...  29.2 us
    convert_element_type x20, other arithmetic, receive(): self.value = self.value.astype(self.keep)  22.4 us
    pallas_call x1, Pallas kernels, long_back(): pl.pallas_call(back_kernel, grid=(RADIX // 4,), in_specs=[SM, whole((8, i...  22.2 us
    unnamed x207, local copies, waits for them, and re-layouts  20.6 us
    pallas_call x1, Pallas kernels, long_conv(): pl.pallas_call(conv_kernel, grid=(RADIX // 4,), in_specs=[SM, whole((8, i...  17.5 us
  transfers between devices with their start and end apart: 73, of which 18 were waited for; matrix products, arithmetic and copies ran while one was open for 36% of the time, Pallas kernels for 13%

profile of v3, /device:TPU:0, one launch (start us, length us, event | category | flops | bytes accessed | tf_op | source)
XLA Modules:
  0.0 509.0 jit_solution(14033418590089424502)
XLA Ops:
  13.7 4.0 collective-permute-start
  17.8 2.4 dynamic-slice_bitcast_fusion.9
  22.0 2.6 collective-permute-start.2
  26.9 4.9 multiply_sine_fusion.2
  37.5 4.2 multiply_sine_fusion.1
  46.9 3.9 multiply_sine_fusion
  52.2 6.1 %collective-permute-done.5 = f32[192,64]{1,0:T(8,128)S(1)} collective-permute-done((f32[192,64]{1,0:T(8,128)S(1)}, f32[192,64]{1,0:T(8,128)S(1)}, u32[]{:S(2)}, u32[]{:S(2)}) %collective-permute-start.5) | collective-permute-done | bytes 49184 | tf_op jit(solution)/shard_map/ppermute | solution.py:309
  60.1 3.4 collective-permute-done.9
  63.9 5.3 %convolution_multiply_fusion = f32[2048,384]{1,0:T(8,128)} fusion(f32[2048,384]{1,0:T(8,128)S(1)} %copy-done.8, f32[2048,64]{0,1:T(8,128)S(1)} %get-tuple-element.125, f32[768,64]{1,0:T(8,128)S(1)} %bitcast.323, s32[]{:T(128)S(6)} %select_n.329), kind=kOutput, calls=%fused_computation.44 | convolution fusion | flops 604766208 | bytes 7012356 | tf_op jit(solution)/shard_map/dot_general | solution.py:608
  72.2 9.5 %shard_map.478.k_ref = f32[4,2,512,384]{3,2,1,0:T(8,128)} custom-call(f32[4,16]{1,0:T(4,128)S(1)} %copy-done.5, f32[8,256,384]{2,1,0:T(8,128)} %bitcast.350, bf16[4,2,512,512]{3,2,1,0:T(8,128)(2,1)} %constant.309.clone.f_ref), custom_call_target="tpu_custom_call" | custom-call | tf_op jit(solution)/shard_map/pallas_call | solution.py:137
  84.6 8.1 %collective-permute-done.15 = f32[64,128]{1,0:T(8,128)S(1)} collective-permute-done((f32[64,128]{1,0:T(8,128)S(1)}, f32[64,128]{1,0:T(8,128)S(1)}, u32[]{:S(2)}, u32[]{:S(2)}) %collective-permute-start.15) | collective-permute-done | bytes 32800 | tf_op jit(solution)/shard_map/ppermute | solution.py:309
  102.4 5.4 %add_multiply_fusion = f32[1024,2304]{1,0:T(8,128)S(1)} fusion(f32[2304]{0:T(1024)S(1)} %add.556, f32[1024]{0:T(1024)S(1)} %copy-done.59, bf16[2304,384]{1,0:T(8,128)(2,1)} %bitcast.398, bf16[2304,384]{1,0:T(8,128)(2,1)S(1)} %bitcast.396, f32[1024,768]{1,0:T(8,128)S(1)} %copy-done.15, f32[768]{0:T(1024)S(1)} %add.553, f32[768]{0:T(1024)S(1)} %mul.352), kind=kOutput, calls=%fused_computation.9 | convolution fusion | flops 3638034432 | bytes 16141312 | tf_op jit(solution)/shard_map/dot_general | solution.py:488
  107.8 3.6 copy-done.7
  113.1 12.1 %fusion = (f32[2,512,2304]{2,1,0:T(8,128)S(1)}, f32[2,512,2304]{2,1,0:T(8,128)}) fusion(f32[2,2,2304]{2,1,0:T(2,128)S(1)} %get-tuple-element.245, f32[2,512,2304]{2,1,0:T(8,128)} %bitcast.339), kind=kLoop, calls=%fused_computation.2 | loop fusion | flops 4718592 | bytes 28348416 | tf_op jit(solution)/shard_map/concatenate | solution.py:686
  125.6 5.7 %fusion.2 = f32[1024,2304]{1,0:T(8,128)S(1)} fusion(f32[2,512,2304]{2,1,0:T(8,128)} %get-tuple-element.251, f32[2,512,2304]{2,1,0:T(8,128)S(1)} %get-tuple-element.250, f32[1024,2304]{1,0:T(8,128)S(1)} %bitcast.342, f32[2304]{0:T(1024)S(1)} %mul.360, f32[2304]{0:T(1024)S(1)} %mul.357, f32[2304]{0:T(1024)S(1)} %mul.349, f32[2304]{0:T(1024)S(1)} %add.551), kind=kLoop, calls=%fused_computation.6 | loop fusion | flops 14155776 | bytes 37785600 | tf_op jit(solution)/shard_map/add | solution.py:693
  131.4 3.6 copy-done.6
  140.3 6.3 %convert_element_type.424 = bf16[2,512,2304]{2,1,0:T(8,128)(2,1)} convert(f32[2,512,2304]{2,1,0:T(8,128)} %bitcast.340) | non-fusion elementwise | flops 2359296 | bytes 14155776 | tf_op jit(solution)/shard_map/convert_element_type | solution.py:735
  149.0 17.5 %shard_map.482 = (bf16[4,2,512,384]{3,2,1,0:T(8,128)(2,1)}, f32[8,256,384]{2,1,0:T(8,128)}) custom-call(f32[4,16]{1,0:T(4,128)S(1)} %copy-done.5, bf16[8,256,384]{2,1,0:T(8,128)(2,1)S(1)} %bitcast.322, f32[4,2,512,384]{3,2,1,0:T(8,128)} %shard_map.478.k_ref, bf16[4,2,512,512]{3,2,1,0:T(8,128)(2,1)} %constant.309.clone.f_ref, ...), custom_call_target="tpu_custom_call" | custom-call | tf_op jit(solution)/shard_map/pallas_call | solution.py:146
  169.3 3.4 pad_maximum_fusion.1.p_ref
  175.3 2.6 fusion.13.g_ref
  179.3 8.4 %fusion.71 = (bf16[32,96,768]{2,1,0:T(8,128)(2,1)}, bf16[32,96,768]{2,1,0:T(8,128)(2,1)}) fusion(bf16[32,216,768]{2,1,0:T(8,128)(2,1)} %bitcast.352), kind=kLoop, calls=%fused_computation.317 | loop fusion | bytes 18874368 | tf_op jit(solution)/shard_map/slice | solution.py:752
  187.7 5.0 copy.111
  195.3 39.1 %shard_map.483 = (f32[1024,768]{1,0:T(8,128)}, f32[1024,768]{1,0:T(8,128)}, bf16[3072,768]{1,0:T(8,128)(2,1)}, bf16[768,3072]{1,0:T(8,128)(2,1)}, f32[4,1,768]{2,1,0:T(1,128)S(1)}) custom-call(bf16[1024,768]{1,0:T(8,128)(2,1)S(1)} %add_convert_fusion.1.x_ref, bf16[1024,768]{1,0:T(8,128)(2,1)} %fusion.13.g_ref, bf16[3072,768]{1,0:T(8,128)(2,1)} %bitcast.376, ...), custom_call_target="tpu_custom_call" | custom-call | flops 28991029248 | bytes 28311552 | tf_op jit(solution)/shard_map/pallas_call | solution.py:199
  234.4 3.1 multiply_reduce_fusion
  242.9 5.7 %fusion.69 = (f32[768]{0:T(1024)S(1)}, f32[1024,768]{1,0:T(8,128)S(1)}, bf16[1024,768]{1,0:T(8,128)(2,1)}, f32[768]{0:T(1024)S(1)}) fusion(f32[1024]{0:T(1024)S(1)} %broadcast_multiply_fusion.2, f32[1024,768]{1,0:T(8,128)S(1)} %get-tuple-element.333, f32[1024]{0:T(1024)S(1)} %broadcast_multiply_fusion.4, f32[1024]{0:T(1024)S(1)} %broadcast_multiply_fusion.3, ...), kind=kLoop, calls=%fused_computation.315 | loop fusion | flops 14940672 | bytes 15761408 | tf_op jit(solution)/shard_map/reduce_sum | solution.py:775
  254.6 3.6 fusion.10
  258.2 3.1 fusion.4
  261.3 3.2 fusion.5
  269.3 2.6 slice_bitcast_fusion
  273.7 22.2 %shard_map.484 = (f32[8,256,384]{2,1,0:T(8,128)}, f32[8,256,384]{2,1,0:T(8,128)}) custom-call(f32[4,16]{1,0:T(4,128)S(1)} %copy-done.5, bf16[8,256,384]{2,1,0:T(8,128)(2,1)S(1)} %bitcast.321, f32[4,2,512,384]{3,2,1,0:T(8,128)} %shard_map.478.k_ref, bf16[4,2,512,384]{3,2,1,0:T(8,128)(2,1)} %get-tuple-element.159.s_ref, ...), custom_call_target="tpu_custom_call" | custom-call | tf_op jit(solution)/shard_map/pallas_call | solution.py:156
  297.2 4.0 mul.388
  314.9 14.5 %shard_map.485 = (bf16[2,512,2304]{2,1,0:T(8,128)(2,1)}, f32[8,2304]{1,0:T(8,128)S(1)}) custom-call(bf16[2,528,2304]{2,1,0:T(8,128)(2,1)} %pad_maximum_fusion.1.p_ref, f32[2,512,768]{2,1,0:T(8,128)} %bitcast.349, bf16[2,512,768]{2,1,0:T(8,128)(2,1)} %bitcast.364, bf16[2,512,768]{2,1,0:T(8,128)(2,1)} %bitcast.365, bf16[2,512,768]{2,1,0:T(8,128)(2,1)} %bitcast.347, ...), custom_call_target="tpu_custom_call" | custom-call | tf_op jit(solution)/shard_map/pallas_call | solution.py:257
  329.5 7.4 %multiply_reduce_fusion.1 = (f32[768]{0:T(1024)S(1)}, f32[1024]{0:T(1024)S(1)}, f32[1024]{0:T(1024)S(1)}, f32[768]{0:T(1024)S(1)}, f32[1024,768]{1,0:T(8,128)S(1)}) fusion(f32[1024,768]{1,0:T(8,128)S(1)} %copy-done.16, f32[768]{0:T(1024)S(1)} %mul.352, bf16[1024,2304]{1,0:T(8,128)(2,1)} %bitcast.437, bf16[2304,384]{1,0:T(8,128)(2,1)} %bitcast.399, ...), kind=kOutput, calls=%fused_computation.29 | convolution fusion | flops 3636457984 | bytes 14566400 | tf_op jit(solution)/shard_map/dot_general | solution.py:492
  336.9 5.5 %convolution_convert_fusion = bf16[2304,768]{1,0:T(8,128)(2,1)} fusion(bf16[1024,2304]{1,0:T(8,128)(2,1)S(1)} %bitcast.438, f32[1024,768]{1,0:T(8,128)S(1)} %copy-done.16, f32[768]{0:T(1024)S(1)} %add.553, f32[768]{0:T(1024)S(1)} %mul.352), kind=kOutput, calls=%fused_computation.10 | convolution fusion | flops 3628007424 | bytes 11409408 | tf_op jit(solution)/shard_map/dot_general | solution.py:496
  353.3 5.1 collective-permute-done.38
  358.4 5.9 %collective-permute-done.37 = bf16[2,96,768]{2,1,0:T(8,128)(2,1)} collective-permute-done((bf16[2,96,768]{2,1,0:T(8,128)(2,1)}, bf16[2,96,768]{2,1,0:T(8,128)(2,1)}, u32[]{:S(2)}, u32[]{:S(2)}) %collective-permute-start.37) | collective-permute-done | bytes 294944 | tf_op jit(solution)/shard_map/ppermute | solution.py:309
  364.3 2.4 fusion.72
  375.3 3.0 collective-permute-done.39
  382.1 2.6 collective-permute-done.40
  391.5 15.4 %collective-permute-done.44 = bf16[8,72,384]{2,1,0:T(8,128)(2,1)S(1)} collective-permute-done((bf16[8,72,384]{2,1,0:T(8,128)(2,1)S(1)}, bf16[8,72,384]{2,1,0:T(8,128)(2,1)S(1)}, u32[]{:S(2)}, u32[]{:S(2)}) %collective-permute-start.44) | collective-permute-done | bytes 442400 | tf_op jit(solution)/shard_map/ppermute | solution.py:309
  407.2 5.1 convolution_dynamic-update-slice_fusion
  412.3 4.8 convolution_multiply_fusion.1
  429.1 3.0 fusion.34
  432.1 3.1 fusion.36
  446.8 3.3 maximum_select_fusion
  463.0 4.9 multiply_reduce_fusion.7
  467.9 3.2 fusion.32
  479.6 3.3 maximum_select_fusion.1
  (571 shorter events, 183.4 us)
Async XLA Ops:
  7.4 170.6 %all-gather.3.cloned.1.call-start = ((), (), s32[]{:S(2)}) async-start(), calls=%async_computation | async-start | bytes 10948608 | tf_op jit(solution)/shard_map/all_gather | solution.py:577
  13.7 21.5 %collective-permute-start = (f32[24,64]{1,0:T(8,128)S(1)}, f32[24,64]{1,0:T(8,128)}, u32[]{:S(2)}, u32[]{:S(2)}) collective-permute-start(f32[24,64]{1,0:T(8,128)S(1)} %convert_bitcast_fusion), channel_id=1, source_target_pairs={{0,16},{1,17},{2,18},{3,19},{4,20},{5,21},{6,22},{7,23},{8,24},{9,... | collective-permute-start | bytes 18440 | tf_op jit(solution)/shard_map/ppermute | solution.py:309
  20.1 61.6 %collective-permute-start.14 = (bf16[512,768]{1,0:T(8,128)(2,1)}, bf16[512,768]{1,0:T(8,128)(2,1)}, u32[]{:S(2)}, u32[]{:S(2)}) collective-permute-start(bf16[512,768]{1,0:T(8,128)(2,1)} %get-tuple-element.283), channel_id=1, source_target_pairs={{0,2},{1,3},{2,0},{3,1},{4,6},{5,7},{6,4},{7,5},{8,10},{9,11},{10,... | collective-permute-start | bytes 2359304 | tf_op jit(solution)/shard_map/ppermute | solution.py:309
  21.6 20.8 %collective-permute-start.3 = (bf16[72,384]{1,0:T(8,128)(2,1)S(1)}, bf16[72,384]{1,0:T(8,128)(2,1)S(1)}, u32[]{:S(2)}, u32[]{:S(2)}) collective-permute-start(bf16[72,384]{1,0:T(8,128)(2,1)S(1)} %get-tuple-element.303), channel_id=1, source_target_pairs={{0,16},{1,17},{2,18},{3,19},{4,20},{5,21},{6,22},{7,23},{8,24},{9,... | collective-permute-start | bytes 165896 | tf_op jit(solution)/shard_map/ppermute | solution.py:309
  22.0 20.4 %collective-permute-start.2 = (bf16[72,384]{1,0:T(8,128)(2,1)S(1)}, bf16[72,384]{1,0:T(8,128)(2,1)S(1)}, u32[]{:S(2)}, u32[]{:S(2)}) collective-permute-start(bf16[72,384]{1,0:T(8,128)(2,1)S(1)} %get-tuple-element.304), channel_id=1, source_target_pairs={{0,16},{1,17},{2,18},{3,19},{4,20},{5,21},{6,22},{7,23},{8,24},{9,... | collective-permute-start | bytes 165896 | tf_op jit(solution)/shard_map/ppermute | solution.py:309
  43.2 7.7 %collective-permute-start.4 = (f32[96,64]{1,0:T(8,128)S(1)}, f32[96,64]{1,0:T(8,128)S(1)}, u32[]{:S(2)}, u32[]{:S(2)}) collective-permute-start(f32[96,64]{1,0:T(8,128)S(1)} %pad_maximum_fusion.22), channel_id=1, source_target_pairs={{0,4},{1,5},{2,6},{3,7},{4,0},{5,1},{6,2},{7,3},{8,12},{9,13},{10,... | collective-permute-start | bytes 73736 | tf_op jit(solution)/shard_map/ppermute | solution.py:309
  44.7 13.6 %collective-permute-start.7 = (bf16[144,384]{1,0:T(8,128)(2,1)S(1)}, bf16[144,384]{1,0:T(8,128)(2,1)S(1)}, u32[]{:S(2)}, u32[]{:S(2)}) collective-permute-start(bf16[144,384]{1,0:T(8,128)(2,1)S(1)} %pad_maximum_fusion.20), channel_id=1, source_target_pairs={{0,8},{1,9},{2,10},{3,11},{4,12},{5,13},{6,14},{7,15},{8,0},{9,1},... | collective-permute-start | bytes 331784 | tf_op jit(solution)/shard_map/ppermute | solution.py:309
  45.5 13.4 %collective-permute-start.6 = (bf16[144,384]{1,0:T(8,128)(2,1)S(1)}, bf16[144,384]{1,0:T(8,128)(2,1)S(1)}, u32[]{:S(2)}, u32[]{:S(2)}) collective-permute-start(bf16[144,384]{1,0:T(8,128)(2,1)S(1)} %pad_maximum_fusion.19), channel_id=1, source_target_pairs={{0,8},{1,9},{2,10},{3,11},{4,12},{5,13},{6,14},{7,15},{8,0},{9,1},... | collective-permute-start | bytes 331784 | tf_op jit(solution)/shard_map/ppermute | solution.py:309
  59.1 10.0 %collective-permute-start.11 = (bf16[288,384]{1,0:T(8,128)(2,1)S(1)}, bf16[288,384]{1,0:T(8,128)(2,1)S(1)}, u32[]{:S(2)}, u32[]{:S(2)}) collective-permute-start(bf16[288,384]{1,0:T(8,128)(2,1)S(1)} %pad_maximum_fusion.18), channel_id=1, source_target_pairs={{0,2},{1,3},{2,0},{3,1},{4,6},{5,7},{6,4},{7,5},{8,10},{9,11},{10,... | collective-permute-start | bytes 663560 | tf_op jit(solution)/shard_map/ppermute | solution.py:309
  59.8 9.4 %collective-permute-start.10 = (bf16[288,384]{1,0:T(8,128)(2,1)S(1)}, bf16[288,384]{1,0:T(8,128)(2,1)S(1)}, u32[]{:S(2)}, u32[]{:S(2)}) collective-permute-start(bf16[288,384]{1,0:T(8,128)(2,1)S(1)} %pad_maximum_fusion.17), channel_id=1, source_target_pairs={{0,4},{1,5},{2,6},{3,7},{4,0},{5,1},{6,2},{7,3},{8,12},{9,13},{10,... | collective-permute-start | bytes 663560 | tf_op jit(solution)/shard_map/ppermute | solution.py:309
  69.2 12.5 %collective-permute-start.13 = (f32[32,128]{1,0:T(8,128)S(1)}, f32[32,128]{1,0:T(8,128)S(1)}, u32[]{:S(2)}, u32[]{:S(2)}) collective-permute-start(f32[32,128]{1,0:T(8,128)S(1)} %pad_maximum_fusion.26), channel_id=1, source_target_pairs={{0,4},{1,5},{2,6},{3,7},{4,0},{5,1},{6,2},{7,3},{8,12},{9,13},{10,... | collective-permute-start | bytes 49160 | tf_op jit(solution)/shard_map/ppermute | solution.py:309
  69.8 22.9 %collective-permute-start.17 = (bf16[576,384]{1,0:T(8,128)(2,1)S(1)}, bf16[576,384]{1,0:T(8,128)(2,1)S(1)}, u32[]{:S(2)}, u32[]{:S(2)}) collective-permute-start(bf16[576,384]{1,0:T(8,128)(2,1)S(1)} %pad_maximum_fusion.16), channel_id=1, source_target_pairs={{0,4},{1,5},{2,6},{3,7},{4,0},{5,1},{6,2},{7,3},{8,12},{9,13},{10,... | collective-permute-start | bytes 1327112 | tf_op jit(solution)/shard_map/ppermute | solution.py:309
  71.5 21.2 %collective-permute-start.16 = (bf16[576,384]{1,0:T(8,128)(2,1)S(1)}, bf16[576,384]{1,0:T(8,128)(2,1)S(1)}, u32[]{:S(2)}, u32[]{:S(2)}) collective-permute-start(bf16[576,384]{1,0:T(8,128)(2,1)S(1)} %pad_maximum_fusion.15), channel_id=1, source_target_pairs={{0,2},{1,3},{2,0},{3,1},{4,6},{5,7},{6,4},{7,5},{8,10},{9,11},{10,... | collective-permute-start | bytes 1327112 | tf_op jit(solution)/shard_map/ppermute | solution.py:309
  81.8 10.9 %collective-permute-start.15 = (f32[64,128]{1,0:T(8,128)S(1)}, f32[64,128]{1,0:T(8,128)S(1)}, u32[]{:S(2)}, u32[]{:S(2)}) collective-permute-start(f32[64,128]{1,0:T(8,128)S(1)} %pad_maximum_fusion.24), channel_id=1, source_target_pairs={{0,2},{1,3},{2,0},{3,1},{4,6},{5,7},{6,4},{7,5},{8,10},{9,11},{10,... | collective-permute-start | bytes 98312 | tf_op jit(solution)/shard_map/ppermute | solution.py:309
  136.2 10.9 %collective-permute-start.22 = (bf16[1024,384]{1,0:T(8,128)(2,1)}, bf16[1024,384]{1,0:T(8,128)(2,1)}, u32[]{:S(2)}, u32[]{:S(2)}) collective-permute-start(bf16[1024,384]{1,0:T(8,128)(2,1)} %constant_dynamic-slice_fusion.14), channel_id=1, source_target_pairs={{0,1},{1,0},{2,3},{3,2},{4,5},{5,4},{6,7},{7,6},{8,9},{9,8},{10,11... | collective-permute-start | bytes 2359304 | tf_op jit(solution)/shard_map/ppermute | solution.py:706
  137.4 37.9 %collective-permute-start.24 = (bf16[512,768]{1,0:T(8,128)(2,1)}, bf16[512,768]{1,0:T(8,128)(2,1)}, u32[]{:S(2)}, u32[]{:S(2)}) collective-permute-start(bf16[512,768]{1,0:T(8,128)(2,1)} %get-tuple-element.275), channel_id=1, source_target_pairs={{0,2},{1,3},{2,0},{3,1},{4,6},{5,7},{6,4},{7,5},{8,10},{9,11},{10,... | collective-permute-start | bytes 2359304 | tf_op jit(solution)/shard_map/ppermute | solution.py:309
  242.3 15.8 %collective-permute-start.26 = (bf16[16,24,3072]{2,1,0:T(8,128)(2,1)}, bf16[16,24,3072]{2,1,0:T(8,128)(2,1)}, u32[]{:S(2)}, u32[]{:S(2)}) collective-permute-start(bf16[16,24,3072]{2,1,0:T(8,128)(2,1)} %dynamic-slice_bitcast_fusion), channel_id=1, source_target_pairs={{0,1},{1,0},{2,3},{3,2},{4,5},{5,4},{6,7},{7,6},{8,9},{9,8},{10,11... | collective-permute-start | bytes 7077896 | tf_op jit(solution)/shard_map/ppermute | solution.py:309
  242.8 15.3 %collective-permute-start.25 = (bf16[16,96,768]{2,1,0:T(8,128)(2,1)}, bf16[16,96,768]{2,1,0:T(8,128)(2,1)}, u32[]{:S(2)}, u32[]{:S(2)}) collective-permute-start(bf16[16,96,768]{2,1,0:T(8,128)(2,1)} %dynamic-slice_bitcast_fusion.1), channel_id=1, source_target_pairs={{0,1},{1,0},{2,3},{3,2},{4,5},{5,4},{6,7},{7,6},{8,9},{9,8},{10,11... | collective-permute-start | bytes 7077896 | tf_op jit(solution)/shard_map/ppermute | solution.py:309
  251.9 44.0 %collective-permute-start.28 = (bf16[16,24,768]{2,1,0:T(8,128)(2,1)}, bf16[16,24,768]{2,1,0:T(8,128)(2,1)}, u32[]{:S(2)}, u32[]{:S(2)}) collective-permute-start(bf16[16,24,768]{2,1,0:T(8,128)(2,1)} %dynamic-slice_bitcast_fusion.12), channel_id=1, source_target_pairs={{0,1},{1,0},{2,3},{3,2},{4,5},{5,4},{6,7},{7,6},{8,9},{9,8},{10,11... | collective-permute-start | bytes 1769480 | tf_op jit(solution)/shard_map/ppermute | solution.py:309
  266.2 29.8 %collective-permute-start.29 = (bf16[4,192,768]{2,1,0:T(8,128)(2,1)S(1)}, bf16[4,192,768]{2,1,0:T(8,128)(2,1)}, u32[]{:S(2)}, u32[]{:S(2)}) collective-permute-start(bf16[4,192,768]{2,1,0:T(8,128)(2,1)S(1)} %dynamic-slice_bitcast_fusion.3), channel_id=1, source_target_pairs={{0,4},{1,5},{2,6},{3,7},{4,0},{5,1},{6,2},{7,3},{8,12},{9,13},{10,... | collective-permute-start | bytes 3538952 | tf_op jit(solution)/shard_map/ppermute | solution.py:309
  267.4 28.6 %collective-permute-start.30 = (bf16[8,24,3072]{2,1,0:T(8,128)(2,1)}, bf16[8,24,3072]{2,1,0:T(8,128)(2,1)}, u32[]{:S(2)}, u32[]{:S(2)}) collective-permute-start(bf16[8,24,3072]{2,1,0:T(8,128)(2,1)} %dynamic-slice_bitcast_fusion.2), channel_id=1, source_target_pairs={{0,2},{1,3},{2,0},{3,1},{4,6},{5,7},{6,4},{7,5},{8,10},{9,11},{10,... | collective-permute-start | bytes 3538952 | tf_op jit(solution)/shard_map/ppermute | solution.py:309
  302.0 27.4 %collective-permute-start.33 = (bf16[8,24,768]{2,1,0:T(8,128)(2,1)}, bf16[8,24,768]{2,1,0:T(8,128)(2,1)}, u32[]{:S(2)}, u32[]{:S(2)}) collective-permute-start(bf16[8,24,768]{2,1,0:T(8,128)(2,1)} %dynamic-slice_bitcast_fusion.17), channel_id=1, source_target_pairs={{0,2},{1,3},{2,0},{3,1},{4,6},{5,7},{6,4},{7,5},{8,10},{9,11},{10,... | collective-permute-start | bytes 884744 | tf_op jit(solution)/shard_map/ppermute | solution.py:309
  307.0 22.4 %collective-permute-start.35 = (bf16[4,24,3072]{2,1,0:T(8,128)(2,1)S(1)}, bf16[4,24,3072]{2,1,0:T(8,128)(2,1)S(1)}, u32[]{:S(2)}, u32[]{:S(2)}) collective-permute-start(bf16[4,24,3072]{2,1,0:T(8,128)(2,1)S(1)} %dynamic-slice_bitcast_fusion.10), channel_id=1, source_target_pairs={{0,4},{1,5},{2,6},{3,7},{4,0},{5,1},{6,2},{7,3},{8,12},{9,13},{10,... | collective-permute-start | bytes 1769480 | tf_op jit(solution)/shard_map/ppermute | solution.py:309
  310.7 18.7 %collective-permute-start.34 = (bf16[4,96,768]{2,1,0:T(8,128)(2,1)S(1)}, bf16[4,96,768]{2,1,0:T(8,128)(2,1)}, u32[]{:S(2)}, u32[]{:S(2)}) collective-permute-start(bf16[4,96,768]{2,1,0:T(8,128)(2,1)S(1)} %dynamic-slice_bitcast_fusion.11), channel_id=1, source_target_pairs={{0,2},{1,3},{2,0},{3,1},{4,6},{5,7},{6,4},{7,5},{8,10},{9,11},{10,... | collective-permute-start | bytes 1769480 | tf_op jit(solution)/shard_map/ppermute | solution.py:309
  348.2 10.1 %collective-permute-start.38 = (bf16[2,24,3072]{2,1,0:T(8,128)(2,1)}, bf16[2,24,3072]{2,1,0:T(8,128)(2,1)}, u32[]{:S(2)}, u32[]{:S(2)}) collective-permute-start(bf16[2,24,3072]{2,1,0:T(8,128)(2,1)} %dynamic-slice_bitcast_fusion.15), channel_id=1, source_target_pairs={{0,8},{1,9},{2,10},{3,11},{4,12},{5,13},{6,14},{7,15},{8,0},{9,1},... | collective-permute-start | bytes 884744 | tf_op jit(solution)/shard_map/ppermute | solution.py:309
  349.4 14.9 %collective-permute-start.37 = (bf16[2,96,768]{2,1,0:T(8,128)(2,1)}, bf16[2,96,768]{2,1,0:T(8,128)(2,1)}, u32[]{:S(2)}, u32[]{:S(2)}) collective-permute-start(bf16[2,96,768]{2,1,0:T(8,128)(2,1)} %dynamic-slice_bitcast_fusion.16), channel_id=1, source_target_pairs={{0,8},{1,9},{2,10},{3,11},{4,12},{5,13},{6,14},{7,15},{8,0},{9,1},... | collective-permute-start | bytes 884744 | tf_op jit(solution)/shard_map/ppermute | solution.py:309
  366.8 17.9 %collective-permute-start.43 = (bf16[16,72,384]{2,1,0:T(8,128)(2,1)S(1)}, bf16[16,72,384]{2,1,0:T(8,128)(2,1)S(1)}, u32[]{:S(2)}, u32[]{:S(2)}) collective-permute-start(bf16[16,72,384]{2,1,0:T(8,128)(2,1)S(1)} %dynamic-slice_bitcast_fusion.4), channel_id=1, source_target_pairs={{0,1},{1,0},{2,3},{3,2},{4,5},{5,4},{6,7},{7,6},{8,9},{9,8},{10,11... | collective-permute-start | bytes 2654216 | tf_op jit(solution)/shard_map/ppermute | solution.py:309
  366.9 17.8 %collective-permute-start.42 = (bf16[16,72,384]{2,1,0:T(8,128)(2,1)S(1)}, bf16[16,72,384]{2,1,0:T(8,128)(2,1)S(1)}, u32[]{:S(2)}, u32[]{:S(2)}) collective-permute-start(bf16[16,72,384]{2,1,0:T(8,128)(2,1)S(1)} %dynamic-slice_bitcast_fusion.5), channel_id=1, source_target_pairs={{0,1},{1,0},{2,3},{3,2},{4,5},{5,4},{6,7},{7,6},{8,9},{9,8},{10,11... | collective-permute-start | bytes 2654216 | tf_op jit(solution)/shard_map/ppermute | solution.py:309
  368.5 13.6 %collective-permute-start.41 = (bf16[1,24,3072]{2,1,0:T(8,128)(2,1)S(1)}, bf16[1,24,3072]{2,1,0:T(8,128)(2,1)S(1)}, u32[]{:S(2)}, u32[]{:S(2)}) collective-permute-start(bf16[1,24,3072]{2,1,0:T(8,128)(2,1)S(1)} %constant_dynamic-slice_fusion.11), channel_id=1, source_target_pairs={{0,16},{1,17},{2,18},{3,19},{4,20},{5,21},{6,22},{7,23},{8,24},{9,... | collective-permute-start | bytes 442376 | tf_op jit(solution)/shard_map/ppermute | solution.py:309
  371.2 13.5 %collective-permute-start.40 = (bf16[1,96,768]{2,1,0:T(8,128)(2,1)S(1)}, bf16[1,96,768]{2,1,0:T(8,128)(2,1)S(1)}, u32[]{:S(2)}, u32[]{:S(2)}) collective-permute-start(bf16[1,96,768]{2,1,0:T(8,128)(2,1)S(1)} %constant_dynamic-slice_fusion.12), channel_id=1, source_target_pairs={{0,16},{1,17},{2,18},{3,19},{4,20},{5,21},{6,22},{7,23},{8,24},{9,... | collective-permute-start | bytes 442376 | tf_op jit(solution)/shard_map/ppermute | solution.py:309
  378.3 48.8 %collective-permute-start.51 = (bf16[512,768]{1,0:T(8,128)(2,1)}, bf16[512,768]{1,0:T(8,128)(2,1)}, u32[]{:S(2)}, u32[]{:S(2)}) collective-permute-start(bf16[512,768]{1,0:T(8,128)(2,1)} %get-tuple-element.267), channel_id=1, source_target_pairs={{0,2},{1,3},{2,0},{3,1},{4,6},{5,7},{6,4},{7,5},{8,10},{9,11},{10,... | collective-permute-start | bytes 2359304 | tf_op jit(solution)/shard_map/ppermute | solution.py:309
  382.1 45.2 %collective-permute-start.49 = (f32[16,8,128]{2,1,0:T(8,128)}, f32[16,8,128]{2,1,0:T(8,128)}, u32[]{:S(2)}, u32[]{:S(2)}) collective-permute-start(f32[16,8,128]{2,1,0:T(8,128)} %dynamic-slice_bitcast_fusion.26), channel_id=1, source_target_pairs={{0,1},{1,0},{2,3},{3,2},{4,5},{5,4},{6,7},{7,6},{8,9},{9,8},{10,11... | collective-permute-start | bytes 196616 | tf_op jit(solution)/shard_map/ppermute | solution.py:309
  385.5 21.4 %collective-permute-start.44 = (bf16[8,72,384]{2,1,0:T(8,128)(2,1)S(1)}, bf16[8,72,384]{2,1,0:T(8,128)(2,1)S(1)}, u32[]{:S(2)}, u32[]{:S(2)}) collective-permute-start(bf16[8,72,384]{2,1,0:T(8,128)(2,1)S(1)} %dynamic-slice_bitcast_fusion.14), channel_id=1, source_target_pairs={{0,2},{1,3},{2,0},{3,1},{4,6},{5,7},{6,4},{7,5},{8,10},{9,11},{10,... | collective-permute-start | bytes 1327112 | tf_op jit(solution)/shard_map/ppermute | solution.py:309
  387.0 19.9 %collective-permute-start.45 = (bf16[4,144,384]{2,1,0:T(8,128)(2,1)S(1)}, bf16[4,144,384]{2,1,0:T(8,128)(2,1)S(1)}, u32[]{:S(2)}, u32[]{:S(2)}) collective-permute-start(bf16[4,144,384]{2,1,0:T(8,128)(2,1)S(1)} %dynamic-slice_bitcast_fusion.13), channel_id=1, source_target_pairs={{0,4},{1,5},{2,6},{3,7},{4,0},{5,1},{6,2},{7,3},{8,12},{9,13},{10,... | collective-permute-start | bytes 1327112 | tf_op jit(solution)/shard_map/ppermute | solution.py:309
  418.1 9.3 %collective-permute-start.50 = (f32[16,24,64]{2,1,0:T(8,128)}, f32[16,24,64]{2,1,0:T(8,128)}, u32[]{:S(2)}, u32[]{:S(2)}) collective-permute-start(f32[16,24,64]{2,1,0:T(8,128)} %dynamic-slice_bitcast_fusion.20), channel_id=1, source_target_pairs={{0,1},{1,0},{2,3},{3,2},{4,5},{5,4},{6,7},{7,6},{8,9},{9,8},{10,11... | collective-permute-start | bytes 294920 | tf_op jit(solution)/shard_map/ppermute | solution.py:309
  419.5 8.1 %collective-permute-start.47 = (bf16[4,72,384]{2,1,0:T(8,128)(2,1)}, bf16[4,72,384]{2,1,0:T(8,128)(2,1)S(1)}, u32[]{:S(2)}, u32[]{:S(2)}) collective-permute-start(bf16[4,72,384]{2,1,0:T(8,128)(2,1)} %dynamic-slice_bitcast_fusion.19), channel_id=1, source_target_pairs={{0,4},{1,5},{2,6},{3,7},{4,0},{5,1},{6,2},{7,3},{8,12},{9,13},{10,... | collective-permute-start | bytes 663560 | tf_op jit(solution)/shard_map/ppermute | solution.py:309
  421.2 7.9 %collective-permute-start.48 = (bf16[4,72,384]{2,1,0:T(8,128)(2,1)}, bf16[4,72,384]{2,1,0:T(8,128)(2,1)}, u32[]{:S(2)}, u32[]{:S(2)}) collective-permute-start(bf16[4,72,384]{2,1,0:T(8,128)(2,1)} %dynamic-slice_bitcast_fusion.18), channel_id=1, source_target_pairs={{0,2},{1,3},{2,0},{3,1},{4,6},{5,7},{6,4},{7,5},{8,10},{9,11},{10,... | collective-permute-start | bytes 663560 | tf_op jit(solution)/shard_map/ppermute | solution.py:309
  427.1 45.0 %collective-permute-start.60 = (bf16[512,768]{1,0:T(8,128)(2,1)}, bf16[512,768]{1,0:T(8,128)(2,1)}, u32[]{:S(2)}, u32[]{:S(2)}) collective-permute-start(bf16[512,768]{1,0:T(8,128)(2,1)} %get-tuple-element.265), channel_id=1, source_target_pairs={{0,2},{1,3},{2,0},{3,1},{4,6},{5,7},{6,4},{7,5},{8,10},{9,11},{10,... | collective-permute-start | bytes 2359304 | tf_op jit(solution)/shard_map/ppermute | solution.py:309
  440.1 10.6 %collective-permute-start.54 = (f32[8,8,128]{2,1,0:T(8,128)}, f32[8,8,128]{2,1,0:T(8,128)S(1)}, u32[]{:S(2)}, u32[]{:S(2)}) collective-permute-start(f32[8,8,128]{2,1,0:T(8,128)} %dynamic-slice_bitcast_fusion.28), channel_id=1, source_target_pairs={{0,2},{1,3},{2,0},{3,1},{4,6},{5,7},{6,4},{7,5},{8,10},{9,11},{10,... | collective-permute-start | bytes 98312 | tf_op jit(solution)/shard_map/ppermute | solution.py:309
  456.2 15.9 %collective-permute-start.58 = (f32[4,8,128]{2,1,0:T(8,128)}, f32[4,8,128]{2,1,0:T(8,128)}, u32[]{:S(2)}, u32[]{:S(2)}) collective-permute-start(f32[4,8,128]{2,1,0:T(8,128)} %fusion.57), channel_id=1, source_target_pairs={{0,4},{1,5},{2,6},{3,7},{4,0},{5,1},{6,2},{7,3},{8,12},{9,13},{10,... | collective-permute-start | bytes 49160 | tf_op jit(solution)/shard_map/ppermute | solution.py:309
  458.5 15.7 %collective-permute-start.59 = (f32[4,24,64]{2,1,0:T(8,128)}, f32[4,24,64]{2,1,0:T(8,128)}, u32[]{:S(2)}, u32[]{:S(2)}) collective-permute-start(f32[4,24,64]{2,1,0:T(8,128)} %dynamic-slice_bitcast_fusion.27), channel_id=1, source_target_pairs={{0,4},{1,5},{2,6},{3,7},{4,0},{5,1},{6,2},{7,3},{8,12},{9,13},{10,... | collective-permute-start | bytes 73736 | tf_op jit(solution)/shard_map/ppermute | solution.py:309
  460.1 14.2 %collective-permute-start.56 = (bf16[1,72,384]{2,1,0:T(8,128)(2,1)}, bf16[1,72,384]{2,1,0:T(8,128)(2,1)}, u32[]{:S(2)}, u32[]{:S(2)}) collective-permute-start(bf16[1,72,384]{2,1,0:T(8,128)(2,1)} %constant_dynamic-slice_fusion.9), channel_id=1, source_target_pairs={{0,16},{1,17},{2,18},{3,19},{4,20},{5,21},{6,22},{7,23},{8,24},{9,... | collective-permute-start | bytes 165896 | tf_op jit(solution)/shard_map/ppermute | solution.py:309
  461.6 12.7 %collective-permute-start.57 = (bf16[1,72,384]{2,1,0:T(8,128)(2,1)}, bf16[1,72,384]{2,1,0:T(8,128)(2,1)}, u32[]{:S(2)}, u32[]{:S(2)}) collective-permute-start(bf16[1,72,384]{2,1,0:T(8,128)(2,1)} %constant_dynamic-slice_fusion.8), channel_id=1, source_target_pairs={{0,16},{1,17},{2,18},{3,19},{4,20},{5,21},{6,22},{7,23},{8,24},{9,... | collective-permute-start | bytes 165896 | tf_op jit(solution)/shard_map/ppermute | solution.py:309
  472.0 10.8 %collective-permute-start.65 = (f32[10560]{0:T(1024)S(1)}, f32[10560]{0:T(1024)S(1)}, u32[]{:S(2)}, u32[]{:S(2)}) collective-permute-start(f32[10560]{0:T(1024)S(1)} %concatenate.197), channel_id=1, source_target_pairs={{0,3},{1,2},{2,1},{3,0},{4,7},{5,6},{6,5},{7,4},{8,11},{9,10},{10,... | collective-permute-start | bytes 126728 | tf_op jit(solution)/shard_map/ppermute | solution.py:398
  472.1 10.7 %collective-permute-start.64 = (f32[10560]{0:T(1024)S(1)}, f32[10560]{0:T(1024)S(1)}, u32[]{:S(2)}, u32[]{:S(2)}) collective-permute-start(f32[10560]{0:T(1024)S(1)} %concatenate.197), channel_id=1, source_target_pairs={{0,2},{1,3},{2,0},{3,1},{4,6},{5,7},{6,4},{7,5},{8,10},{9,11},{10,... | collective-permute-start | bytes 126728 | tf_op jit(solution)/shard_map/ppermute | solution.py:398
  474.2 8.7 %collective-permute-start.63 = (f32[10560]{0:T(1024)S(1)}, f32[10560]{0:T(1024)S(1)}, u32[]{:S(2)}, u32[]{:S(2)}) collective-permute-start(f32[10560]{0:T(1024)S(1)} %concatenate.197), channel_id=1, source_target_pairs={{0,1},{1,0},{2,3},{3,2},{4,5},{5,4},{6,7},{7,6},{8,9},{9,8},{10,11... | collective-permute-start | bytes 126728 | tf_op jit(solution)/shard_map/ppermute | solution.py:398
  482.9 9.4 %collective-permute-start.70 = (f32[10560]{0:T(1024)S(1)}, f32[10560]{0:T(1024)S(1)}, u32[]{:S(2)}, u32[]{:S(2)}) collective-permute-start(f32[10560]{0:T(1024)S(1)} %add_add_fusion.1), channel_id=1, source_target_pairs={{0,12},{1,13},{2,14},{3,15},{4,8},{5,9},{6,10},{7,11},{8,4},{9,5},... | collective-permute-start | bytes 126728 | tf_op jit(solution)/shard_map/ppermute | solution.py:398
  484.4 8.0 %collective-permute-start.69 = (f32[10560]{0:T(1024)S(1)}, f32[10560]{0:T(1024)S(1)}, u32[]{:S(2)}, u32[]{:S(2)}) collective-permute-start(f32[10560]{0:T(1024)S(1)} %add_add_fusion.1), channel_id=1, source_target_pairs={{0,8},{1,9},{2,10},{3,11},{4,12},{5,13},{6,14},{7,15},{8,0},{9,1},... | collective-permute-start | bytes 126728 | tf_op jit(solution)/shard_map/ppermute | solution.py:398
  (118 other events, 1291.6 us)
Sparse Core Ops, SparseCore 0:
  13.1 103.1 all-gather.2
